TPU v7x, 32 devices: a whole 2x2x4 slice. The times are simulated.
32 devices in a mesh: seq: 16 (over z, x, core), ch: 2 (over y).
Axes of the slice: x: 2, y: 2, z: 4, core: 2. Of those that a mesh axis runs over, the one named last changes fastest.
Arguments:
- signal: float32 [4096, 4096], P('seq', 'ch'), may hold values from -6 to 6
- filters: float32 [4096, 256], P(('seq', 'ch')), may hold values from -1 to 1
- skip_gain: float32 [4096], P('ch'), may hold values from -1 to 1
Outputs:
- filtered: float32 [4096, 4096], P('seq', 'ch')
All inputs are finite; a program needn't handle non-finite values.
Results may differ from a plain program's by a relative error of at most 0.00009.
Values sent between devices are 32-bit elements; how exact they have to be, the bound alone decides.
No kernel may reach another device: no remote copies, remote signals or barrier semaphores. Data moves between devices by JAX's collectives and lax.ppermute only.
A program may use at most 128 MiB of HBM per device.

v0:
```python
import functools
import math

import jax
import jax.numpy as jnp
from jax import lax
from jax.experimental import pallas as pl
from jax.experimental.pallas import tpu as pltpu
from jax.sharding import PartitionSpec as P

GROUP = 16
HALF = 128
CHUNKS = 1

HIGHEST_PRECISION = lax.Precision.HIGHEST


def split_halves(values):
    high = values.astype(jnp.bfloat16)
    low = (values - high.astype(jnp.float32)).astype(jnp.bfloat16)
    return high, low


def turn_kernel(in_ref, out_ref):
    out_ref[...] = in_ref[...].T


def turn_out(signal, chunk, chunks):
    rows, width = signal.shape
    cols = width // chunks
    steps = cols // HALF
    return pl.pallas_call(
        turn_kernel,
        grid=(steps,),
        in_specs=[pl.BlockSpec((rows, HALF), lambda i: (0, chunk * steps + i))],
        out_specs=pl.BlockSpec((HALF, rows), lambda i: (i, 0)),
        out_shape=jax.ShapeDtypeStruct((cols, rows), jnp.float32),
        name="turn_out",
    )(signal)


def home_kernel(back_ref, signal_ref, gain_ref, *rest):
    out_ref = rest[-1]
    out_ref[...] = back_ref[...].T + gain_ref[...] * signal_ref[...]


def turn_home(back, signal, gain, partial_out, chunk, chunks):
    rows, width = signal.shape
    steps = width // chunks // HALF
    here = lambda i: (0, chunk * steps + i)
    in_specs = [
        pl.BlockSpec((HALF, rows), lambda i: (i, 0)),
        pl.BlockSpec((rows, HALF), here),
        pl.BlockSpec((1, HALF), here),
    ]
    operands = [back, signal, gain]
    aliases = {}
    if partial_out is not None:
        in_specs.append(pl.BlockSpec(memory_space=pl.ANY))
        operands.append(partial_out)
        aliases = {3: 0}
    return pl.pallas_call(
        home_kernel,
        grid=(steps,),
        in_specs=in_specs,
        out_specs=pl.BlockSpec((rows, HALF), here),
        out_shape=jax.ShapeDtypeStruct((rows, width), jnp.float32),
        input_output_aliases=aliases,
        name="turn_home",
    )(*operands)


def conv_kernel(first, taps_ref, sig_ref, out_ref, high_ref, low_ref, sum_ref):
    blocks, _, rows = sig_ref.shape
    lags = blocks * rows
    group = first + pl.program_id(0)
    lines = [
        jnp.broadcast_to(taps_ref[i, pl.ds(group, 1), :], (8, HALF)) for i in range(lags // HALF)
    ]
    blank = jnp.zeros((8, HALF), jnp.float32)
    strip = jnp.concatenate([blank] + lines + [blank], axis=1)
    strip = pltpu.roll(strip, 0, 1, stride=1, stride_axis=0)
    for p in range(HALF // 16):
        pair = jnp.concatenate(
            [pltpu.roll(strip, 16 * p, 1) if p else strip, pltpu.roll(strip, 16 * p + 8, 1)], axis=0
        )
        high, low = split_halves(pair)
        high_ref[16 * p : 16 * p + 16, :] = high
        low_ref[16 * p : 16 * p + 16, :] = low
    sig_high, sig_low = split_halves(sig_ref[...].reshape(blocks * GROUP, rows))

    def window(ref, lag_block):
        start = lag_block * rows
        return jnp.concatenate(
            [ref[:, start + HALF * (k) : start + HALF * k + rows] for k in reversed(range(rows // HALF))],
            axis=0,
        )

    for d in range(blocks):
        n = (blocks - d) * GROUP
        taps_high, taps_low = window(high_ref, d), window(low_ref, d)
        both = jnp.concatenate([sig_high[:n], sig_low[:n]], axis=0)
        part = jnp.dot(both, taps_high, preferred_element_type=jnp.float32)
        term = part[:n] + part[n:]
        term = term + jnp.dot(sig_high[:n], taps_low, preferred_element_type=jnp.float32)
        if d == 0:
            sum_ref[...] = term
        else:
            sum_ref[d * GROUP :, :] += term
    out_ref[...] = sum_ref[...].reshape(blocks, GROUP, rows)


def convolve(taps, arrived, chunk):
    blocks, width, rows = arrived.shape
    groups = width // GROUP
    lanes = blocks * rows + 2 * HALF
    products = 3 * 2 * groups * GROUP * rows * rows * blocks * (blocks + 1) // 2
    spec = pl.BlockSpec((blocks, GROUP, rows), lambda g: (0, g, 0))
    return pl.pallas_call(
        functools.partial(conv_kernel, chunk * groups),
        grid=(groups,),
        in_specs=[pl.BlockSpec(taps.shape, lambda g: (0, 0, 0)), spec],
        out_specs=spec,
        out_shape=jax.ShapeDtypeStruct(arrived.shape, jnp.float32),
        scratch_shapes=[
            pltpu.VMEM((HALF, lanes), jnp.bfloat16),
            pltpu.VMEM((HALF, lanes), jnp.bfloat16),
            pltpu.VMEM((blocks * GROUP, rows), jnp.float32),
        ],
        compiler_params=pltpu.CompilerParams(vmem_limit_bytes=40 * 1024 * 1024),
        cost_estimate=pl.CostEstimate(
            flops=products, bytes_accessed=8 * blocks * width * rows, transcendentals=0
        ),
        name="convolve",
    )(taps, arrived)


def fast_body(signal, filters, skip_gain):
    blocks = lax.axis_size("seq")
    sides = lax.axis_size("ch")
    rows, width = signal.shape
    lag_rows, groups = filters.shape
    chunks = CHUNKS
    per_chunk = width // chunks // blocks
    local = groups // sides // blocks
    by_home = filters.T.reshape(sides, chunks, blocks, local // chunks, lag_rows)
    by_home = by_home.transpose(2, 0, 1, 3, 4).reshape(blocks * sides, local, lag_rows)
    taps = lax.all_to_all(by_home, ("seq", "ch"), split_axis=0, concat_axis=0, tiled=True)
    gain = skip_gain.reshape(1, width)
    out = None
    for k in range(chunks):
        leaving = turn_out(signal, k, chunks).reshape(blocks, per_chunk, rows)
        arrived = lax.all_to_all(leaving, "seq", split_axis=0, concat_axis=0, tiled=True)
        values = convolve(taps, arrived, k)
        back = lax.all_to_all(values, "seq", split_axis=0, concat_axis=0, tiled=True)
        out = turn_home(back.reshape(blocks * per_chunk, rows), signal, gain, out, k, chunks)
    return out


def angle_table(row_count, col_count, length, sign):
    row_index = jnp.arange(row_count, dtype=jnp.int32)[:, None]
    col_index = jnp.arange(col_count, dtype=jnp.int32)[None, :]
    phase = row_index * col_index % length
    angle = sign * 2.0 * math.pi / length * phase.astype(jnp.float32)
    return (jnp.cos(angle), jnp.sin(angle))


def complex_apply(form, table, real_part, imag_part):
    cosine, sine = table

    def product(matrix, values):
        return jnp.einsum(form, matrix, values, precision=HIGHEST_PRECISION)

    if imag_part is None:
        return (product(cosine, real_part), product(sine, real_part))
    return (
        product(cosine, real_part) - product(sine, imag_part),
        product(cosine, imag_part) + product(sine, real_part),
    )


def rotate(real_part, imag_part, cosine, sine):
    return (real_part * cosine - imag_part * sine, real_part * sine + imag_part * cosine)


def local_convolve(whole_sig, whole_taps, blocks, rows):
    width = whole_sig.shape[1]
    span = 2 * blocks * rows
    sig_blocks = whole_sig.reshape(blocks, rows, width)
    tap_blocks = whole_taps.reshape(blocks, rows, width)
    outer = angle_table(2 * blocks, blocks, 2 * blocks, -1.0)
    sig_real, sig_imag = complex_apply("kn,nbc->kbc", outer, sig_blocks, None)
    filt_real, filt_imag = complex_apply("kn,nbc->kbc", outer, tap_blocks, None)
    phase = (
        jnp.arange(2 * blocks, dtype=jnp.int32)[:, None]
        * jnp.arange(rows, dtype=jnp.int32)[None, :]
        % span
    )
    twist = 2.0 * math.pi / span * phase.astype(jnp.float32)
    twist_cos = jnp.cos(twist)[:, :, None]
    twist_sin = jnp.sin(twist)[:, :, None]
    sig_real, sig_imag = rotate(sig_real, sig_imag, twist_cos, -twist_sin)
    filt_real, filt_imag = rotate(filt_real, filt_imag, twist_cos, -twist_sin)
    inner = angle_table(rows, rows, rows, -1.0)
    sig_real, sig_imag = complex_apply("kn,bnc->bkc", inner, sig_real, sig_imag)
    filt_real, filt_imag = complex_apply("kn,bnc->bkc", inner, filt_real, filt_imag)
    prod_real, prod_imag = rotate(sig_real, sig_imag, filt_real, filt_imag)
    inverse_inner = angle_table(rows, rows, rows, 1.0)
    back_real, back_imag = complex_apply("nk,bkc->bnc", inverse_inner, prod_real, prod_imag)
    back_real, back_imag = rotate(back_real, back_imag, twist_cos, twist_sin)
    outer_back = angle_table(blocks, 2 * blocks, 2 * blocks, 1.0)
    values = jnp.einsum(
        "nk,kbc->nbc", outer_back[0], back_real, precision=HIGHEST_PRECISION
    ) - jnp.einsum("nk,kbc->nbc", outer_back[1], back_imag, precision=HIGHEST_PRECISION)
    return values.reshape(blocks * rows, width) / span


def spectral_body(signal, filters, skip_gain):
    blocks = lax.axis_size("seq")
    rows = signal.shape[0]
    taps = lax.all_to_all(filters, "ch", split_axis=1, concat_axis=0, tiled=True)
    local_groups = taps.shape[1]
    per_channel = jnp.broadcast_to(taps[:, :, None], (rows, local_groups, GROUP)).reshape(
        rows, local_groups * GROUP
    )
    whole_sig, whole_taps = (
        lax.all_to_all(signal, "seq", split_axis=1, concat_axis=0, tiled=True),
        lax.all_to_all(per_channel, "seq", split_axis=1, concat_axis=0, tiled=True),
    )
    values = local_convolve(whole_sig, whole_taps, blocks, rows)
    homed = lax.all_to_all(values, "seq", split_axis=0, concat_axis=1, tiled=True)
    return homed + skip_gain[None, :] * signal


def body(signal, filters, skip_gain):
    blocks = lax.axis_size("seq")
    rows, width = signal.shape
    lag_rows = filters.shape[0]
    fits = (
        width % (blocks * CHUNKS * GROUP) == 0
        and width % (CHUNKS * HALF) == 0
        and rows % HALF == 0
        and lag_rows == HALF
    )
    if fits:
        return fast_body(signal, filters, skip_gain)
    return spectral_body(signal, filters, skip_gain)


def solution(mesh):
    placed = (P("seq", "ch"), P(("seq", "ch"), None), P("ch"))
    return jax.shard_map(
        body, mesh=mesh, in_specs=placed, out_specs=P("seq", "ch"), check_vma=False
    )
```

profile of v0, /device:TPU:9, one launch (start us, length us, event | category | flops | bytes accessed | tf_op | source)
XLA Modules:
  0.0 150.6 jit_solution(15608897607285620341)
XLA Ops:
  0.0 1.0 copy.5
  1.0 0.6 copy.6
  1.6 6.4 %all-to-all-start = ((f32[32,8,128]{2,1,0:T(8,128)}), f32[32,8,128]{2,1,0:T(8,128)S(1)}, u32[]{:S(2)}, u32[]{:S(2)}) async-start(f32[32,8,128]{2,1,0:T(8,128)} %bitcast.3), calls=%async_computation | async-start | bytes 262144 | tf_op jit(solution)/shard_map/all_to_all | solution.py:148
  8.0 10.0 %turn_out.1 = f32[2048,256]{1,0:T(8,128)} custom-call(f32[256,2048]{1,0:T(8,128)} %signal_ref.1), custom_call_target="tpu_custom_call" | custom-call | tf_op jit(solution)/shard_map/turn_out/pallas_call | solution.py:32
  18.0 0.0 all-to-all-done.taps_ref
  18.0 53.9 %all_to_all.15.sig_ref = f32[16,128,256]{2,1,0:T(8,128)S(1)} all-to-all(f32[16,128,256]{2,1,0:T(8,128)} %bitcast.9), channel_id=1, replica_groups=mesh['seq'=16,'ch'=2] {'seq'}, dimensions={0} | all-to-all | bytes 4194304 | tf_op jit(solution)/shard_map/all_to_all | solution.py:153
  72.0 15.8 %convolve.1 = f32[16,128,256]{2,1,0:T(8,128)S(1)} custom-call(f32[32,8,128]{2,1,0:T(8,128)S(1)} %all-to-all-done.taps_ref, f32[16,128,256]{2,1,0:T(8,128)S(1)} %all_to_all.15.sig_ref), custom_call_target="tpu_custom_call" | custom-call | flops 6845104128 | bytes 4194304 | tf_op jit(solution)/shard_map/convolve/pallas_call | solution.py:119
  87.8 52.3 %all_to_all.16 = f32[16,128,256]{2,1,0:T(8,128)} all-to-all(f32[16,128,256]{2,1,0:T(8,128)S(1)} %convolve.1), channel_id=1, replica_groups=mesh['seq'=16,'ch'=2] {'seq'}, dimensions={0} | all-to-all | bytes 4194304 | tf_op jit(solution)/shard_map/all_to_all | solution.py:155
  140.1 10.5 %turn_home.1 = f32[256,2048]{1,0:T(8,128)} custom-call(f32[2048,256]{1,0:T(8,128)} %bitcast.10, f32[256,2048]{1,0:T(8,128)} %signal_ref.1, f32[1,2048]{1,0:T(1,128)} %bitcast.12), custom_call_target="tpu_custom_call" | custom-call | tf_op jit(solution)/shard_map/turn_home/pallas_call | solution.py:62
Async XLA Ops:
  1.6 16.4 %all-to-all-start = ((f32[32,8,128]{2,1,0:T(8,128)}), f32[32,8,128]{2,1,0:T(8,128)S(1)}, u32[]{:S(2)}, u32[]{:S(2)}) async-start(f32[32,8,128]{2,1,0:T(8,128)} %bitcast.3), calls=%async_computation | async-start | bytes 262144 | tf_op jit(solution)/shard_map/all_to_all | solution.py:148
where the time goes:
time: 152 us; the launch traced here: 151 us
  blocking collectives  106 us (70%)
  Pallas kernels  36.4 us (24%)
  starting transfers between devices  6.36 us (4%)
  local copies, waits for them, and re-layouts  1.64 us (1%)
    all_to_all x1, blocking collectives, fast_body(): lax.all_to_all(leaving, 'seq', split_axis=0, concat_axis=0, tiled=True)  53.9 us
    all_to_all x1, blocking collectives, fast_body(): lax.all_to_all(values, 'seq', split_axis=0, concat_axis=0, tiled=True)  52.3 us
    pallas_call x1, Pallas kernels, convolve(): pl.pallas_call(functools.partial(conv_kernel, chunk * groups), grid=(grou...  15.8 us
    pallas_call x1, Pallas kernels, turn_home(): pl.pallas_call(home_kernel, grid=(steps,), in_specs=in_specs, out_specs=p...  10.5 us
    pallas_call x1, Pallas kernels, turn_out(): pl.pallas_call(turn_kernel, grid=(steps,), in_specs=[pl.BlockSpec((rows,...  10 us
    all_to_all x1, starting transfers between devices, fast_body(): lax.all_to_all(by_home, ('seq', 'ch'), split_axis=0, concat_axis=0, tiled...  6.36 us
  transfers between devices with their start and end apart: 1, of which 0 were waited for; matrix products, arithmetic and copies ran while one was open for 0% of the time, Pallas kernels for 7%

commit v1 on v0

--- a/solution.py
+++ b/solution.py
@@ -10,7 +10,7 @@
 
 GROUP = 16
 HALF = 128
-CHUNKS = 1
+VMEM_BYTES = 60 * 1024 * 1024
 
 HIGHEST_PRECISION = lax.Precision.HIGHEST
 
@@ -21,37 +21,80 @@
     return high, low
 
 
-def turn_kernel(in_ref, out_ref):
-    out_ref[...] = in_ref[...].T
-
-
-def turn_out(signal, chunk, chunks):
+def turned(in_ref):
+    return in_ref[...].T
+
+
+def turn_taps_kernel(counts, sig_ref, taps_ref, out_ref):
+    blocks, _, rows = out_ref.shape
+    per_chunk = sig_ref.shape[1] // blocks
+    lag_rows, groups = taps_ref.shape
+    out_ref[:, :per_chunk, :] = turned(sig_ref).reshape(blocks, per_chunk, rows)
+    lines = turned(taps_ref)
+    sides = rows // lag_rows
+    for side in range(sides):
+        row = per_chunk
+        start = side * (groups // sides)
+        for count in counts:
+            for q in range(blocks):
+                here = start + q * count
+                at = slice(side * lag_rows, (side + 1) * lag_rows)
+                out_ref[q, row : row + count, at] = lines[here : here + count]
+            row += count
+            start += blocks * count
+
+
+def turn_taps(signal, filters, blocks, counts):
     rows, width = signal.shape
-    cols = width // chunks
-    steps = cols // HALF
+    cols = blocks * counts[0] * GROUP
+    shape = (blocks, counts[0] * GROUP + sum(counts), rows)
+    return pl.pallas_call(
+        functools.partial(turn_taps_kernel, counts),
+        grid=(1,),
+        in_specs=[
+            pl.BlockSpec((rows, cols), lambda i: (0, 0)),
+            pl.BlockSpec(filters.shape, lambda i: (0, 0)),
+        ],
+        out_specs=pl.BlockSpec(shape, lambda i: (0, 0, 0)),
+        out_shape=jax.ShapeDtypeStruct(shape, jnp.float32),
+        compiler_params=pltpu.CompilerParams(vmem_limit_bytes=VMEM_BYTES),
+        cost_estimate=pl.CostEstimate(flops=0, bytes_accessed=8 * rows * cols, transcendentals=0),
+        name="turn_taps",
+    )(signal, filters)
+
+
+def turn_kernel(sig_ref, out_ref):
+    out_ref[...] = turned(sig_ref)
+
+
+def turn(signal, start, cols):
+    rows = signal.shape[0]
+    step = math.gcd(start, cols)
     return pl.pallas_call(
         turn_kernel,
-        grid=(steps,),
-        in_specs=[pl.BlockSpec((rows, HALF), lambda i: (0, chunk * steps + i))],
-        out_specs=pl.BlockSpec((HALF, rows), lambda i: (i, 0)),
+        grid=(cols // step,),
+        in_specs=[pl.BlockSpec((rows, step), lambda i: (0, start // step + i))],
+        out_specs=pl.BlockSpec((step, rows), lambda i: (i, 0)),
         out_shape=jax.ShapeDtypeStruct((cols, rows), jnp.float32),
-        name="turn_out",
+        compiler_params=pltpu.CompilerParams(vmem_limit_bytes=VMEM_BYTES),
+        cost_estimate=pl.CostEstimate(flops=0, bytes_accessed=8 * rows * cols, transcendentals=0),
+        name="turn",
     )(signal)
 
 
-def home_kernel(back_ref, signal_ref, gain_ref, *rest):
-    out_ref = rest[-1]
-    out_ref[...] = back_ref[...].T + gain_ref[...] * signal_ref[...]
-
-
-def turn_home(back, signal, gain, partial_out, chunk, chunks):
+def home_kernel(back_ref, sig_ref, gain_ref, *rest):
+    rest[-1][...] = turned(back_ref) + gain_ref[...] * sig_ref[...]
+
+
+def home(back, signal, gain, start, partial_out):
     rows, width = signal.shape
-    steps = width // chunks // HALF
-    here = lambda i: (0, chunk * steps + i)
+    cols = back.shape[0]
+    step = math.gcd(start, cols)
+    here = lambda i: (0, start // step + i)
     in_specs = [
-        pl.BlockSpec((HALF, rows), lambda i: (i, 0)),
-        pl.BlockSpec((rows, HALF), here),
-        pl.BlockSpec((1, HALF), here),
+        pl.BlockSpec((step, rows), lambda i: (i, 0)),
+        pl.BlockSpec((rows, step), here),
+        pl.BlockSpec((1, step), here),
     ]
     operands = [back, signal, gain]
     aliases = {}
@@ -61,22 +104,28 @@
         aliases = {3: 0}
     return pl.pallas_call(
         home_kernel,
-        grid=(steps,),
+        grid=(cols // step,),
         in_specs=in_specs,
-        out_specs=pl.BlockSpec((rows, HALF), here),
+        out_specs=pl.BlockSpec((rows, step), here),
         out_shape=jax.ShapeDtypeStruct((rows, width), jnp.float32),
         input_output_aliases=aliases,
-        name="turn_home",
+        compiler_params=pltpu.CompilerParams(vmem_limit_bytes=VMEM_BYTES),
+        cost_estimate=pl.CostEstimate(flops=0, bytes_accessed=12 * rows * cols, transcendentals=0),
+        name="home",
     )(*operands)
 
 
-def conv_kernel(first, taps_ref, sig_ref, out_ref, high_ref, low_ref, sum_ref):
-    blocks, _, rows = sig_ref.shape
-    lags = blocks * rows
-    group = first + pl.program_id(0)
-    lines = [
-        jnp.broadcast_to(taps_ref[i, pl.ds(group, 1), :], (8, HALF)) for i in range(lags // HALF)
-    ]
+def convolve_group(side, group, own_ref, other_ref, signal, high_ref, low_ref, sum_ref):
+    blocks = own_ref.shape[0]
+    rows = signal.shape[1]
+
+    def line(ref, q):
+        return jnp.broadcast_to(ref[q, pl.ds(group, 1), :], (8, HALF))
+
+    lines = []
+    for q in range(blocks):
+        own, other = line(own_ref, q), line(other_ref, q)
+        lines += [jnp.where(side == 0, own, other), jnp.where(side == 0, other, own)]
     blank = jnp.zeros((8, HALF), jnp.float32)
     strip = jnp.concatenate([blank] + lines + [blank], axis=1)
     strip = pltpu.roll(strip, 0, 1, stride=1, stride_axis=0)
@@ -87,13 +136,12 @@
         high, low = split_halves(pair)
         high_ref[16 * p : 16 * p + 16, :] = high
         low_ref[16 * p : 16 * p + 16, :] = low
-    sig_high, sig_low = split_halves(sig_ref[...].reshape(blocks * GROUP, rows))
+    sig_high, sig_low = split_halves(signal)
 
     def window(ref, lag_block):
         start = lag_block * rows
         return jnp.concatenate(
-            [ref[:, start + HALF * (k) : start + HALF * k + rows] for k in reversed(range(rows // HALF))],
-            axis=0,
+            [ref[:, start + HALF * k : start + HALF * k + rows] for k in (1, 0)], axis=0
         )
 
     for d in range(blocks):
@@ -107,53 +155,82 @@
             sum_ref[...] = term
         else:
             sum_ref[d * GROUP :, :] += term
+
+
+def conv_kernel(first, place_ref, own_ref, other_ref, sig_ref, out_ref, high_ref, low_ref, sum_ref):
+    blocks, _, rows = sig_ref.shape
+    signal = sig_ref[...].reshape(blocks * GROUP, rows)
+    group = first + pl.program_id(0)
+    convolve_group(place_ref[1], group, own_ref, other_ref, signal, high_ref, low_ref, sum_ref)
     out_ref[...] = sum_ref[...].reshape(blocks, GROUP, rows)
 
 
-def convolve(taps, arrived, chunk):
-    blocks, width, rows = arrived.shape
-    groups = width // GROUP
+def conv_scratch(blocks, rows):
     lanes = blocks * rows + 2 * HALF
-    products = 3 * 2 * groups * GROUP * rows * rows * blocks * (blocks + 1) // 2
+    return [
+        pltpu.VMEM((HALF, lanes), jnp.bfloat16),
+        pltpu.VMEM((HALF, lanes), jnp.bfloat16),
+        pltpu.VMEM((blocks * GROUP, rows), jnp.float32),
+    ]
+
+
+def conv_cost(blocks, groups, rows):
+    products = 3 * groups * GROUP * rows * rows * blocks * (blocks + 1)
+    return pl.CostEstimate(
+        flops=products, bytes_accessed=8 * blocks * groups * GROUP * rows, transcendentals=0
+    )
+
+
+def convolve(place, own, other, arrived, first, groups):
+    blocks, _, rows = arrived.shape
     spec = pl.BlockSpec((blocks, GROUP, rows), lambda g: (0, g, 0))
+    taps_spec = pl.BlockSpec(own.shape, lambda g: (0, 0, 0))
     return pl.pallas_call(
-        functools.partial(conv_kernel, chunk * groups),
+        functools.partial(conv_kernel, first),
         grid=(groups,),
-        in_specs=[pl.BlockSpec(taps.shape, lambda g: (0, 0, 0)), spec],
+        in_specs=[pl.BlockSpec(memory_space=pltpu.SMEM), taps_spec, taps_spec, spec],
         out_specs=spec,
-        out_shape=jax.ShapeDtypeStruct(arrived.shape, jnp.float32),
-        scratch_shapes=[
-            pltpu.VMEM((HALF, lanes), jnp.bfloat16),
-            pltpu.VMEM((HALF, lanes), jnp.bfloat16),
-            pltpu.VMEM((blocks * GROUP, rows), jnp.float32),
-        ],
-        compiler_params=pltpu.CompilerParams(vmem_limit_bytes=40 * 1024 * 1024),
-        cost_estimate=pl.CostEstimate(
-            flops=products, bytes_accessed=8 * blocks * width * rows, transcendentals=0
-        ),
+        out_shape=jax.ShapeDtypeStruct((blocks, groups * GROUP, rows), jnp.float32),
+        scratch_shapes=conv_scratch(blocks, rows),
+        compiler_params=pltpu.CompilerParams(vmem_limit_bytes=VMEM_BYTES),
+        cost_estimate=conv_cost(blocks, groups, rows),
         name="convolve",
-    )(taps, arrived)
+    )(place, own, other, arrived)
+
+
+def exchange(values, axis, step):
+    size = lax.axis_size(axis)
+    return lax.ppermute(values, axis, [(i, i ^ step) for i in range(size)])
+
+
+def spread(values):
+    return lax.all_to_all(values, "seq", split_axis=0, concat_axis=0, tiled=True)
 
 
 def fast_body(signal, filters, skip_gain):
     blocks = lax.axis_size("seq")
-    sides = lax.axis_size("ch")
     rows, width = signal.shape
-    lag_rows, groups = filters.shape
-    chunks = CHUNKS
-    per_chunk = width // chunks // blocks
-    local = groups // sides // blocks
-    by_home = filters.T.reshape(sides, chunks, blocks, local // chunks, lag_rows)
-    by_home = by_home.transpose(2, 0, 1, 3, 4).reshape(blocks * sides, local, lag_rows)
-    taps = lax.all_to_all(by_home, ("seq", "ch"), split_axis=0, concat_axis=0, tiled=True)
+    counts = (width // blocks // GROUP // 2,) * 2
+    side = lax.axis_index("ch")
+    place = jnp.stack([lax.axis_index("seq"), side]).astype(jnp.int32)
     gain = skip_gain.reshape(1, width)
+    starts = [blocks * GROUP * sum(counts[:k]) for k in range(len(counts) + 1)]
+    arrived = []
+    for k in range(len(counts)):
+        if k == 0:
+            leaving = turn_taps(signal, filters, blocks, counts)
+        else:
+            leaving = turn(signal, starts[k], starts[k + 1] - starts[k])
+            leaving = leaving.reshape(blocks, -1, rows)
+        arrived.append(spread(leaving))
+    taps = arrived[0][:, counts[0] * GROUP :, :]
+    own = lax.dynamic_slice_in_dim(taps, side * HALF, HALF, axis=2)
+    other = exchange(lax.dynamic_slice_in_dim(taps, (1 - side) * HALF, HALF, axis=2), "ch", 1)
     out = None
-    for k in range(chunks):
-        leaving = turn_out(signal, k, chunks).reshape(blocks, per_chunk, rows)
-        arrived = lax.all_to_all(leaving, "seq", split_axis=0, concat_axis=0, tiled=True)
-        values = convolve(taps, arrived, k)
-        back = lax.all_to_all(values, "seq", split_axis=0, concat_axis=0, tiled=True)
-        out = turn_home(back.reshape(blocks * per_chunk, rows), signal, gain, out, k, chunks)
+    for k, count in enumerate(counts):
+        values = convolve(place, own, other, arrived[k], sum(counts[:k]), count)
+        back = spread(values).reshape(-1, rows)
+        out = home(back, signal, gain, starts[k], out)
     return out
 
 
@@ -237,9 +314,10 @@
     rows, width = signal.shape
     lag_rows = filters.shape[0]
     fits = (
-        width % (blocks * CHUNKS * GROUP) == 0
-        and width % (CHUNKS * HALF) == 0
-        and rows % HALF == 0
+        blocks > 1
+        and lax.axis_size("ch") == 2
+        and width % (blocks * 2 * GROUP) == 0
+        and rows == 2 * HALF
         and lag_rows == HALF
     )
     if fits:

time: 152 us -> 131 us (0.86)
  blocking collectives: 106 us -> 0 us
  waiting for transfers between devices: 0.01 us -> 74.4 us
  starting transfers between devices: 6.36 us -> 22.8 us
  Pallas kernels: 36.4 us -> 30 us
    all_to_all x2 -> x0, blocking collectives: 106 us -> none  [the longest x1 53.9 us: fast_body(): lax.all_to_all(leaving, 'seq', split_axis=0, concat_axis=0, tiled=True)]
    all_to_all x1 -> x4, waiting for transfers between devices: 0.01 us -> 72.9 us  [spread(): lax.all_to_all(values, 'seq', split_axis=0, concat_axis=0, tiled=True)]
    all_to_all x1 -> x4, starting transfers between devices: 6.36 us -> 21.6 us  [spread(): lax.all_to_all(values, 'seq', split_axis=0, concat_axis=0, tiled=True)]
    pallas_call x3 -> x6, Pallas kernels: 36.4 us -> 30 us  [the longest x2 19.1 us: convolve(): pl.pallas_call(functools.partial(conv_kernel, first), grid=(groups,), in_...]
    ppermute x0 -> x1, waiting for transfers between devices: none -> 1.58 us  [exchange(): return lax.ppermute(values, axis, [(i, i ^ step) for i in range(size)])]
  transfers between devices with their start and end apart: 1 -> 5, of which waited for: 0 -> 5; matrix products, arithmetic and copies ran while one was open for 0% -> 1% of each run, Pallas kernels for 7% -> 19%
where the time goes in v1:
time: 131 us; the launch traced here: 130 us
  waiting for transfers between devices  74.4 us (57%)
  Pallas kernels  30 us (23%)
  starting transfers between devices  22.8 us (17%)
  local copies, waits for them, and re-layouts  2.27 us (2%)
    all_to_all x4, waiting for transfers between devices, spread(): lax.all_to_all(values, 'seq', split_axis=0, concat_axis=0, tiled=True)  72.9 us
    all_to_all x4, starting transfers between devices, spread(): lax.all_to_all(values, 'seq', split_axis=0, concat_axis=0, tiled=True)  21.6 us
    pallas_call x2, Pallas kernels, convolve(): pl.pallas_call(functools.partial(conv_kernel, first), grid=(groups,), in_...  19.1 us
    pallas_call x2, Pallas kernels, home(): pl.pallas_call(home_kernel, grid=(cols // step,), in_specs=in_specs, out_...  5.7 us
  transfers between devices with their start and end apart: 5, of which 5 were waited for; matrix products, arithmetic and copies ran while one was open for 1% of the time, Pallas kernels for 19%

profile of v1, /device:TPU:9, one launch (start us, length us, event | category | flops | bytes accessed | tf_op | source)
XLA Modules:
  0.0 130.1 jit_solution(1281693137524922658)
XLA Ops:
  0.0 2.6 %turn_taps.1 = f32[16,72,256]{2,1,0:T(8,128)} custom-call(f32[256,2048]{1,0:T(8,128)} %sig_ref.7, f32[128,256]{1,0:T(8,128)} %taps_ref.1), custom_call_target="tpu_custom_call" | custom-call | bytes 2097152 | tf_op jit(solution)/shard_map/turn_taps/pallas_call | solution.py:51
  2.6 6.6 %all-to-all-start = ((f32[16,72,256]{2,1,0:T(8,128)}), f32[16,72,256]{2,1,0:T(8,128)S(1)}, u32[]{:S(2)}, u32[]{:S(2)}) async-start(f32[16,72,256]{2,1,0:T(8,128)} %turn_taps.1), calls=%async_computation | async-start | bytes 2359296 | tf_op jit(solution)/shard_map/all_to_all | solution.py:207
  9.2 2.5 %turn.1 = f32[1024,256]{1,0:T(8,128)} custom-call(f32[256,2048]{1,0:T(8,128)} %sig_ref.7), custom_call_target="tpu_custom_call" | custom-call | bytes 2097152 | tf_op jit(solution)/shard_map/turn/pallas_call | solution.py:73
  11.7 25.0 %all-to-all-done.sig_ref = f32[16,72,256]{2,1,0:T(8,128)S(1)} async-done(((f32[16,72,256]{2,1,0:T(8,128)}), f32[16,72,256]{2,1,0:T(8,128)S(1)}, u32[]{:S(2)}, u32[]{:S(2)}) %all-to-all-start) | async-done | bytes 1179680 | tf_op jit(solution)/shard_map/all_to_all | solution.py:207
  36.7 0.0 copy-start.2
  36.7 5.1 %all-to-all-start.1 = ((f32[16,64,256]{2,1,0:T(8,128)}), f32[16,64,256]{2,1,0:T(8,128)S(1)}, u32[]{:S(2)}, u32[]{:S(2)}) async-start(f32[16,64,256]{2,1,0:T(8,128)} %bitcast.6), calls=%async_computation.1 | async-start | bytes 2097152 | tf_op jit(solution)/shard_map/all_to_all | solution.py:207
  41.8 0.6 constant_dynamic-slice_fusion
  42.5 1.2 collective-permute-start
  43.7 0.6 pad_add_fusion.place_ref
  44.3 1.6 %collective-permute-done.other_ref = f32[16,8,128]{2,1,0:T(8,128)S(1)} collective-permute-done((f32[16,8,128]{2,1,0:T(8,128)S(1)}, f32[16,8,128]{2,1,0:T(8,128)S(1)}, u32[]{:S(2)}, u32[]{:S(2)}) %collective-permute-start) | collective-permute-done | bytes 65568 | tf_op jit(solution)/shard_map/ppermute | solution.py:203
  45.9 0.0 copy-start.4
  45.9 0.0 copy-done.2
  45.9 0.6 copy-done.4
  46.5 9.6 %convolve.3 = f32[16,64,256]{2,1,0:T(8,128)} custom-call(s32[2]{0:T(128)} %pad_add_fusion.place_ref, f32[16,8,128]{2,1,0:T(8,128)} %get-tuple-element.6.own_ref, f32[16,8,128]{2,1,0:T(8,128)} %copy-done.4, f32[16,72,256]{2,1,0:T(8,128)} %copy-done.2), custom_call_target="tpu_custom_call" | custom-call | flops 3422552064 | bytes 2097152 | tf_op jit(solution)/shard_map/convolve/pallas_call | solution.py:188
  56.1 10.6 %all-to-all-done.1.sig_ref = f32[16,64,256]{2,1,0:T(8,128)S(1)} async-done(((f32[16,64,256]{2,1,0:T(8,128)}), f32[16,64,256]{2,1,0:T(8,128)S(1)}, u32[]{:S(2)}, u32[]{:S(2)}) %all-to-all-start.1) | async-done | bytes 1048608 | tf_op jit(solution)/shard_map/all_to_all | solution.py:207
  66.7 0.0 copy-start.3
  66.7 5.0 %all-to-all-start.3 = ((f32[16,64,256]{2,1,0:T(8,128)}), f32[16,64,256]{2,1,0:T(8,128)S(1)}, u32[]{:S(2)}, u32[]{:S(2)}) async-start(f32[16,64,256]{2,1,0:T(8,128)} %convolve.3), calls=%async_computation.3 | async-start | bytes 2097152 | tf_op jit(solution)/shard_map/all_to_all | solution.py:207
  71.6 0.0 copy-done.3
  71.6 9.6 %convolve.2 = f32[16,64,256]{2,1,0:T(8,128)} custom-call(s32[2]{0:T(128)} %pad_add_fusion.place_ref, f32[16,8,128]{2,1,0:T(8,128)} %get-tuple-element.6.own_ref, f32[16,8,128]{2,1,0:T(8,128)} %copy-done.4, f32[16,64,256]{2,1,0:T(8,128)} %copy-done.3), custom_call_target="tpu_custom_call" | custom-call | flops 3422552064 | bytes 2097152 | tf_op jit(solution)/shard_map/convolve/pallas_call | solution.py:188
  81.2 15.3 %all-to-all-done.3 = f32[16,64,256]{2,1,0:T(8,128)S(1)} async-done(((f32[16,64,256]{2,1,0:T(8,128)}), f32[16,64,256]{2,1,0:T(8,128)S(1)}, u32[]{:S(2)}, u32[]{:S(2)}) %all-to-all-start.3) | async-done | bytes 1048608 | tf_op jit(solution)/shard_map/all_to_all | solution.py:207
  96.5 0.0 copy-start
  96.5 5.0 %all-to-all-start.2 = ((f32[16,64,256]{2,1,0:T(8,128)}), f32[16,64,256]{2,1,0:T(8,128)S(1)}, u32[]{:S(2)}, u32[]{:S(2)}) async-start(f32[16,64,256]{2,1,0:T(8,128)} %convolve.2), calls=%async_computation.2 | async-start | bytes 2097152 | tf_op jit(solution)/shard_map/all_to_all | solution.py:207
  101.5 0.0 copy-done
  101.5 2.9 %home.2.rest_0_ = f32[256,2048]{1,0:T(8,128)} custom-call(f32[1024,256]{1,0:T(8,128)} %bitcast.7, f32[256,2048]{1,0:T(8,128)} %sig_ref.7, f32[1,2048]{1,0:T(1,128)} %bitcast.9), custom_call_target="tpu_custom_call" | custom-call | bytes 3145728 | tf_op jit(solution)/shard_map/home/pallas_call | solution.py:105
  104.3 22.0 %all-to-all-done.2 = f32[16,64,256]{2,1,0:T(8,128)S(1)} async-done(((f32[16,64,256]{2,1,0:T(8,128)}), f32[16,64,256]{2,1,0:T(8,128)S(1)}, u32[]{:S(2)}, u32[]{:S(2)}) %all-to-all-start.2) | async-done | bytes 1048608 | tf_op jit(solution)/shard_map/all_to_all | solution.py:207
  126.3 0.0 copy-start.1
  126.3 1.0 copy-done.1
  127.3 2.9 %home.3 = f32[256,2048]{1,0:T(8,128)} custom-call(f32[1024,256]{1,0:T(8,128)} %bitcast.8, f32[256,2048]{1,0:T(8,128)} %sig_ref.7, f32[1,2048]{1,0:T(1,128)} %bitcast.10, f32[256,2048]{1,0:T(8,128)} %home.2.rest_0_), custom_call_target="tpu_custom_call", output_to_operand_aliasing={{}: (3, {})} | custom-call | bytes 3145728 | tf_op jit(solution)/shard_map/home/pallas_call | solution.py:105
  (1 shorter events, 0.0 us)
Async XLA Ops:
  2.6 34.1 %all-to-all-start = ((f32[16,72,256]{2,1,0:T(8,128)}), f32[16,72,256]{2,1,0:T(8,128)S(1)}, u32[]{:S(2)}, u32[]{:S(2)}) async-start(f32[16,72,256]{2,1,0:T(8,128)} %turn_taps.1), calls=%async_computation | async-start | bytes 2359296 | tf_op jit(solution)/shard_map/all_to_all | solution.py:207
  36.7 9.2 %copy-start.2 = (f32[16,72,256]{2,1,0:T(8,128)}, f32[16,72,256]{2,1,0:T(8,128)S(1)}, u32[]{:S(2)}) copy-start(f32[16,72,256]{2,1,0:T(8,128)S(1)} %all-to-all-done.sig_ref) | copy-start | bytes 3538948
  36.7 29.9 %all-to-all-start.1 = ((f32[16,64,256]{2,1,0:T(8,128)}), f32[16,64,256]{2,1,0:T(8,128)S(1)}, u32[]{:S(2)}, u32[]{:S(2)}) async-start(f32[16,64,256]{2,1,0:T(8,128)} %bitcast.6), calls=%async_computation.1 | async-start | bytes 2097152 | tf_op jit(solution)/shard_map/all_to_all | solution.py:207
  42.5 3.4 %collective-permute-start = (f32[16,8,128]{2,1,0:T(8,128)S(1)}, f32[16,8,128]{2,1,0:T(8,128)S(1)}, u32[]{:S(2)}, u32[]{:S(2)}) collective-permute-start(f32[16,8,128]{2,1,0:T(8,128)S(1)} %get-tuple-element.5), channel_id=1, source_target_pairs={{0,1},{1,0},{2,3},{3,2},{4,5},{5,4},{6,7},{7,6},{8,9},{9,8},{10,11... | collective-permute-start | bytes 196616 | tf_op jit(solution)/shard_map/ppermute | solution.py:203
  45.9 0.6 copy-start.4
  66.7 5.0 %copy-start.3 = (f32[16,64,256]{2,1,0:T(8,128)}, f32[16,64,256]{2,1,0:T(8,128)S(1)}, u32[]{:S(2)}) copy-start(f32[16,64,256]{2,1,0:T(8,128)S(1)} %all-to-all-done.1.sig_ref) | copy-start | bytes 3145732
  66.7 29.8 %all-to-all-start.3 = ((f32[16,64,256]{2,1,0:T(8,128)}), f32[16,64,256]{2,1,0:T(8,128)S(1)}, u32[]{:S(2)}, u32[]{:S(2)}) async-start(f32[16,64,256]{2,1,0:T(8,128)} %convolve.3), calls=%async_computation.3 | async-start | bytes 2097152 | tf_op jit(solution)/shard_map/all_to_all | solution.py:207
  96.5 5.0 %copy-start = (f32[16,64,256]{2,1,0:T(8,128)}, f32[16,64,256]{2,1,0:T(8,128)S(1)}, u32[]{:S(2)}) copy-start(f32[16,64,256]{2,1,0:T(8,128)S(1)} %all-to-all-done.3) | copy-start | bytes 3145732
  96.5 29.8 %all-to-all-start.2 = ((f32[16,64,256]{2,1,0:T(8,128)}), f32[16,64,256]{2,1,0:T(8,128)S(1)}, u32[]{:S(2)}, u32[]{:S(2)}) async-start(f32[16,64,256]{2,1,0:T(8,128)} %convolve.2), calls=%async_computation.2 | async-start | bytes 2097152 | tf_op jit(solution)/shard_map/all_to_all | solution.py:207
  126.3 1.0 copy-start.1

commit v2 on v1

--- a/solution.py
+++ b/solution.py
@@ -10,6 +10,7 @@
 
 GROUP = 16
 HALF = 128
+PAIR = 2
 VMEM_BYTES = 60 * 1024 * 1024
 
 HIGHEST_PRECISION = lax.Precision.HIGHEST
@@ -115,9 +116,8 @@
     )(*operands)
 
 
-def convolve_group(side, group, own_ref, other_ref, signal, high_ref, low_ref, sum_ref):
+def shifted_taps(side, group, own_ref, other_ref, high_ref, low_ref):
     blocks = own_ref.shape[0]
-    rows = signal.shape[1]
 
     def line(ref, q):
         return jnp.broadcast_to(ref[q, pl.ds(group, 1), :], (8, HALF))
@@ -136,6 +136,11 @@
         high, low = split_halves(pair)
         high_ref[16 * p : 16 * p + 16, :] = high
         low_ref[16 * p : 16 * p + 16, :] = low
+
+
+def causal_sums(signal, high_ref, low_ref, sum_ref):
+    rows = signal.shape[1]
+    blocks = signal.shape[0] // GROUP
     sig_high, sig_low = split_halves(signal)
 
     def window(ref, lag_block):
@@ -157,45 +162,85 @@
             sum_ref[d * GROUP :, :] += term
 
 
-def conv_kernel(first, place_ref, own_ref, other_ref, sig_ref, out_ref, high_ref, low_ref, sum_ref):
+def conv_kernel(first, place_ref, own_ref, other_ref, sig_ref, *rest):
+    outs, scratch = rest[: -3 * PAIR], rest[-3 * PAIR :]
     blocks, _, rows = sig_ref.shape
-    signal = sig_ref[...].reshape(blocks * GROUP, rows)
-    group = first + pl.program_id(0)
-    convolve_group(place_ref[1], group, own_ref, other_ref, signal, high_ref, low_ref, sum_ref)
-    out_ref[...] = sum_ref[...].reshape(blocks, GROUP, rows)
-
-
-def conv_scratch(blocks, rows):
+    me, side = place_ref[0], place_ref[1]
+    for u in range(PAIR):
+        group = first + PAIR * pl.program_id(0) + u
+        shifted_taps(side, group, own_ref, other_ref, scratch[3 * u], scratch[3 * u + 1])
+    for u in range(PAIR):
+        high_ref, low_ref, sum_ref = scratch[3 * u : 3 * u + 3]
+        at = slice(u * GROUP, (u + 1) * GROUP)
+        causal_sums(sig_ref[:, at, :].reshape(blocks * GROUP, rows), high_ref, low_ref, sum_ref)
+        if len(outs) == 1:
+            outs[0][:, at, :] = sum_ref[...].reshape(blocks, GROUP, rows)
+            continue
+        for j in range(blocks):
+            row = pl.multiple_of((me ^ j) * GROUP, GROUP)
+            outs[j][at, :] = sum_ref[pl.ds(row, GROUP), :]
+
+
+def convolve(place, own, other, arrived, first, groups, apart):
+    blocks, _, rows = arrived.shape
+    spec = pl.BlockSpec((blocks, PAIR * GROUP, rows), lambda g: (0, g, 0))
+    taps_spec = pl.BlockSpec(own.shape, lambda g: (0, 0, 0))
+    out_specs, shapes = [spec], [(blocks, groups * GROUP, rows)]
+    if apart:
+        out_specs = [pl.BlockSpec((PAIR * GROUP, rows), lambda g: (g, 0))] * blocks
+        shapes = [(groups * GROUP, rows)] * blocks
     lanes = blocks * rows + 2 * HALF
-    return [
+    scratch = [
         pltpu.VMEM((HALF, lanes), jnp.bfloat16),
         pltpu.VMEM((HALF, lanes), jnp.bfloat16),
         pltpu.VMEM((blocks * GROUP, rows), jnp.float32),
     ]
-
-
-def conv_cost(blocks, groups, rows):
-    products = 3 * groups * GROUP * rows * rows * blocks * (blocks + 1)
-    return pl.CostEstimate(
-        flops=products, bytes_accessed=8 * blocks * groups * GROUP * rows, transcendentals=0
-    )
-
-
-def convolve(place, own, other, arrived, first, groups):
-    blocks, _, rows = arrived.shape
-    spec = pl.BlockSpec((blocks, GROUP, rows), lambda g: (0, g, 0))
-    taps_spec = pl.BlockSpec(own.shape, lambda g: (0, 0, 0))
     return pl.pallas_call(
         functools.partial(conv_kernel, first),
-        grid=(groups,),
+        grid=(groups // PAIR,),
         in_specs=[pl.BlockSpec(memory_space=pltpu.SMEM), taps_spec, taps_spec, spec],
-        out_specs=spec,
-        out_shape=jax.ShapeDtypeStruct((blocks, groups * GROUP, rows), jnp.float32),
-        scratch_shapes=conv_scratch(blocks, rows),
-        compiler_params=pltpu.CompilerParams(vmem_limit_bytes=VMEM_BYTES),
-        cost_estimate=conv_cost(blocks, groups, rows),
+        out_specs=out_specs,
+        out_shape=[jax.ShapeDtypeStruct(shape, jnp.float32) for shape in shapes],
+        scratch_shapes=scratch * PAIR,
+        compiler_params=pltpu.CompilerParams(vmem_limit_bytes=VMEM_BYTES),
+        cost_estimate=pl.CostEstimate(
+            flops=3 * groups * GROUP * rows * rows * blocks * (blocks + 1),
+            bytes_accessed=8 * blocks * groups * GROUP * rows,
+            transcendentals=0,
+        ),
         name="convolve",
     )(place, own, other, arrived)
+
+
+def home_apart_kernel(place_ref, *rest):
+    back_refs, (sig_ref, gain_ref, _, out_ref, hold_ref) = rest[:-5], rest[-5:]
+    me = place_ref[0]
+    for j, back_ref in enumerate(back_refs):
+        hold_ref[me ^ j] = back_ref[...]
+    values = hold_ref[...].reshape(sig_ref.shape[1], sig_ref.shape[0])
+    out_ref[...] = values.T + gain_ref[...] * sig_ref[...]
+
+
+def home_apart(place, backs, signal, gain, partial_out):
+    rows, width = signal.shape
+    blocks, per_chunk = len(backs), backs[0].shape[0]
+    cols = blocks * per_chunk
+    here = lambda i: (0, 1)
+    return pl.pallas_call(
+        home_apart_kernel,
+        grid=(1,),
+        in_specs=[pl.BlockSpec(memory_space=pltpu.SMEM)]
+        + [pl.BlockSpec((per_chunk, rows), lambda i: (0, 0))] * blocks
+        + [pl.BlockSpec((rows, cols), here), pl.BlockSpec((1, cols), here)]
+        + [pl.BlockSpec(memory_space=pl.ANY)],
+        out_specs=pl.BlockSpec((rows, cols), here),
+        out_shape=jax.ShapeDtypeStruct((rows, width), jnp.float32),
+        input_output_aliases={blocks + 3: 0},
+        scratch_shapes=[pltpu.VMEM((blocks, per_chunk, rows), jnp.float32)],
+        compiler_params=pltpu.CompilerParams(vmem_limit_bytes=VMEM_BYTES),
+        cost_estimate=pl.CostEstimate(flops=0, bytes_accessed=12 * rows * cols, transcendentals=0),
+        name="home_apart",
+    )(place, *backs, signal, gain, partial_out)
 
 
 def exchange(values, axis, step):
@@ -207,31 +252,29 @@
     return lax.all_to_all(values, "seq", split_axis=0, concat_axis=0, tiled=True)
 
 
+def after(value, *others):
+    return lax.optimization_barrier((value, *others))[0]
+
+
 def fast_body(signal, filters, skip_gain):
     blocks = lax.axis_size("seq")
     rows, width = signal.shape
-    counts = (width // blocks // GROUP // 2,) * 2
+    count = width // blocks // GROUP // 2
+    cols = width // 2
     side = lax.axis_index("ch")
     place = jnp.stack([lax.axis_index("seq"), side]).astype(jnp.int32)
     gain = skip_gain.reshape(1, width)
-    starts = [blocks * GROUP * sum(counts[:k]) for k in range(len(counts) + 1)]
-    arrived = []
-    for k in range(len(counts)):
-        if k == 0:
-            leaving = turn_taps(signal, filters, blocks, counts)
-        else:
-            leaving = turn(signal, starts[k], starts[k + 1] - starts[k])
-            leaving = leaving.reshape(blocks, -1, rows)
-        arrived.append(spread(leaving))
-    taps = arrived[0][:, counts[0] * GROUP :, :]
+    first = spread(turn_taps(signal, filters, blocks, (count, count)))
+    second = spread(turn(signal, cols, cols).reshape(blocks, -1, rows))
+    taps = first[:, count * GROUP :, :]
     own = lax.dynamic_slice_in_dim(taps, side * HALF, HALF, axis=2)
     other = exchange(lax.dynamic_slice_in_dim(taps, (1 - side) * HALF, HALF, axis=2), "ch", 1)
-    out = None
-    for k, count in enumerate(counts):
-        values = convolve(place, own, other, arrived[k], sum(counts[:k]), count)
-        back = spread(values).reshape(-1, rows)
-        out = home(back, signal, gain, starts[k], out)
-    return out
+    (values,) = convolve(place, own, other, first, 0, count, False)
+    back = spread(values).reshape(-1, rows)
+    parts = convolve(place, own, other, second, count, count, True)
+    parts = [exchange(part, "seq", j) if j else part for j, part in enumerate(parts)]
+    out = home(back, signal, gain, 0, None)
+    return home_apart(place, parts, signal, gain, out)
 
 
 def angle_table(row_count, col_count, length, sign):
@@ -315,8 +358,9 @@
     lag_rows = filters.shape[0]
     fits = (
         blocks > 1
+        and blocks & (blocks - 1) == 0
         and lax.axis_size("ch") == 2
-        and width % (blocks * 2 * GROUP) == 0
+        and width % (blocks * 2 * PAIR * GROUP) == 0
         and rows == 2 * HALF
         and lag_rows == HALF
     )

time: 131 us -> 124 us (0.947)
  waiting for transfers between devices: 74.4 us -> 51.9 us
  starting transfers between devices: 22.8 us -> 43.1 us
  Pallas kernels: 30 us -> 25 us
    all_to_all x4 -> x3, waiting for transfers between devices: 72.9 us -> 38.3 us  [spread(): lax.all_to_all(values, 'seq', split_axis=0, concat_axis=0, tiled=True)]
    ppermute x1 -> x16, starting transfers between devices: 1.24 us -> 26.5 us  [exchange(): return lax.ppermute(values, axis, [(i, i ^ step) for i in range(size)])]
    ppermute x1 -> x16, waiting for transfers between devices: 1.58 us -> 13.6 us  [exchange(): return lax.ppermute(values, axis, [(i, i ^ step) for i in range(size)])]
    all_to_all x4 -> x3, starting transfers between devices: 21.6 us -> 16.6 us  [spread(): lax.all_to_all(values, 'seq', split_axis=0, concat_axis=0, tiled=True)]
    pallas_call x2 -> x1, Pallas kernels: 5.7 us -> 2.85 us  [home(): pl.pallas_call(home_kernel, grid=(cols // step,), in_specs=in_specs, out_...]
    pallas_call x2 -> x3, Pallas kernels: 19.1 us -> 17 us  [the longest x2 14 us: convolve(): pl.pallas_call(functools.partial(conv_kernel, first), grid=(groups // PAI...]
  transfers between devices with their start and end apart: 5 -> 19, of which waited for: 5 -> 11; matrix products, arithmetic and copies ran while one was open for 1% -> 1% of each run, Pallas kernels for 19% -> 16%
where the time goes in v2:
time: 124 us
  waiting for transfers between devices  51.9 us (42%)
  starting transfers between devices  43.1 us (35%)
  Pallas kernels  25 us (20%)
  local copies, waits for them, and re-layouts  2.85 us (2%)
    all_to_all x3, waiting for transfers between devices, spread(): lax.all_to_all(values, 'seq', split_axis=0, concat_axis=0, tiled=True)  38.3 us
    ppermute x16, starting transfers between devices, exchange(): return lax.ppermute(values, axis, [(i, i ^ step) for i in range(size)])  26.5 us
    all_to_all x3, starting transfers between devices, spread(): lax.all_to_all(values, 'seq', split_axis=0, concat_axis=0, tiled=True)  16.6 us
    pallas_call x2, Pallas kernels, convolve(): pl.pallas_call(functools.partial(conv_kernel, first), grid=(groups // PAI...  14 us
    ppermute x16, waiting for transfers between devices, exchange(): return lax.ppermute(values, axis, [(i, i ^ step) for i in range(size)])  13.6 us
    pallas_call x1, Pallas kernels, home_apart(): pl.pallas_call(home_apart_kernel, grid=(1,), in_specs=[pl.BlockSpec(memor...  3.06 us
    pallas_call x1, Pallas kernels, home(): pl.pallas_call(home_kernel, grid=(cols // step,), in_specs=in_specs, out_...  2.85 us
    pallas_call x1, Pallas kernels, turn_taps(): pl.pallas_call(functools.partial(turn_taps_kernel, counts), grid=(1,), in...  2.61 us
  transfers between devices with their start and end apart: 19, of which 11 were waited for; matrix products, arithmetic and copies ran while one was open for 1% of the time, Pallas kernels for 16%

profile of v2, /device:TPU:9, one launch (start us, length us, event | category | flops | bytes accessed | tf_op | source)
XLA Modules:
  0.0 123.6 jit_solution(4807133318730380438)
XLA Ops:
  0.0 2.6 %turn_taps.1 = f32[16,72,256]{2,1,0:T(8,128)} custom-call(f32[256,2048]{1,0:T(8,128)} %rest_16_.1, f32[128,256]{1,0:T(8,128)} %taps_ref.1), custom_call_target="tpu_custom_call" | custom-call | bytes 2097152 | tf_op jit(solution)/shard_map/turn_taps/pallas_call | solution.py:52
  2.6 6.6 %all-to-all-start = ((f32[16,72,256]{2,1,0:T(8,128)}), f32[16,72,256]{2,1,0:T(8,128)S(1)}, u32[]{:S(2)}, u32[]{:S(2)}) async-start(f32[16,72,256]{2,1,0:T(8,128)} %turn_taps.1), calls=%async_computation | async-start | bytes 2359296 | tf_op jit(solution)/shard_map/all_to_all | solution.py:252
  9.2 2.5 %turn.1 = f32[1024,256]{1,0:T(8,128)} custom-call(f32[256,2048]{1,0:T(8,128)} %rest_16_.1), custom_call_target="tpu_custom_call" | custom-call | bytes 2097152 | tf_op jit(solution)/shard_map/turn/pallas_call | solution.py:74
  11.7 25.0 %all-to-all-done.sig_ref = f32[16,72,256]{2,1,0:T(8,128)S(1)} async-done(((f32[16,72,256]{2,1,0:T(8,128)}), f32[16,72,256]{2,1,0:T(8,128)S(1)}, u32[]{:S(2)}, u32[]{:S(2)}) %all-to-all-start) | async-done | bytes 1179680 | tf_op jit(solution)/shard_map/all_to_all | solution.py:252
  36.7 5.1 %all-to-all-start.1 = ((f32[16,64,256]{2,1,0:T(8,128)}), f32[16,64,256]{2,1,0:T(8,128)S(1)}, u32[]{:S(2)}, u32[]{:S(2)}) async-start(f32[16,64,256]{2,1,0:T(8,128)} %bitcast.6), calls=%async_computation.1 | async-start | bytes 2097152 | tf_op jit(solution)/shard_map/all_to_all | solution.py:252
  42.5 1.2 %collective-permute-start = (f32[16,8,128]{2,1,0:T(8,128)S(1)}, f32[16,8,128]{2,1,0:T(8,128)S(1)}, u32[]{:S(2)}, u32[]{:S(2)}) collective-permute-start(f32[16,8,128]{2,1,0:T(8,128)S(1)} %get-tuple-element.37), channel_id=1, source_target_pairs={{0,1},{1,0},{2,3},{3,2},{4,5},{5,4},{6,7},{7,6},{8,9},{9,8},{10,11... | collective-permute-start | bytes 196616 | tf_op jit(solution)/shard_map/ppermute | solution.py:248
  44.3 1.6 %collective-permute-done.other_ref = f32[16,8,128]{2,1,0:T(8,128)S(1)} collective-permute-done((f32[16,8,128]{2,1,0:T(8,128)S(1)}, f32[16,8,128]{2,1,0:T(8,128)S(1)}, u32[]{:S(2)}, u32[]{:S(2)}) %collective-permute-start) | collective-permute-done | bytes 65568 | tf_op jit(solution)/shard_map/ppermute | solution.py:248
  46.5 6.9 %convolve.3 = f32[16,64,256]{2,1,0:T(8,128)} custom-call(s32[2]{0:T(128)} %pad_add_fusion.place_ref, f32[16,8,128]{2,1,0:T(8,128)} %get-tuple-element.38.own_ref, f32[16,8,128]{2,1,0:T(8,128)} %copy-done.18, f32[16,72,256]{2,1,0:T(8,128)} %copy-done.1), custom_call_target="tpu_custom_call" | custom-call | flops 3422552064 | bytes 2097152 | tf_op jit(solution)/shard_map/convolve/pallas_call | solution.py:198
  53.4 13.2 %all-to-all-done.1.sig_ref = f32[16,64,256]{2,1,0:T(8,128)S(1)} async-done(((f32[16,64,256]{2,1,0:T(8,128)}), f32[16,64,256]{2,1,0:T(8,128)S(1)}, u32[]{:S(2)}, u32[]{:S(2)}) %all-to-all-start.1) | async-done | bytes 1048608 | tf_op jit(solution)/shard_map/all_to_all | solution.py:252
  66.7 5.0 %all-to-all-start.2 = ((f32[16,64,256]{2,1,0:T(8,128)}), f32[16,64,256]{2,1,0:T(8,128)S(1)}, u32[]{:S(2)}, u32[]{:S(2)}) async-start(f32[16,64,256]{2,1,0:T(8,128)} %convolve.3), calls=%async_computation.2 | async-start | bytes 2097152 | tf_op jit(solution)/shard_map/all_to_all | solution.py:252
  71.6 7.1 %convolve.2 = (f32[64,256]{1,0:T(8,128)}, f32[64,256]{1,0:T(8,128)}, f32[64,256]{1,0:T(8,128)}, f32[64,256]{1,0:T(8,128)}, f32[64,256]{1,0:T(8,128)}, /*index=5*...) custom-call(s32[2]{0:T(128)} %pad_add_fusion.place_ref, ...), custom_call_target="tpu_custom_call" | custom-call | flops 3422552064 | bytes 2097152 | tf_op jit(solution)/shard_map/convolve/pallas_call | solution.py:198
  79.1 1.2 collective-permute-start.2
  81.0 1.6 %collective-permute-start.5 = (f32[64,256]{1,0:T(8,128)}, f32[64,256]{1,0:T(8,128)S(1)}, u32[]{:S(2)}, u32[]{:S(2)}) collective-permute-start(f32[64,256]{1,0:T(8,128)} %get-tuple-element.26), channel_id=1, source_target_pairs={{0,10},{2,8},{4,14},{6,12},{8,2},{10,0},{12,6},{14,4},{16,26},{18,... | collective-permute-start | bytes 196616 | tf_op jit(solution)/shard_map/ppermute | solution.py:248
  82.6 1.2 collective-permute-start.6
  83.8 1.2 %collective-permute-done.2.rest_2_ = f32[64,256]{1,0:T(8,128)S(1)} collective-permute-done((f32[64,256]{1,0:T(8,128)}, f32[64,256]{1,0:T(8,128)S(1)}, u32[]{:S(2)}, u32[]{:S(2)}) %collective-permute-start.2) | collective-permute-done | bytes 65568 | tf_op jit(solution)/shard_map/ppermute | solution.py:248
  85.1 2.0 %collective-permute-start.7 = (f32[64,256]{1,0:T(8,128)}, f32[64,256]{1,0:T(8,128)S(1)}, u32[]{:S(2)}, u32[]{:S(2)}) collective-permute-start(f32[64,256]{1,0:T(8,128)} %get-tuple-element.28), channel_id=1, source_target_pairs={{0,14},{2,12},{4,10},{6,8},{8,6},{10,4},{12,2},{14,0},{16,30},{18,... | collective-permute-start | bytes 196616 | tf_op jit(solution)/shard_map/ppermute | solution.py:248
  87.0 0.8 collective-permute-done.3.rest_3_
  87.9 1.0 collective-permute-start.8
  88.9 2.6 %collective-permute-done.4.rest_4_ = f32[64,256]{1,0:T(8,128)S(1)} collective-permute-done((f32[64,256]{1,0:T(8,128)}, f32[64,256]{1,0:T(8,128)S(1)}, u32[]{:S(2)}, u32[]{:S(2)}) %collective-permute-start.4) | collective-permute-done | bytes 65568 | tf_op jit(solution)/shard_map/ppermute | solution.py:248
  91.5 2.2 %collective-permute-start.9 = (f32[64,256]{1,0:T(8,128)}, f32[64,256]{1,0:T(8,128)S(1)}, u32[]{:S(2)}, u32[]{:S(2)}) collective-permute-start(f32[64,256]{1,0:T(8,128)} %get-tuple-element.30), channel_id=1, source_target_pairs={{0,18},{2,16},{4,22},{6,20},{8,26},{10,24},{12,30},{14,28},{16,2},... | collective-permute-start | bytes 196616 | tf_op jit(solution)/shard_map/ppermute | solution.py:248
  93.7 2.0 %collective-permute-start.10 = (f32[64,256]{1,0:T(8,128)}, f32[64,256]{1,0:T(8,128)S(1)}, u32[]{:S(2)}, u32[]{:S(2)}) collective-permute-start(f32[64,256]{1,0:T(8,128)} %get-tuple-element.31), channel_id=1, source_target_pairs={{0,20},{2,22},{4,16},{6,18},{8,28},{10,30},{12,24},{14,26},{16,4},... | collective-permute-start | bytes 196616 | tf_op jit(solution)/shard_map/ppermute | solution.py:248
  95.7 1.8 %collective-permute-start.11 = (f32[64,256]{1,0:T(8,128)}, f32[64,256]{1,0:T(8,128)S(1)}, u32[]{:S(2)}, u32[]{:S(2)}) collective-permute-start(f32[64,256]{1,0:T(8,128)} %get-tuple-element.32), channel_id=1, source_target_pairs={{0,22},{2,20},{4,18},{6,16},{8,30},{10,28},{12,26},{14,24},{16,6},... | collective-permute-start | bytes 196616 | tf_op jit(solution)/shard_map/ppermute | solution.py:248
  97.9 2.0 %collective-permute-start.12 = (f32[64,256]{1,0:T(8,128)}, f32[64,256]{1,0:T(8,128)S(1)}, u32[]{:S(2)}, u32[]{:S(2)}) collective-permute-start(f32[64,256]{1,0:T(8,128)} %get-tuple-element.33), channel_id=1, source_target_pairs={{0,24},{2,26},{4,28},{6,30},{8,16},{10,18},{12,20},{14,22},{16,8},... | collective-permute-start | bytes 196616 | tf_op jit(solution)/shard_map/ppermute | solution.py:248
  100.0 5.4 %collective-permute-start.13 = (f32[64,256]{1,0:T(8,128)}, f32[64,256]{1,0:T(8,128)S(1)}, u32[]{:S(2)}, u32[]{:S(2)}) collective-permute-start(f32[64,256]{1,0:T(8,128)} %get-tuple-element.34), channel_id=1, source_target_pairs={{0,26},{2,24},{4,30},{6,28},{8,18},{10,16},{12,22},{14,20},{16,10}... | collective-permute-start | bytes 196616 | tf_op jit(solution)/shard_map/ppermute | solution.py:248
  105.4 1.2 collective-permute-start.14
  106.6 2.5 %collective-permute-start.15 = (f32[64,256]{1,0:T(8,128)}, f32[64,256]{1,0:T(8,128)S(1)}, u32[]{:S(2)}, u32[]{:S(2)}) collective-permute-start(f32[64,256]{1,0:T(8,128)} %get-tuple-element.36), channel_id=1, source_target_pairs={{0,30},{2,28},{4,26},{6,24},{8,22},{10,20},{12,18},{14,16},{16,14}... | collective-permute-start | bytes 196616 | tf_op jit(solution)/shard_map/ppermute | solution.py:248
  109.1 1.0 copy-done
  110.1 2.9 %home.1.rest_18_ = f32[256,2048]{1,0:T(8,128)} custom-call(f32[1024,256]{1,0:T(8,128)} %bitcast.5, f32[256,2048]{1,0:T(8,128)} %rest_16_.1, f32[1,2048]{1,0:T(1,128)} %bitcast.7), custom_call_target="tpu_custom_call" | custom-call | bytes 3145728 | tf_op jit(solution)/shard_map/home/pallas_call | solution.py:106
  113.0 3.7 %collective-permute-done.13.rest_13_ = f32[64,256]{1,0:T(8,128)S(1)} collective-permute-done((f32[64,256]{1,0:T(8,128)}, f32[64,256]{1,0:T(8,128)S(1)}, u32[]{:S(2)}, u32[]{:S(2)}) %collective-permute-start.13) | collective-permute-done | bytes 65568 | tf_op jit(solution)/shard_map/ppermute | solution.py:248
  116.7 1.7 %collective-permute-done.14.rest_14_ = f32[64,256]{1,0:T(8,128)S(1)} collective-permute-done((f32[64,256]{1,0:T(8,128)}, f32[64,256]{1,0:T(8,128)S(1)}, u32[]{:S(2)}, u32[]{:S(2)}) %collective-permute-start.14) | collective-permute-done | bytes 65568 | tf_op jit(solution)/shard_map/ppermute | solution.py:248
  118.3 1.6 %collective-permute-done.15.rest_15_ = f32[64,256]{1,0:T(8,128)S(1)} collective-permute-done((f32[64,256]{1,0:T(8,128)}, f32[64,256]{1,0:T(8,128)S(1)}, u32[]{:S(2)}, u32[]{:S(2)}) %collective-permute-start.15) | collective-permute-done | bytes 65568 | tf_op jit(solution)/shard_map/ppermute | solution.py:248
  120.6 3.1 %home_apart.1 = f32[256,2048]{1,0:T(8,128)} custom-call(s32[2]{0:T(128)} %pad_add_fusion.place_ref, f32[64,256]{1,0:T(8,128)} %get-tuple-element.21.rest_0_, f32[64,256]{1,0:T(8,128)} %copy-done.3, f32[64,256]{1,0:T(8,128)} %copy-done.4, f32[64,256]{1,0:T(8,128)} %copy-done.5, f32[64,256]{1,0:T(8,128)} %copy-done.6, ...), custom_call_target="tpu_custom_call", output_to_operand_aliasing={{}: (19, {})} | custom-call | bytes 3145728 | tf_op jit(solution)/shard_map/home_apart/pallas_call | solution.py:229
  (53 shorter events, 4.0 us)
Async XLA Ops:
  2.6 34.1 %all-to-all-start = ((f32[16,72,256]{2,1,0:T(8,128)}), f32[16,72,256]{2,1,0:T(8,128)S(1)}, u32[]{:S(2)}, u32[]{:S(2)}) async-start(f32[16,72,256]{2,1,0:T(8,128)} %turn_taps.1), calls=%async_computation | async-start | bytes 2359296 | tf_op jit(solution)/shard_map/all_to_all | solution.py:252
  36.7 9.2 %copy-start.1 = (f32[16,72,256]{2,1,0:T(8,128)}, f32[16,72,256]{2,1,0:T(8,128)S(1)}, u32[]{:S(2)}) copy-start(f32[16,72,256]{2,1,0:T(8,128)S(1)} %all-to-all-done.sig_ref) | copy-start | bytes 3538948
  36.7 29.9 %all-to-all-start.1 = ((f32[16,64,256]{2,1,0:T(8,128)}), f32[16,64,256]{2,1,0:T(8,128)S(1)}, u32[]{:S(2)}, u32[]{:S(2)}) async-start(f32[16,64,256]{2,1,0:T(8,128)} %bitcast.6), calls=%async_computation.1 | async-start | bytes 2097152 | tf_op jit(solution)/shard_map/all_to_all | solution.py:252
  42.5 3.4 %collective-permute-start = (f32[16,8,128]{2,1,0:T(8,128)S(1)}, f32[16,8,128]{2,1,0:T(8,128)S(1)}, u32[]{:S(2)}, u32[]{:S(2)}) collective-permute-start(f32[16,8,128]{2,1,0:T(8,128)S(1)} %get-tuple-element.37), channel_id=1, source_target_pairs={{0,1},{1,0},{2,3},{3,2},{4,5},{5,4},{6,7},{7,6},{8,9},{9,8},{10,11... | collective-permute-start | bytes 196616 | tf_op jit(solution)/shard_map/ppermute | solution.py:248
  66.7 42.4 %all-to-all-start.2 = ((f32[16,64,256]{2,1,0:T(8,128)}), f32[16,64,256]{2,1,0:T(8,128)S(1)}, u32[]{:S(2)}, u32[]{:S(2)}) async-start(f32[16,64,256]{2,1,0:T(8,128)} %convolve.3), calls=%async_computation.2 | async-start | bytes 2097152 | tf_op jit(solution)/shard_map/all_to_all | solution.py:252
  78.7 3.9 %collective-permute-start.1 = (f32[64,256]{1,0:T(8,128)}, f32[64,256]{1,0:T(8,128)S(1)}, u32[]{:S(2)}, u32[]{:S(2)}) collective-permute-start(f32[64,256]{1,0:T(8,128)} %get-tuple-element.22), channel_id=1, source_target_pairs={{0,2},{2,0},{4,6},{6,4},{8,10},{10,8},{12,14},{14,12},{16,18},{18,... | collective-permute-start | bytes 196616 | tf_op jit(solution)/shard_map/ppermute | solution.py:248
  79.1 5.9 %collective-permute-start.2 = (f32[64,256]{1,0:T(8,128)}, f32[64,256]{1,0:T(8,128)S(1)}, u32[]{:S(2)}, u32[]{:S(2)}) collective-permute-start(f32[64,256]{1,0:T(8,128)} %get-tuple-element.23), channel_id=1, source_target_pairs={{0,4},{2,6},{4,0},{6,2},{8,12},{10,14},{12,8},{14,10},{16,20},{18,... | collective-permute-start | bytes 196616 | tf_op jit(solution)/shard_map/ppermute | solution.py:248
  80.3 7.5 %collective-permute-start.3 = (f32[64,256]{1,0:T(8,128)}, f32[64,256]{1,0:T(8,128)S(1)}, u32[]{:S(2)}, u32[]{:S(2)}) collective-permute-start(f32[64,256]{1,0:T(8,128)} %get-tuple-element.24), channel_id=1, source_target_pairs={{0,6},{2,4},{4,2},{6,0},{8,14},{10,12},{12,10},{14,8},{16,22},{18,... | collective-permute-start | bytes 196616 | tf_op jit(solution)/shard_map/ppermute | solution.py:248
  80.9 10.6 %collective-permute-start.4 = (f32[64,256]{1,0:T(8,128)}, f32[64,256]{1,0:T(8,128)S(1)}, u32[]{:S(2)}, u32[]{:S(2)}) collective-permute-start(f32[64,256]{1,0:T(8,128)} %get-tuple-element.25), channel_id=1, source_target_pairs={{0,8},{2,10},{4,12},{6,14},{8,0},{10,2},{12,4},{14,6},{16,24},{18,... | collective-permute-start | bytes 196616 | tf_op jit(solution)/shard_map/ppermute | solution.py:248
  81.0 12.7 %collective-permute-start.5 = (f32[64,256]{1,0:T(8,128)}, f32[64,256]{1,0:T(8,128)S(1)}, u32[]{:S(2)}, u32[]{:S(2)}) collective-permute-start(f32[64,256]{1,0:T(8,128)} %get-tuple-element.26), channel_id=1, source_target_pairs={{0,10},{2,8},{4,14},{6,12},{8,2},{10,0},{12,6},{14,4},{16,26},{18,... | collective-permute-start | bytes 196616 | tf_op jit(solution)/shard_map/ppermute | solution.py:248
  82.6 37.3 %copy-start.3 = (f32[64,256]{1,0:T(8,128)}, f32[64,256]{1,0:T(8,128)S(1)}, u32[]{:S(2)}) copy-start(f32[64,256]{1,0:T(8,128)S(1)} %collective-permute-done.1.rest_1_) | copy-start | bytes 196612
  82.6 13.1 %collective-permute-start.6 = (f32[64,256]{1,0:T(8,128)}, f32[64,256]{1,0:T(8,128)S(1)}, u32[]{:S(2)}, u32[]{:S(2)}) collective-permute-start(f32[64,256]{1,0:T(8,128)} %get-tuple-element.27), channel_id=1, source_target_pairs={{0,12},{2,14},{4,8},{6,10},{8,4},{10,6},{12,0},{14,2},{16,28},{18,... | collective-permute-start | bytes 196616 | tf_op jit(solution)/shard_map/ppermute | solution.py:248
  85.1 34.9 %copy-start.4 = (f32[64,256]{1,0:T(8,128)}, f32[64,256]{1,0:T(8,128)S(1)}, u32[]{:S(2)}) copy-start(f32[64,256]{1,0:T(8,128)S(1)} %collective-permute-done.2.rest_2_) | copy-start | bytes 196612
  85.1 12.9 %collective-permute-start.7 = (f32[64,256]{1,0:T(8,128)}, f32[64,256]{1,0:T(8,128)S(1)}, u32[]{:S(2)}, u32[]{:S(2)}) collective-permute-start(f32[64,256]{1,0:T(8,128)} %get-tuple-element.28), channel_id=1, source_target_pairs={{0,14},{2,12},{4,10},{6,8},{8,6},{10,4},{12,2},{14,0},{16,30},{18,... | collective-permute-start | bytes 196616 | tf_op jit(solution)/shard_map/ppermute | solution.py:248
  87.9 32.1 %copy-start.5 = (f32[64,256]{1,0:T(8,128)}, f32[64,256]{1,0:T(8,128)S(1)}, u32[]{:S(2)}) copy-start(f32[64,256]{1,0:T(8,128)S(1)} %collective-permute-done.3.rest_3_) | copy-start | bytes 196612
  87.9 12.1 %collective-permute-start.8 = (f32[64,256]{1,0:T(8,128)}, f32[64,256]{1,0:T(8,128)S(1)}, u32[]{:S(2)}, u32[]{:S(2)}) collective-permute-start(f32[64,256]{1,0:T(8,128)} %get-tuple-element.29), channel_id=1, source_target_pairs={{0,16},{2,18},{4,20},{6,22},{8,24},{10,26},{12,28},{14,30},{16,0},... | collective-permute-start | bytes 196616 | tf_op jit(solution)/shard_map/ppermute | solution.py:248
  91.5 28.4 %copy-start.6 = (f32[64,256]{1,0:T(8,128)}, f32[64,256]{1,0:T(8,128)S(1)}, u32[]{:S(2)}) copy-start(f32[64,256]{1,0:T(8,128)S(1)} %collective-permute-done.4.rest_4_) | copy-start | bytes 196612
  91.5 13.9 %collective-permute-start.9 = (f32[64,256]{1,0:T(8,128)}, f32[64,256]{1,0:T(8,128)S(1)}, u32[]{:S(2)}, u32[]{:S(2)}) collective-permute-start(f32[64,256]{1,0:T(8,128)} %get-tuple-element.30), channel_id=1, source_target_pairs={{0,18},{2,16},{4,22},{6,20},{8,26},{10,24},{12,30},{14,28},{16,2},... | collective-permute-start | bytes 196616 | tf_op jit(solution)/shard_map/ppermute | solution.py:248
  93.7 26.3 %copy-start.7 = (f32[64,256]{1,0:T(8,128)}, f32[64,256]{1,0:T(8,128)S(1)}, u32[]{:S(2)}) copy-start(f32[64,256]{1,0:T(8,128)S(1)} %collective-permute-done.5.rest_5_) | copy-start | bytes 196612
  93.7 12.9 %collective-permute-start.10 = (f32[64,256]{1,0:T(8,128)}, f32[64,256]{1,0:T(8,128)S(1)}, u32[]{:S(2)}, u32[]{:S(2)}) collective-permute-start(f32[64,256]{1,0:T(8,128)} %get-tuple-element.31), channel_id=1, source_target_pairs={{0,20},{2,22},{4,16},{6,18},{8,28},{10,30},{12,24},{14,26},{16,4},... | collective-permute-start | bytes 196616 | tf_op jit(solution)/shard_map/ppermute | solution.py:248
  95.7 24.2 %copy-start.8 = (f32[64,256]{1,0:T(8,128)}, f32[64,256]{1,0:T(8,128)S(1)}, u32[]{:S(2)}) copy-start(f32[64,256]{1,0:T(8,128)S(1)} %collective-permute-done.6.rest_6_) | copy-start | bytes 196612
  95.7 17.2 %collective-permute-start.11 = (f32[64,256]{1,0:T(8,128)}, f32[64,256]{1,0:T(8,128)S(1)}, u32[]{:S(2)}, u32[]{:S(2)}) collective-permute-start(f32[64,256]{1,0:T(8,128)} %get-tuple-element.32), channel_id=1, source_target_pairs={{0,22},{2,20},{4,18},{6,16},{8,30},{10,28},{12,26},{14,24},{16,6},... | collective-permute-start | bytes 196616 | tf_op jit(solution)/shard_map/ppermute | solution.py:248
  97.9 22.0 %copy-start.9 = (f32[64,256]{1,0:T(8,128)}, f32[64,256]{1,0:T(8,128)S(1)}, u32[]{:S(2)}) copy-start(f32[64,256]{1,0:T(8,128)S(1)} %collective-permute-done.7.rest_7_) | copy-start | bytes 196612
  97.9 15.0 %collective-permute-start.12 = (f32[64,256]{1,0:T(8,128)}, f32[64,256]{1,0:T(8,128)S(1)}, u32[]{:S(2)}, u32[]{:S(2)}) collective-permute-start(f32[64,256]{1,0:T(8,128)} %get-tuple-element.33), channel_id=1, source_target_pairs={{0,24},{2,26},{4,28},{6,30},{8,16},{10,18},{12,20},{14,22},{16,8},... | collective-permute-start | bytes 196616 | tf_op jit(solution)/shard_map/ppermute | solution.py:248
  100.0 20.0 %copy-start.10 = (f32[64,256]{1,0:T(8,128)}, f32[64,256]{1,0:T(8,128)S(1)}, u32[]{:S(2)}) copy-start(f32[64,256]{1,0:T(8,128)S(1)} %collective-permute-done.8.rest_8_) | copy-start | bytes 196612
  100.0 16.7 %collective-permute-start.13 = (f32[64,256]{1,0:T(8,128)}, f32[64,256]{1,0:T(8,128)S(1)}, u32[]{:S(2)}, u32[]{:S(2)}) collective-permute-start(f32[64,256]{1,0:T(8,128)} %get-tuple-element.34), channel_id=1, source_target_pairs={{0,26},{2,24},{4,30},{6,28},{8,18},{10,16},{12,22},{14,20},{16,10}... | collective-permute-start | bytes 196616 | tf_op jit(solution)/shard_map/ppermute | solution.py:248
  105.4 14.6 %copy-start.11 = (f32[64,256]{1,0:T(8,128)}, f32[64,256]{1,0:T(8,128)S(1)}, u32[]{:S(2)}) copy-start(f32[64,256]{1,0:T(8,128)S(1)} %collective-permute-done.9.rest_9_) | copy-start | bytes 196612
  105.4 13.0 %collective-permute-start.14 = (f32[64,256]{1,0:T(8,128)}, f32[64,256]{1,0:T(8,128)S(1)}, u32[]{:S(2)}, u32[]{:S(2)}) collective-permute-start(f32[64,256]{1,0:T(8,128)} %get-tuple-element.35), channel_id=1, source_target_pairs={{0,28},{2,30},{4,24},{6,26},{8,20},{10,22},{12,16},{14,18},{16,12}... | collective-permute-start | bytes 196616 | tf_op jit(solution)/shard_map/ppermute | solution.py:248
  106.6 13.4 %copy-start.12 = (f32[64,256]{1,0:T(8,128)}, f32[64,256]{1,0:T(8,128)S(1)}, u32[]{:S(2)}) copy-start(f32[64,256]{1,0:T(8,128)S(1)} %collective-permute-done.10.rest_10_) | copy-start | bytes 196612
  106.6 13.3 %collective-permute-start.15 = (f32[64,256]{1,0:T(8,128)}, f32[64,256]{1,0:T(8,128)S(1)}, u32[]{:S(2)}, u32[]{:S(2)}) collective-permute-start(f32[64,256]{1,0:T(8,128)} %get-tuple-element.36), channel_id=1, source_target_pairs={{0,30},{2,28},{4,26},{6,24},{8,22},{10,20},{12,18},{14,16},{16,14}... | collective-permute-start | bytes 196616 | tf_op jit(solution)/shard_map/ppermute | solution.py:248
  113.0 7.0 %copy-start.13 = (f32[64,256]{1,0:T(8,128)}, f32[64,256]{1,0:T(8,128)S(1)}, u32[]{:S(2)}) copy-start(f32[64,256]{1,0:T(8,128)S(1)} %collective-permute-done.11.rest_11_) | copy-start | bytes 196612
  113.0 7.0 %copy-start.14 = (f32[64,256]{1,0:T(8,128)}, f32[64,256]{1,0:T(8,128)S(1)}, u32[]{:S(2)}) copy-start(f32[64,256]{1,0:T(8,128)S(1)} %collective-permute-done.12.rest_12_) | copy-start | bytes 196612
  (6 other events, 12.3 us)

commit v3 on v2

--- a/solution.py
+++ b/solution.py
@@ -64,23 +64,31 @@
     )(signal, filters)
 
 
-def turn_kernel(sig_ref, out_ref):
-    out_ref[...] = turned(sig_ref)
-
-
-def turn(signal, start, cols):
-    rows = signal.shape[0]
-    step = math.gcd(start, cols)
-    return pl.pallas_call(
-        turn_kernel,
-        grid=(cols // step,),
-        in_specs=[pl.BlockSpec((rows, step), lambda i: (0, start // step + i))],
-        out_specs=pl.BlockSpec((step, rows), lambda i: (i, 0)),
-        out_shape=jax.ShapeDtypeStruct((cols, rows), jnp.float32),
+def turn_apart_kernel(place_ref, sig_ref, *rest):
+    outs, hold_ref = rest[:-1], rest[-1]
+    hold_ref[...] = turned(sig_ref).reshape(hold_ref.shape)
+    for j, out_ref in enumerate(outs):
+        out_ref[...] = hold_ref[place_ref[0] ^ j]
+
+
+def turn_apart(place, signal, blocks):
+    rows, width = signal.shape
+    cols = width // 2
+    shape = (cols // blocks, rows)
+    return pl.pallas_call(
+        turn_apart_kernel,
+        grid=(1,),
+        in_specs=[
+            pl.BlockSpec(memory_space=pltpu.SMEM),
+            pl.BlockSpec((rows, cols), lambda i: (0, 1)),
+        ],
+        out_specs=[pl.BlockSpec(shape, lambda i: (0, 0))] * blocks,
+        out_shape=[jax.ShapeDtypeStruct(shape, jnp.float32)] * blocks,
+        scratch_shapes=[pltpu.VMEM((blocks, *shape), jnp.float32)],
         compiler_params=pltpu.CompilerParams(vmem_limit_bytes=VMEM_BYTES),
         cost_estimate=pl.CostEstimate(flops=0, bytes_accessed=8 * rows * cols, transcendentals=0),
-        name="turn",
-    )(signal)
+        name="turn_apart",
+    )(place, signal)
 
 
 def home_kernel(back_ref, sig_ref, gain_ref, *rest):
@@ -163,53 +171,89 @@
 
 
 def conv_kernel(first, place_ref, own_ref, other_ref, sig_ref, *rest):
-    outs, scratch = rest[: -3 * PAIR], rest[-3 * PAIR :]
+    out_ref, scratch = rest[0], rest[-3 * PAIR :]
     blocks, _, rows = sig_ref.shape
+    for u in range(PAIR):
+        group = first + PAIR * pl.program_id(0) + u
+        shifted_taps(place_ref[1], group, own_ref, other_ref, scratch[3 * u], scratch[3 * u + 1])
+    for u in range(PAIR):
+        high_ref, low_ref, sum_ref = scratch[3 * u : 3 * u + 3]
+        at = slice(u * GROUP, (u + 1) * GROUP)
+        causal_sums(sig_ref[:, at, :].reshape(blocks * GROUP, rows), high_ref, low_ref, sum_ref)
+        out_ref[:, at, :] = sum_ref[...].reshape(blocks, GROUP, rows)
+
+
+def conv_apart_kernel(first, blocks, place_ref, own_ref, other_ref, *rest):
+    sigs, outs, hold_ref = rest[:blocks], rest[blocks : 2 * blocks], rest[2 * blocks]
+    scratch = rest[2 * blocks + 1 :]
+    rows = hold_ref.shape[2]
     me, side = place_ref[0], place_ref[1]
+    for j, sig_ref in enumerate(sigs):
+        hold_ref[me ^ j] = sig_ref[...]
     for u in range(PAIR):
         group = first + PAIR * pl.program_id(0) + u
         shifted_taps(side, group, own_ref, other_ref, scratch[3 * u], scratch[3 * u + 1])
     for u in range(PAIR):
         high_ref, low_ref, sum_ref = scratch[3 * u : 3 * u + 3]
         at = slice(u * GROUP, (u + 1) * GROUP)
-        causal_sums(sig_ref[:, at, :].reshape(blocks * GROUP, rows), high_ref, low_ref, sum_ref)
-        if len(outs) == 1:
-            outs[0][:, at, :] = sum_ref[...].reshape(blocks, GROUP, rows)
-            continue
+        causal_sums(hold_ref[:, at, :].reshape(blocks * GROUP, rows), high_ref, low_ref, sum_ref)
         for j in range(blocks):
             row = pl.multiple_of((me ^ j) * GROUP, GROUP)
             outs[j][at, :] = sum_ref[pl.ds(row, GROUP), :]
 
 
-def convolve(place, own, other, arrived, first, groups, apart):
+def conv_scratch(blocks, rows):
+    lanes = blocks * rows + 2 * HALF
+    return [
+        pltpu.VMEM((HALF, lanes), jnp.bfloat16),
+        pltpu.VMEM((HALF, lanes), jnp.bfloat16),
+        pltpu.VMEM((blocks * GROUP, rows), jnp.float32),
+    ] * PAIR
+
+
+def conv_cost(blocks, groups, rows):
+    return pl.CostEstimate(
+        flops=3 * groups * GROUP * rows * rows * blocks * (blocks + 1),
+        bytes_accessed=8 * blocks * groups * GROUP * rows,
+        transcendentals=0,
+    )
+
+
+def convolve(place, own, other, arrived, first, groups):
     blocks, _, rows = arrived.shape
     spec = pl.BlockSpec((blocks, PAIR * GROUP, rows), lambda g: (0, g, 0))
     taps_spec = pl.BlockSpec(own.shape, lambda g: (0, 0, 0))
-    out_specs, shapes = [spec], [(blocks, groups * GROUP, rows)]
-    if apart:
-        out_specs = [pl.BlockSpec((PAIR * GROUP, rows), lambda g: (g, 0))] * blocks
-        shapes = [(groups * GROUP, rows)] * blocks
-    lanes = blocks * rows + 2 * HALF
-    scratch = [
-        pltpu.VMEM((HALF, lanes), jnp.bfloat16),
-        pltpu.VMEM((HALF, lanes), jnp.bfloat16),
-        pltpu.VMEM((blocks * GROUP, rows), jnp.float32),
-    ]
     return pl.pallas_call(
         functools.partial(conv_kernel, first),
         grid=(groups // PAIR,),
         in_specs=[pl.BlockSpec(memory_space=pltpu.SMEM), taps_spec, taps_spec, spec],
-        out_specs=out_specs,
-        out_shape=[jax.ShapeDtypeStruct(shape, jnp.float32) for shape in shapes],
-        scratch_shapes=scratch * PAIR,
-        compiler_params=pltpu.CompilerParams(vmem_limit_bytes=VMEM_BYTES),
-        cost_estimate=pl.CostEstimate(
-            flops=3 * groups * GROUP * rows * rows * blocks * (blocks + 1),
-            bytes_accessed=8 * blocks * groups * GROUP * rows,
-            transcendentals=0,
-        ),
+        out_specs=spec,
+        out_shape=jax.ShapeDtypeStruct((blocks, groups * GROUP, rows), jnp.float32),
+        scratch_shapes=conv_scratch(blocks, rows),
+        compiler_params=pltpu.CompilerParams(vmem_limit_bytes=VMEM_BYTES),
+        cost_estimate=conv_cost(blocks, groups, rows),
         name="convolve",
     )(place, own, other, arrived)
+
+
+def convolve_apart(place, own, other, parts, first):
+    blocks = len(parts)
+    deep, rows = parts[0].shape
+    groups = deep // GROUP
+    taps_spec = pl.BlockSpec(own.shape, lambda g: (0, 0, 0))
+    pieces = [pl.BlockSpec((PAIR * GROUP, rows), lambda g: (g, 0))] * blocks
+    return pl.pallas_call(
+        functools.partial(conv_apart_kernel, first, blocks),
+        grid=(groups // PAIR,),
+        in_specs=[pl.BlockSpec(memory_space=pltpu.SMEM), taps_spec, taps_spec] + pieces,
+        out_specs=pieces,
+        out_shape=[jax.ShapeDtypeStruct((deep, rows), jnp.float32)] * blocks,
+        scratch_shapes=[pltpu.VMEM((blocks, PAIR * GROUP, rows), jnp.float32)]
+        + conv_scratch(blocks, rows),
+        compiler_params=pltpu.CompilerParams(vmem_limit_bytes=VMEM_BYTES),
+        cost_estimate=conv_cost(blocks, groups, rows),
+        name="convolve_apart",
+    )(place, own, other, *parts)
 
 
 def home_apart_kernel(place_ref, *rest):
@@ -256,23 +300,27 @@
     return lax.optimization_barrier((value, *others))[0]
 
 
+def scatter(parts):
+    return [exchange(part, "seq", j) if j else part for j, part in enumerate(parts)]
+
+
 def fast_body(signal, filters, skip_gain):
     blocks = lax.axis_size("seq")
     rows, width = signal.shape
     count = width // blocks // GROUP // 2
-    cols = width // 2
     side = lax.axis_index("ch")
     place = jnp.stack([lax.axis_index("seq"), side]).astype(jnp.int32)
     gain = skip_gain.reshape(1, width)
     first = spread(turn_taps(signal, filters, blocks, (count, count)))
-    second = spread(turn(signal, cols, cols).reshape(blocks, -1, rows))
+    parts = scatter(turn_apart(place, signal, blocks))
+    first = after(first, *parts[1:8])
     taps = first[:, count * GROUP :, :]
     own = lax.dynamic_slice_in_dim(taps, side * HALF, HALF, axis=2)
     other = exchange(lax.dynamic_slice_in_dim(taps, (1 - side) * HALF, HALF, axis=2), "ch", 1)
-    (values,) = convolve(place, own, other, first, 0, count, False)
+    values = convolve(place, own, other, first, 0, count)
+    values = after(values, *parts[8:])
     back = spread(values).reshape(-1, rows)
-    parts = convolve(place, own, other, second, count, count, True)
-    parts = [exchange(part, "seq", j) if j else part for j, part in enumerate(parts)]
+    parts = scatter(convolve_apart(place, own, other, parts, count))
     out = home(back, signal, gain, 0, None)
     return home_apart(place, parts, signal, gain, out)
 

time: 124 us -> 118 us (0.952)
  waiting for transfers between devices: 51.9 us -> 25.5 us
  starting transfers between devices: 43.1 us -> 63 us
    all_to_all x3 -> x2, waiting for transfers between devices: 38.3 us -> 0.01 us  [spread(): lax.all_to_all(values, 'seq', split_axis=0, concat_axis=0, tiled=True)]
    ppermute x16 -> x31, starting transfers between devices: 26.5 us -> 51.7 us  [exchange(): return lax.ppermute(values, axis, [(i, i ^ step) for i in range(size)])]
    ppermute x16 -> x31, waiting for transfers between devices: 13.6 us -> 25.5 us  [exchange(): return lax.ppermute(values, axis, [(i, i ^ step) for i in range(size)])]
    pallas_call x1 -> x2, Pallas kernels: 2.54 us -> 9.85 us  [the longest x1 7.29 us: convolve_apart(): pl.pallas_call(functools.partial(conv_apart_kernel, first, blocks), grid=...]
    pallas_call x2 -> x1, Pallas kernels: 14 us -> 6.93 us  [convolve(): pl.pallas_call(functools.partial(conv_kernel, first), grid=(groups // PAI...]
    all_to_all x3 -> x2, starting transfers between devices: 16.6 us -> 11.3 us  [spread(): lax.all_to_all(values, 'seq', split_axis=0, concat_axis=0, tiled=True)]
  transfers between devices with their start and end apart: 19 -> 33, of which waited for: 11 -> 14; matrix products, arithmetic and copies ran while one was open for 1% -> 1% of each run, Pallas kernels for 16% -> 17%
where the time goes in v3:
time: 118 us; the launch traced here: 117 us
  starting transfers between devices  63 us (53%)
  waiting for transfers between devices  25.5 us (22%)
  Pallas kernels  25.3 us (21%)
  local copies, waits for them, and re-layouts  2.4 us (2%)
    ppermute x31, starting transfers between devices, exchange(): return lax.ppermute(values, axis, [(i, i ^ step) for i in range(size)])  51.7 us
    ppermute x31, waiting for transfers between devices, exchange(): return lax.ppermute(values, axis, [(i, i ^ step) for i in range(size)])  25.5 us
    all_to_all x2, starting transfers between devices, spread(): lax.all_to_all(values, 'seq', split_axis=0, concat_axis=0, tiled=True)  11.3 us
    pallas_call x1, Pallas kernels, convolve_apart(): pl.pallas_call(functools.partial(conv_apart_kernel, first, blocks), grid=...  7.29 us
    pallas_call x1, Pallas kernels, convolve(): pl.pallas_call(functools.partial(conv_kernel, first), grid=(groups // PAI...  6.93 us
    pallas_call x1, Pallas kernels, home_apart(): pl.pallas_call(home_apart_kernel, grid=(1,), in_specs=[pl.BlockSpec(memor...  3.06 us
    pallas_call x1, Pallas kernels, home(): pl.pallas_call(home_kernel, grid=(cols // step,), in_specs=in_specs, out_...  2.85 us
    pallas_call x1, Pallas kernels, turn_taps(): pl.pallas_call(functools.partial(turn_taps_kernel, counts), grid=(1,), in...  2.61 us
  transfers between devices with their start and end apart: 33, of which 14 were waited for; matrix products, arithmetic and copies ran while one was open for 1% of the time, Pallas kernels for 17%

profile of v3, /device:TPU:9, one launch (start us, length us, event | category | flops | bytes accessed | tf_op | source)
XLA Modules:
  0.0 117.1 jit_solution(8815529105324188229)
XLA Ops:
  0.0 2.6 %turn_taps.1 = f32[16,72,256]{2,1,0:T(8,128)} custom-call(f32[256,2048]{1,0:T(8,128)} %rest_16_.1, f32[128,256]{1,0:T(8,128)} %taps_ref.1), custom_call_target="tpu_custom_call" | custom-call | bytes 2097152 | tf_op jit(solution)/shard_map/turn_taps/pallas_call | solution.py:52
  2.6 6.6 %all-to-all-start = ((f32[16,72,256]{2,1,0:T(8,128)}), f32[16,72,256]{2,1,0:T(8,128)S(1)}, u32[]{:S(2)}, u32[]{:S(2)}) async-start(f32[16,72,256]{2,1,0:T(8,128)} %turn_taps.1), calls=%async_computation | async-start | bytes 2359296 | tf_op jit(solution)/shard_map/all_to_all | solution.py:296
  9.8 2.6 %turn_apart.1 = (f32[64,256]{1,0:T(8,128)}, f32[64,256]{1,0:T(8,128)}, f32[64,256]{1,0:T(8,128)}, f32[64,256]{1,0:T(8,128)}, f32[64,256]{1,0:T(8,128)}, /*index=...) custom-call(s32[2]{0:T(128)} %pad_add_fusion.place_ref, ...), custom_call_target="tpu_custom_call" | custom-call | bytes 2097152 | tf_op jit(solution)/shard_map/turn_apart/pallas_call | solution.py:78
  14.6 1.6 %collective-permute-start.4 = (f32[64,256]{1,0:T(8,128)}, f32[64,256]{1,0:T(8,128)S(1)}, u32[]{:S(2)}, u32[]{:S(2)}) collective-permute-start(f32[64,256]{1,0:T(8,128)} %get-tuple-element.43), channel_id=1, source_target_pairs={{0,10},{2,8},{4,14},{6,12},{8,2},{10,0},{12,6},{14,4},{16,26},{18,... | collective-permute-start | bytes 196616 | tf_op jit(solution)/shard_map/ppermute | solution.py:292
  18.1 3.5 %collective-permute-start.6 = (f32[64,256]{1,0:T(8,128)}, f32[64,256]{1,0:T(8,128)S(1)}, u32[]{:S(2)}, u32[]{:S(2)}) collective-permute-start(f32[64,256]{1,0:T(8,128)} %get-tuple-element.45), channel_id=1, source_target_pairs={{0,14},{2,12},{4,10},{6,8},{8,6},{10,4},{12,2},{14,0},{16,30},{18,... | collective-permute-start | bytes 196616 | tf_op jit(solution)/shard_map/ppermute | solution.py:292
  21.6 3.2 %collective-permute-start.8 = (f32[64,256]{1,0:T(8,128)}, f32[64,256]{1,0:T(8,128)S(1)}, u32[]{:S(2)}, u32[]{:S(2)}) collective-permute-start(f32[64,256]{1,0:T(8,128)} %get-tuple-element.48), channel_id=1, source_target_pairs={{0,16},{2,18},{4,20},{6,22},{8,24},{10,26},{12,28},{14,30},{16,0},... | collective-permute-start | bytes 196616 | tf_op jit(solution)/shard_map/ppermute | solution.py:292
  24.8 6.4 %collective-permute-done.3.rest_4_ = f32[64,256]{1,0:T(8,128)S(1)} collective-permute-done((f32[64,256]{1,0:T(8,128)}, f32[64,256]{1,0:T(8,128)S(1)}, u32[]{:S(2)}, u32[]{:S(2)}) %collective-permute-start.3) | collective-permute-done | bytes 65568 | tf_op jit(solution)/shard_map/ppermute | solution.py:292
  31.2 2.2 %collective-permute-start.9 = (f32[64,256]{1,0:T(8,128)}, f32[64,256]{1,0:T(8,128)S(1)}, u32[]{:S(2)}, u32[]{:S(2)}) collective-permute-start(f32[64,256]{1,0:T(8,128)} %get-tuple-element.49), channel_id=1, source_target_pairs={{0,18},{2,16},{4,22},{6,20},{8,26},{10,24},{12,30},{14,28},{16,2},... | collective-permute-start | bytes 196616 | tf_op jit(solution)/shard_map/ppermute | solution.py:292
  33.4 2.1 %collective-permute-start.10 = (f32[64,256]{1,0:T(8,128)}, f32[64,256]{1,0:T(8,128)S(1)}, u32[]{:S(2)}, u32[]{:S(2)}) collective-permute-start(f32[64,256]{1,0:T(8,128)} %get-tuple-element.50), channel_id=1, source_target_pairs={{0,20},{2,22},{4,16},{6,18},{8,28},{10,30},{12,24},{14,26},{16,4},... | collective-permute-start | bytes 196616 | tf_op jit(solution)/shard_map/ppermute | solution.py:292
  35.5 2.4 %collective-permute-done.6.rest_7_ = f32[64,256]{1,0:T(8,128)S(1)} collective-permute-done((f32[64,256]{1,0:T(8,128)}, f32[64,256]{1,0:T(8,128)S(1)}, u32[]{:S(2)}, u32[]{:S(2)}) %collective-permute-start.6) | collective-permute-done | bytes 65568 | tf_op jit(solution)/shard_map/ppermute | solution.py:292
  38.6 1.2 %collective-permute-start.7 = (f32[16,8,128]{2,1,0:T(8,128)S(1)}, f32[16,8,128]{2,1,0:T(8,128)S(1)}, u32[]{:S(2)}, u32[]{:S(2)}) collective-permute-start(f32[16,8,128]{2,1,0:T(8,128)S(1)} %get-tuple-element.73), channel_id=1, source_target_pairs={{0,1},{1,0},{2,3},{3,2},{4,5},{5,4},{6,7},{7,6},{8,9},{9,8},{10,11... | collective-permute-start | bytes 196616 | tf_op jit(solution)/shard_map/ppermute | solution.py:292
  39.8 4.3 %collective-permute-start.11 = (f32[64,256]{1,0:T(8,128)}, f32[64,256]{1,0:T(8,128)S(1)}, u32[]{:S(2)}, u32[]{:S(2)}) collective-permute-start(f32[64,256]{1,0:T(8,128)} %get-tuple-element.51), channel_id=1, source_target_pairs={{0,22},{2,20},{4,18},{6,16},{8,30},{10,28},{12,26},{14,24},{16,6},... | collective-permute-start | bytes 196616 | tf_op jit(solution)/shard_map/ppermute | solution.py:292
  44.2 3.5 %collective-permute-start.13 = (f32[64,256]{1,0:T(8,128)}, f32[64,256]{1,0:T(8,128)S(1)}, u32[]{:S(2)}, u32[]{:S(2)}) collective-permute-start(f32[64,256]{1,0:T(8,128)} %get-tuple-element.53), channel_id=1, source_target_pairs={{0,26},{2,24},{4,30},{6,28},{8,18},{10,16},{12,22},{14,20},{16,10}... | collective-permute-start | bytes 196616 | tf_op jit(solution)/shard_map/ppermute | solution.py:292
  48.8 6.9 %convolve.1 = f32[16,64,256]{2,1,0:T(8,128)} custom-call(s32[2]{0:T(128)} %pad_add_fusion.place_ref, f32[16,8,128]{2,1,0:T(8,128)} %get-tuple-element.74.own_ref, f32[16,8,128]{2,1,0:T(8,128)} %copy-done.27, f32[16,72,256]{2,1,0:T(8,128)} %copy-done.1), custom_call_target="tpu_custom_call" | custom-call | flops 3422552064 | bytes 2097152 | tf_op jit(solution)/shard_map/convolve/pallas_call | solution.py:226
  55.9 2.7 %collective-permute-done.13.rest_13_ = f32[64,256]{1,0:T(8,128)S(1)} collective-permute-done((f32[64,256]{1,0:T(8,128)}, f32[64,256]{1,0:T(8,128)S(1)}, u32[]{:S(2)}, u32[]{:S(2)}) %collective-permute-start.13) | collective-permute-done | bytes 65568 | tf_op jit(solution)/shard_map/ppermute | solution.py:292
  58.9 1.6 %collective-permute-done.15.rest_15_ = f32[64,256]{1,0:T(8,128)S(1)} collective-permute-done((f32[64,256]{1,0:T(8,128)}, f32[64,256]{1,0:T(8,128)S(1)}, u32[]{:S(2)}, u32[]{:S(2)}) %collective-permute-start.15) | collective-permute-done | bytes 65568 | tf_op jit(solution)/shard_map/ppermute | solution.py:292
  60.5 4.7 %all-to-all-start.1 = ((f32[16,64,256]{2,1,0:T(8,128)}), f32[16,64,256]{2,1,0:T(8,128)S(1)}, u32[]{:S(2)}, u32[]{:S(2)}) async-start(f32[16,64,256]{2,1,0:T(8,128)} %convolve.1), calls=%async_computation.1 | async-start | bytes 2097152 | tf_op jit(solution)/shard_map/all_to_all | solution.py:296
  65.2 7.3 %convolve_apart.1 = (f32[64,256]{1,0:T(8,128)}, f32[64,256]{1,0:T(8,128)}, f32[64,256]{1,0:T(8,128)}, f32[64,256]{1,0:T(8,128)}, f32[64,256]{1,0:T(8,128)}, /*in...) custom-call(s32[2]{0:T(128)} %pad_add_fusion.place_ref, ...), custom_call_target="tpu_custom_call" | custom-call | flops 3422552064 | bytes 2097152 | tf_op jit(solution)/shard_map/convolve_apart/pallas_call | solution.py:245
  74.8 1.6 %collective-permute-start.20 = (f32[64,256]{1,0:T(8,128)}, f32[64,256]{1,0:T(8,128)S(1)}, u32[]{:S(2)}, u32[]{:S(2)}) collective-permute-start(f32[64,256]{1,0:T(8,128)} %get-tuple-element.61), channel_id=1, source_target_pairs={{0,10},{2,8},{4,14},{6,12},{8,2},{10,0},{12,6},{14,4},{16,26},{18,... | collective-permute-start | bytes 196616 | tf_op jit(solution)/shard_map/ppermute | solution.py:292
  78.6 2.2 %collective-permute-start.22 = (f32[64,256]{1,0:T(8,128)}, f32[64,256]{1,0:T(8,128)S(1)}, u32[]{:S(2)}, u32[]{:S(2)}) collective-permute-start(f32[64,256]{1,0:T(8,128)} %get-tuple-element.63), channel_id=1, source_target_pairs={{0,14},{2,12},{4,10},{6,8},{8,6},{10,4},{12,2},{14,0},{16,30},{18,... | collective-permute-start | bytes 196616 | tf_op jit(solution)/shard_map/ppermute | solution.py:292
  82.5 2.5 %collective-permute-done.19.rest_4_ = f32[64,256]{1,0:T(8,128)S(1)} collective-permute-done((f32[64,256]{1,0:T(8,128)}, f32[64,256]{1,0:T(8,128)S(1)}, u32[]{:S(2)}, u32[]{:S(2)}) %collective-permute-start.19) | collective-permute-done | bytes 65568 | tf_op jit(solution)/shard_map/ppermute | solution.py:292
  85.0 2.2 %collective-permute-start.24 = (f32[64,256]{1,0:T(8,128)}, f32[64,256]{1,0:T(8,128)S(1)}, u32[]{:S(2)}, u32[]{:S(2)}) collective-permute-start(f32[64,256]{1,0:T(8,128)} %get-tuple-element.65), channel_id=1, source_target_pairs={{0,18},{2,16},{4,22},{6,20},{8,26},{10,24},{12,30},{14,28},{16,2},... | collective-permute-start | bytes 196616 | tf_op jit(solution)/shard_map/ppermute | solution.py:292
  87.2 2.0 %collective-permute-start.25 = (f32[64,256]{1,0:T(8,128)}, f32[64,256]{1,0:T(8,128)S(1)}, u32[]{:S(2)}, u32[]{:S(2)}) collective-permute-start(f32[64,256]{1,0:T(8,128)} %get-tuple-element.66), channel_id=1, source_target_pairs={{0,20},{2,22},{4,16},{6,18},{8,28},{10,30},{12,24},{14,26},{16,4},... | collective-permute-start | bytes 196616 | tf_op jit(solution)/shard_map/ppermute | solution.py:292
  89.2 1.8 %collective-permute-start.26 = (f32[64,256]{1,0:T(8,128)}, f32[64,256]{1,0:T(8,128)S(1)}, u32[]{:S(2)}, u32[]{:S(2)}) collective-permute-start(f32[64,256]{1,0:T(8,128)} %get-tuple-element.67), channel_id=1, source_target_pairs={{0,22},{2,20},{4,18},{6,16},{8,30},{10,28},{12,26},{14,24},{16,6},... | collective-permute-start | bytes 196616 | tf_op jit(solution)/shard_map/ppermute | solution.py:292
  91.4 2.0 %collective-permute-start.27 = (f32[64,256]{1,0:T(8,128)}, f32[64,256]{1,0:T(8,128)S(1)}, u32[]{:S(2)}, u32[]{:S(2)}) collective-permute-start(f32[64,256]{1,0:T(8,128)} %get-tuple-element.68), channel_id=1, source_target_pairs={{0,24},{2,26},{4,28},{6,30},{8,16},{10,18},{12,20},{14,22},{16,8},... | collective-permute-start | bytes 196616 | tf_op jit(solution)/shard_map/ppermute | solution.py:292
  93.5 5.4 %collective-permute-start.28 = (f32[64,256]{1,0:T(8,128)}, f32[64,256]{1,0:T(8,128)S(1)}, u32[]{:S(2)}, u32[]{:S(2)}) collective-permute-start(f32[64,256]{1,0:T(8,128)} %get-tuple-element.69), channel_id=1, source_target_pairs={{0,26},{2,24},{4,30},{6,28},{8,18},{10,16},{12,22},{14,20},{16,10}... | collective-permute-start | bytes 196616 | tf_op jit(solution)/shard_map/ppermute | solution.py:292
  100.1 2.5 %collective-permute-start.30 = (f32[64,256]{1,0:T(8,128)}, f32[64,256]{1,0:T(8,128)S(1)}, u32[]{:S(2)}, u32[]{:S(2)}) collective-permute-start(f32[64,256]{1,0:T(8,128)} %get-tuple-element.71), channel_id=1, source_target_pairs={{0,30},{2,28},{4,26},{6,24},{8,22},{10,20},{12,18},{14,16},{16,14}... | collective-permute-start | bytes 196616 | tf_op jit(solution)/shard_map/ppermute | solution.py:292
  103.7 2.9 %home.1.rest_18_ = f32[256,2048]{1,0:T(8,128)} custom-call(f32[1024,256]{1,0:T(8,128)} %bitcast.4, f32[256,2048]{1,0:T(8,128)} %rest_16_.1, f32[1,2048]{1,0:T(1,128)} %bitcast.5), custom_call_target="tpu_custom_call" | custom-call | bytes 3145728 | tf_op jit(solution)/shard_map/home/pallas_call | solution.py:114
  106.5 3.6 %collective-permute-done.28.rest_13_ = f32[64,256]{1,0:T(8,128)S(1)} collective-permute-done((f32[64,256]{1,0:T(8,128)}, f32[64,256]{1,0:T(8,128)S(1)}, u32[]{:S(2)}, u32[]{:S(2)}) %collective-permute-start.28) | collective-permute-done | bytes 65568 | tf_op jit(solution)/shard_map/ppermute | solution.py:292
  110.2 1.7 %collective-permute-done.29.rest_14_ = f32[64,256]{1,0:T(8,128)S(1)} collective-permute-done((f32[64,256]{1,0:T(8,128)}, f32[64,256]{1,0:T(8,128)S(1)}, u32[]{:S(2)}, u32[]{:S(2)}) %collective-permute-start.29) | collective-permute-done | bytes 65568 | tf_op jit(solution)/shard_map/ppermute | solution.py:292
  111.8 1.6 %collective-permute-done.30.rest_15_ = f32[64,256]{1,0:T(8,128)S(1)} collective-permute-done((f32[64,256]{1,0:T(8,128)}, f32[64,256]{1,0:T(8,128)S(1)}, u32[]{:S(2)}, u32[]{:S(2)}) %collective-permute-start.30) | collective-permute-done | bytes 65568 | tf_op jit(solution)/shard_map/ppermute | solution.py:292
  114.1 3.1 %home_apart.1 = f32[256,2048]{1,0:T(8,128)} custom-call(s32[2]{0:T(128)} %pad_add_fusion.place_ref, f32[64,256]{1,0:T(8,128)} %get-tuple-element.56.rest_0_, f32[64,256]{1,0:T(8,128)} %copy-done.2, f32[64,256]{1,0:T(8,128)} %copy-done.3, f32[64,256]{1,0:T(8,128)} %copy-done.4, f32[64,256]{1,0:T(8,128)} %copy-done.5, ...), custom_call_target="tpu_custom_call", output_to_operand_aliasing={{}: (19, {})} | custom-call | bytes 3145728 | tf_op jit(solution)/shard_map/home_apart/pallas_call | solution.py:273
  (109 shorter events, 16.3 us)
Async XLA Ops:
  2.6 35.3 %all-to-all-start = ((f32[16,72,256]{2,1,0:T(8,128)}), f32[16,72,256]{2,1,0:T(8,128)S(1)}, u32[]{:S(2)}, u32[]{:S(2)}) async-start(f32[16,72,256]{2,1,0:T(8,128)} %turn_taps.1), calls=%async_computation | async-start | bytes 2359296 | tf_op jit(solution)/shard_map/all_to_all | solution.py:296
  12.8 5.3 %collective-permute-start.1 = (f32[64,256]{1,0:T(8,128)}, f32[64,256]{1,0:T(8,128)S(1)}, u32[]{:S(2)}, u32[]{:S(2)}) collective-permute-start(f32[64,256]{1,0:T(8,128)} %get-tuple-element.40), channel_id=1, source_target_pairs={{0,4},{2,6},{4,0},{6,2},{8,12},{10,14},{12,8},{14,10},{16,20},{18,... | collective-permute-start | bytes 196616 | tf_op jit(solution)/shard_map/ppermute | solution.py:292
  14.0 7.6 %collective-permute-start.2 = (f32[64,256]{1,0:T(8,128)}, f32[64,256]{1,0:T(8,128)S(1)}, u32[]{:S(2)}, u32[]{:S(2)}) collective-permute-start(f32[64,256]{1,0:T(8,128)} %get-tuple-element.41), channel_id=1, source_target_pairs={{0,6},{2,4},{4,2},{6,0},{8,14},{10,12},{12,10},{14,8},{16,22},{18,... | collective-permute-start | bytes 196616 | tf_op jit(solution)/shard_map/ppermute | solution.py:292
  14.6 16.6 %collective-permute-start.3 = (f32[64,256]{1,0:T(8,128)}, f32[64,256]{1,0:T(8,128)S(1)}, u32[]{:S(2)}, u32[]{:S(2)}) collective-permute-start(f32[64,256]{1,0:T(8,128)} %get-tuple-element.42), channel_id=1, source_target_pairs={{0,8},{2,10},{4,12},{6,14},{8,0},{10,2},{12,4},{14,6},{16,24},{18,... | collective-permute-start | bytes 196616 | tf_op jit(solution)/shard_map/ppermute | solution.py:292
  14.6 18.7 %collective-permute-start.4 = (f32[64,256]{1,0:T(8,128)}, f32[64,256]{1,0:T(8,128)S(1)}, u32[]{:S(2)}, u32[]{:S(2)}) collective-permute-start(f32[64,256]{1,0:T(8,128)} %get-tuple-element.43), channel_id=1, source_target_pairs={{0,10},{2,8},{4,14},{6,12},{8,2},{10,0},{12,6},{14,4},{16,26},{18,... | collective-permute-start | bytes 196616 | tf_op jit(solution)/shard_map/ppermute | solution.py:292
  16.3 19.2 %collective-permute-start.5 = (f32[64,256]{1,0:T(8,128)}, f32[64,256]{1,0:T(8,128)S(1)}, u32[]{:S(2)}, u32[]{:S(2)}) collective-permute-start(f32[64,256]{1,0:T(8,128)} %get-tuple-element.44), channel_id=1, source_target_pairs={{0,12},{2,14},{4,8},{6,10},{8,4},{10,6},{12,0},{14,2},{16,28},{18,... | collective-permute-start | bytes 196616 | tf_op jit(solution)/shard_map/ppermute | solution.py:292
  18.1 19.7 %collective-permute-start.6 = (f32[64,256]{1,0:T(8,128)}, f32[64,256]{1,0:T(8,128)S(1)}, u32[]{:S(2)}, u32[]{:S(2)}) collective-permute-start(f32[64,256]{1,0:T(8,128)} %get-tuple-element.45), channel_id=1, source_target_pairs={{0,14},{2,12},{4,10},{6,8},{8,6},{10,4},{12,2},{14,0},{16,30},{18,... | collective-permute-start | bytes 196616 | tf_op jit(solution)/shard_map/ppermute | solution.py:292
  21.6 22.6 %collective-permute-start.8 = (f32[64,256]{1,0:T(8,128)}, f32[64,256]{1,0:T(8,128)S(1)}, u32[]{:S(2)}, u32[]{:S(2)}) collective-permute-start(f32[64,256]{1,0:T(8,128)} %get-tuple-element.48), channel_id=1, source_target_pairs={{0,16},{2,18},{4,20},{6,22},{8,24},{10,26},{12,28},{14,30},{16,0},... | collective-permute-start | bytes 196616 | tf_op jit(solution)/shard_map/ppermute | solution.py:292
  31.2 13.0 %collective-permute-start.9 = (f32[64,256]{1,0:T(8,128)}, f32[64,256]{1,0:T(8,128)S(1)}, u32[]{:S(2)}, u32[]{:S(2)}) collective-permute-start(f32[64,256]{1,0:T(8,128)} %get-tuple-element.49), channel_id=1, source_target_pairs={{0,18},{2,16},{4,22},{6,20},{8,26},{10,24},{12,30},{14,28},{16,2},... | collective-permute-start | bytes 196616 | tf_op jit(solution)/shard_map/ppermute | solution.py:292
  33.4 14.3 %collective-permute-start.10 = (f32[64,256]{1,0:T(8,128)}, f32[64,256]{1,0:T(8,128)S(1)}, u32[]{:S(2)}, u32[]{:S(2)}) collective-permute-start(f32[64,256]{1,0:T(8,128)} %get-tuple-element.50), channel_id=1, source_target_pairs={{0,20},{2,22},{4,16},{6,18},{8,28},{10,30},{12,24},{14,26},{16,4},... | collective-permute-start | bytes 196616 | tf_op jit(solution)/shard_map/ppermute | solution.py:292
  38.6 9.1 %collective-permute-start.7 = (f32[16,8,128]{2,1,0:T(8,128)S(1)}, f32[16,8,128]{2,1,0:T(8,128)S(1)}, u32[]{:S(2)}, u32[]{:S(2)}) collective-permute-start(f32[16,8,128]{2,1,0:T(8,128)S(1)} %get-tuple-element.73), channel_id=1, source_target_pairs={{0,1},{1,0},{2,3},{3,2},{4,5},{5,4},{6,7},{7,6},{8,9},{9,8},{10,11... | collective-permute-start | bytes 196616 | tf_op jit(solution)/shard_map/ppermute | solution.py:292
  39.8 16.0 %collective-permute-start.11 = (f32[64,256]{1,0:T(8,128)}, f32[64,256]{1,0:T(8,128)S(1)}, u32[]{:S(2)}, u32[]{:S(2)}) collective-permute-start(f32[64,256]{1,0:T(8,128)} %get-tuple-element.51), channel_id=1, source_target_pairs={{0,22},{2,20},{4,18},{6,16},{8,30},{10,28},{12,26},{14,24},{16,6},... | collective-permute-start | bytes 196616 | tf_op jit(solution)/shard_map/ppermute | solution.py:292
  44.2 11.7 %collective-permute-start.12 = (f32[64,256]{1,0:T(8,128)}, f32[64,256]{1,0:T(8,128)S(1)}, u32[]{:S(2)}, u32[]{:S(2)}) collective-permute-start(f32[64,256]{1,0:T(8,128)} %get-tuple-element.52), channel_id=1, source_target_pairs={{0,24},{2,26},{4,28},{6,30},{8,16},{10,18},{12,20},{14,22},{16,8},... | collective-permute-start | bytes 196616 | tf_op jit(solution)/shard_map/ppermute | solution.py:292
  44.2 14.3 %collective-permute-start.13 = (f32[64,256]{1,0:T(8,128)}, f32[64,256]{1,0:T(8,128)S(1)}, u32[]{:S(2)}, u32[]{:S(2)}) collective-permute-start(f32[64,256]{1,0:T(8,128)} %get-tuple-element.53), channel_id=1, source_target_pairs={{0,26},{2,24},{4,30},{6,28},{8,18},{10,16},{12,22},{14,20},{16,10}... | collective-permute-start | bytes 196616 | tf_op jit(solution)/shard_map/ppermute | solution.py:292
  47.7 11.2 %collective-permute-start.14 = (f32[64,256]{1,0:T(8,128)}, f32[64,256]{1,0:T(8,128)S(1)}, u32[]{:S(2)}, u32[]{:S(2)}) collective-permute-start(f32[64,256]{1,0:T(8,128)} %get-tuple-element.54), channel_id=1, source_target_pairs={{0,28},{2,30},{4,24},{6,26},{8,20},{10,22},{12,16},{14,18},{16,12}... | collective-permute-start | bytes 196616 | tf_op jit(solution)/shard_map/ppermute | solution.py:292
  47.7 12.7 %collective-permute-start.15 = (f32[64,256]{1,0:T(8,128)}, f32[64,256]{1,0:T(8,128)S(1)}, u32[]{:S(2)}, u32[]{:S(2)}) collective-permute-start(f32[64,256]{1,0:T(8,128)} %get-tuple-element.55), channel_id=1, source_target_pairs={{0,30},{2,28},{4,26},{6,24},{8,22},{10,20},{12,18},{14,16},{16,14}... | collective-permute-start | bytes 196616 | tf_op jit(solution)/shard_map/ppermute | solution.py:292
  60.5 42.2 %all-to-all-start.1 = ((f32[16,64,256]{2,1,0:T(8,128)}), f32[16,64,256]{2,1,0:T(8,128)S(1)}, u32[]{:S(2)}, u32[]{:S(2)}) async-start(f32[16,64,256]{2,1,0:T(8,128)} %convolve.1), calls=%async_computation.1 | async-start | bytes 2097152 | tf_op jit(solution)/shard_map/all_to_all | solution.py:296
  72.5 3.9 %collective-permute-start.16 = (f32[64,256]{1,0:T(8,128)}, f32[64,256]{1,0:T(8,128)S(1)}, u32[]{:S(2)}, u32[]{:S(2)}) collective-permute-start(f32[64,256]{1,0:T(8,128)} %get-tuple-element.57), channel_id=1, source_target_pairs={{0,2},{2,0},{4,6},{6,4},{8,10},{10,8},{12,14},{14,12},{16,18},{18,... | collective-permute-start | bytes 196616 | tf_op jit(solution)/shard_map/ppermute | solution.py:292
  72.9 5.7 %collective-permute-start.17 = (f32[64,256]{1,0:T(8,128)}, f32[64,256]{1,0:T(8,128)S(1)}, u32[]{:S(2)}, u32[]{:S(2)}) collective-permute-start(f32[64,256]{1,0:T(8,128)} %get-tuple-element.58), channel_id=1, source_target_pairs={{0,4},{2,6},{4,0},{6,2},{8,12},{10,14},{12,8},{14,10},{16,20},{18,... | collective-permute-start | bytes 196616 | tf_op jit(solution)/shard_map/ppermute | solution.py:292
  74.1 7.3 %collective-permute-start.18 = (f32[64,256]{1,0:T(8,128)}, f32[64,256]{1,0:T(8,128)S(1)}, u32[]{:S(2)}, u32[]{:S(2)}) collective-permute-start(f32[64,256]{1,0:T(8,128)} %get-tuple-element.59), channel_id=1, source_target_pairs={{0,6},{2,4},{4,2},{6,0},{8,14},{10,12},{12,10},{14,8},{16,22},{18,... | collective-permute-start | bytes 196616 | tf_op jit(solution)/shard_map/ppermute | solution.py:292
  74.7 10.3 %collective-permute-start.19 = (f32[64,256]{1,0:T(8,128)}, f32[64,256]{1,0:T(8,128)S(1)}, u32[]{:S(2)}, u32[]{:S(2)}) collective-permute-start(f32[64,256]{1,0:T(8,128)} %get-tuple-element.60), channel_id=1, source_target_pairs={{0,8},{2,10},{4,12},{6,14},{8,0},{10,2},{12,4},{14,6},{16,24},{18,... | collective-permute-start | bytes 196616 | tf_op jit(solution)/shard_map/ppermute | solution.py:292
  74.8 12.4 %collective-permute-start.20 = (f32[64,256]{1,0:T(8,128)}, f32[64,256]{1,0:T(8,128)S(1)}, u32[]{:S(2)}, u32[]{:S(2)}) collective-permute-start(f32[64,256]{1,0:T(8,128)} %get-tuple-element.61), channel_id=1, source_target_pairs={{0,10},{2,8},{4,14},{6,12},{8,2},{10,0},{12,6},{14,4},{16,26},{18,... | collective-permute-start | bytes 196616 | tf_op jit(solution)/shard_map/ppermute | solution.py:292
  76.4 12.8 %collective-permute-start.21 = (f32[64,256]{1,0:T(8,128)}, f32[64,256]{1,0:T(8,128)S(1)}, u32[]{:S(2)}, u32[]{:S(2)}) collective-permute-start(f32[64,256]{1,0:T(8,128)} %get-tuple-element.62), channel_id=1, source_target_pairs={{0,12},{2,14},{4,8},{6,10},{8,4},{10,6},{12,0},{14,2},{16,28},{18,... | collective-permute-start | bytes 196616 | tf_op jit(solution)/shard_map/ppermute | solution.py:292
  78.6 12.9 %collective-permute-start.22 = (f32[64,256]{1,0:T(8,128)}, f32[64,256]{1,0:T(8,128)S(1)}, u32[]{:S(2)}, u32[]{:S(2)}) collective-permute-start(f32[64,256]{1,0:T(8,128)} %get-tuple-element.63), channel_id=1, source_target_pairs={{0,14},{2,12},{4,10},{6,8},{8,6},{10,4},{12,2},{14,0},{16,30},{18,... | collective-permute-start | bytes 196616 | tf_op jit(solution)/shard_map/ppermute | solution.py:292
  81.4 12.1 %collective-permute-start.23 = (f32[64,256]{1,0:T(8,128)}, f32[64,256]{1,0:T(8,128)S(1)}, u32[]{:S(2)}, u32[]{:S(2)}) collective-permute-start(f32[64,256]{1,0:T(8,128)} %get-tuple-element.64), channel_id=1, source_target_pairs={{0,16},{2,18},{4,20},{6,22},{8,24},{10,26},{12,28},{14,30},{16,0},... | collective-permute-start | bytes 196616 | tf_op jit(solution)/shard_map/ppermute | solution.py:292
  85.0 13.9 %collective-permute-start.24 = (f32[64,256]{1,0:T(8,128)}, f32[64,256]{1,0:T(8,128)S(1)}, u32[]{:S(2)}, u32[]{:S(2)}) collective-permute-start(f32[64,256]{1,0:T(8,128)} %get-tuple-element.65), channel_id=1, source_target_pairs={{0,18},{2,16},{4,22},{6,20},{8,26},{10,24},{12,30},{14,28},{16,2},... | collective-permute-start | bytes 196616 | tf_op jit(solution)/shard_map/ppermute | solution.py:292
  87.2 12.9 %collective-permute-start.25 = (f32[64,256]{1,0:T(8,128)}, f32[64,256]{1,0:T(8,128)S(1)}, u32[]{:S(2)}, u32[]{:S(2)}) collective-permute-start(f32[64,256]{1,0:T(8,128)} %get-tuple-element.66), channel_id=1, source_target_pairs={{0,20},{2,22},{4,16},{6,18},{8,28},{10,30},{12,24},{14,26},{16,4},... | collective-permute-start | bytes 196616 | tf_op jit(solution)/shard_map/ppermute | solution.py:292
  89.2 17.3 %collective-permute-start.26 = (f32[64,256]{1,0:T(8,128)}, f32[64,256]{1,0:T(8,128)S(1)}, u32[]{:S(2)}, u32[]{:S(2)}) collective-permute-start(f32[64,256]{1,0:T(8,128)} %get-tuple-element.67), channel_id=1, source_target_pairs={{0,22},{2,20},{4,18},{6,16},{8,30},{10,28},{12,26},{14,24},{16,6},... | collective-permute-start | bytes 196616 | tf_op jit(solution)/shard_map/ppermute | solution.py:292
  91.4 15.1 %collective-permute-start.27 = (f32[64,256]{1,0:T(8,128)}, f32[64,256]{1,0:T(8,128)S(1)}, u32[]{:S(2)}, u32[]{:S(2)}) collective-permute-start(f32[64,256]{1,0:T(8,128)} %get-tuple-element.68), channel_id=1, source_target_pairs={{0,24},{2,26},{4,28},{6,30},{8,16},{10,18},{12,20},{14,22},{16,8},... | collective-permute-start | bytes 196616 | tf_op jit(solution)/shard_map/ppermute | solution.py:292
  93.5 16.7 %collective-permute-start.28 = (f32[64,256]{1,0:T(8,128)}, f32[64,256]{1,0:T(8,128)S(1)}, u32[]{:S(2)}, u32[]{:S(2)}) collective-permute-start(f32[64,256]{1,0:T(8,128)} %get-tuple-element.69), channel_id=1, source_target_pairs={{0,26},{2,24},{4,30},{6,28},{8,18},{10,16},{12,22},{14,20},{16,10}... | collective-permute-start | bytes 196616 | tf_op jit(solution)/shard_map/ppermute | solution.py:292
  98.9 12.9 %collective-permute-start.29 = (f32[64,256]{1,0:T(8,128)}, f32[64,256]{1,0:T(8,128)S(1)}, u32[]{:S(2)}, u32[]{:S(2)}) collective-permute-start(f32[64,256]{1,0:T(8,128)} %get-tuple-element.70), channel_id=1, source_target_pairs={{0,28},{2,30},{4,24},{6,26},{8,20},{10,22},{12,16},{14,18},{16,12}... | collective-permute-start | bytes 196616 | tf_op jit(solution)/shard_map/ppermute | solution.py:292
  100.1 13.3 %collective-permute-start.30 = (f32[64,256]{1,0:T(8,128)}, f32[64,256]{1,0:T(8,128)S(1)}, u32[]{:S(2)}, u32[]{:S(2)}) collective-permute-start(f32[64,256]{1,0:T(8,128)} %get-tuple-element.71), channel_id=1, source_target_pairs={{0,30},{2,28},{4,26},{6,24},{8,22},{10,20},{12,18},{14,16},{16,14}... | collective-permute-start | bytes 196616 | tf_op jit(solution)/shard_map/ppermute | solution.py:292
  (34 other events, 553.5 us)

commit v4 on v3

--- a/solution.py
+++ b/solution.py
@@ -11,6 +11,7 @@
 GROUP = 16
 HALF = 128
 PAIR = 2
+CORES = 2
 VMEM_BYTES = 60 * 1024 * 1024
 
 HIGHEST_PRECISION = lax.Precision.HIGHEST
@@ -68,13 +69,15 @@
     outs, hold_ref = rest[:-1], rest[-1]
     hold_ref[...] = turned(sig_ref).reshape(hold_ref.shape)
     for j, out_ref in enumerate(outs):
-        out_ref[...] = hold_ref[place_ref[0] ^ j]
+        for e in range(CORES):
+            out_ref[e] = hold_ref[place_ref[0] ^ (CORES * j + e)]
 
 
 def turn_apart(place, signal, blocks):
     rows, width = signal.shape
     cols = width // 2
     shape = (cols // blocks, rows)
+    pairs = blocks // CORES
     return pl.pallas_call(
         turn_apart_kernel,
         grid=(1,),
@@ -82,8 +85,8 @@
             pl.BlockSpec(memory_space=pltpu.SMEM),
             pl.BlockSpec((rows, cols), lambda i: (0, 1)),
         ],
-        out_specs=[pl.BlockSpec(shape, lambda i: (0, 0))] * blocks,
-        out_shape=[jax.ShapeDtypeStruct(shape, jnp.float32)] * blocks,
+        out_specs=[pl.BlockSpec((CORES, *shape), lambda i: (0, 0, 0))] * pairs,
+        out_shape=[jax.ShapeDtypeStruct((CORES, *shape), jnp.float32)] * pairs,
         scratch_shapes=[pltpu.VMEM((blocks, *shape), jnp.float32)],
         compiler_params=pltpu.CompilerParams(vmem_limit_bytes=VMEM_BYTES),
         cost_estimate=pl.CostEstimate(flops=0, bytes_accessed=8 * rows * cols, transcendentals=0),
@@ -183,13 +186,15 @@
         out_ref[:, at, :] = sum_ref[...].reshape(blocks, GROUP, rows)
 
 
-def conv_apart_kernel(first, blocks, place_ref, own_ref, other_ref, *rest):
-    sigs, outs, hold_ref = rest[:blocks], rest[blocks : 2 * blocks], rest[2 * blocks]
-    scratch = rest[2 * blocks + 1 :]
+def conv_apart_kernel(first, pairs, place_ref, own_ref, other_ref, passed_ref, *rest):
+    blocks = CORES * pairs
+    sigs, outs, hold_ref = rest[:pairs], rest[pairs : pairs + blocks], rest[pairs + blocks]
+    scratch = rest[pairs + blocks + 1 :]
     rows = hold_ref.shape[2]
     me, side = place_ref[0], place_ref[1]
     for j, sig_ref in enumerate(sigs):
-        hold_ref[me ^ j] = sig_ref[...]
+        hold_ref[me ^ (CORES * j)] = sig_ref[0]
+        hold_ref[me ^ (CORES * j + 1)] = passed_ref[j]
     for u in range(PAIR):
         group = first + PAIR * pl.program_id(0) + u
         shifted_taps(side, group, own_ref, other_ref, scratch[3 * u], scratch[3 * u + 1])
@@ -236,24 +241,29 @@
     )(place, own, other, arrived)
 
 
-def convolve_apart(place, own, other, parts, first):
-    blocks = len(parts)
-    deep, rows = parts[0].shape
+def convolve_apart(place, own, other, passed, parts, first):
+    pairs, deep, rows = passed.shape
+    blocks = CORES * pairs
     groups = deep // GROUP
     taps_spec = pl.BlockSpec(own.shape, lambda g: (0, 0, 0))
-    pieces = [pl.BlockSpec((PAIR * GROUP, rows), lambda g: (g, 0))] * blocks
-    return pl.pallas_call(
-        functools.partial(conv_apart_kernel, first, blocks),
+    return pl.pallas_call(
+        functools.partial(conv_apart_kernel, first, pairs),
         grid=(groups // PAIR,),
-        in_specs=[pl.BlockSpec(memory_space=pltpu.SMEM), taps_spec, taps_spec] + pieces,
-        out_specs=pieces,
+        in_specs=[
+            pl.BlockSpec(memory_space=pltpu.SMEM),
+            taps_spec,
+            taps_spec,
+            pl.BlockSpec((pairs, PAIR * GROUP, rows), lambda g: (0, g, 0)),
+        ]
+        + [pl.BlockSpec((1, PAIR * GROUP, rows), lambda g: (0, g, 0))] * pairs,
+        out_specs=[pl.BlockSpec((PAIR * GROUP, rows), lambda g: (g, 0))] * blocks,
         out_shape=[jax.ShapeDtypeStruct((deep, rows), jnp.float32)] * blocks,
         scratch_shapes=[pltpu.VMEM((blocks, PAIR * GROUP, rows), jnp.float32)]
         + conv_scratch(blocks, rows),
         compiler_params=pltpu.CompilerParams(vmem_limit_bytes=VMEM_BYTES),
         cost_estimate=conv_cost(blocks, groups, rows),
         name="convolve_apart",
-    )(place, own, other, *parts)
+    )(place, own, other, passed, *parts)
 
 
 def home_apart_kernel(place_ref, *rest):
@@ -300,8 +310,8 @@
     return lax.optimization_barrier((value, *others))[0]
 
 
-def scatter(parts):
-    return [exchange(part, "seq", j) if j else part for j, part in enumerate(parts)]
+def scatter(parts, stride):
+    return [exchange(part, "seq", stride * j) if j else part for j, part in enumerate(parts)]
 
 
 def fast_body(signal, filters, skip_gain):
@@ -312,15 +322,18 @@
     place = jnp.stack([lax.axis_index("seq"), side]).astype(jnp.int32)
     gain = skip_gain.reshape(1, width)
     first = spread(turn_taps(signal, filters, blocks, (count, count)))
-    parts = scatter(turn_apart(place, signal, blocks))
-    first = after(first, *parts[1:8])
+    raw = turn_apart(place, signal, blocks)
+    parts = scatter(raw[:6], CORES)
+    first = after(first, *parts[1:4])
+    parts += [exchange(after(part, first), "seq", CORES * (6 + j)) for j, part in enumerate(raw[6:])]
     taps = first[:, count * GROUP :, :]
     own = lax.dynamic_slice_in_dim(taps, side * HALF, HALF, axis=2)
     other = exchange(lax.dynamic_slice_in_dim(taps, (1 - side) * HALF, HALF, axis=2), "ch", 1)
     values = convolve(place, own, other, first, 0, count)
-    values = after(values, *parts[8:])
+    values = after(values, *parts[4:8])
     back = spread(values).reshape(-1, rows)
-    parts = scatter(convolve_apart(place, own, other, parts, count))
+    passed = exchange(jnp.stack([part[1] for part in parts]), "seq", 1)
+    parts = scatter(convolve_apart(place, own, other, passed, parts, count), 1)
     out = home(back, signal, gain, 0, None)
     return home_apart(place, parts, signal, gain, out)
 
@@ -405,7 +418,7 @@
     rows, width = signal.shape
     lag_rows = filters.shape[0]
     fits = (
-        blocks > 1
+        blocks >= 2 * CORES
         and blocks & (blocks - 1) == 0
         and lax.axis_size("ch") == 2
         and width % (blocks * 2 * PAIR * GROUP) == 0

time: 118 us -> 117 us (level)
  starting transfers between devices: 63 us -> 55.8 us
  waiting for transfers between devices: 25.5 us -> 29.8 us
  local copies, waits for them, and re-layouts: 2.4 us -> 4.63 us
    ppermute x31 -> x24, starting transfers between devices: 51.7 us -> 45.3 us  [exchange(): return lax.ppermute(values, axis, [(i, i ^ step) for i in range(size)])]
    ppermute x31 -> x24, waiting for transfers between devices: 25.5 us -> 29 us  [exchange(): return lax.ppermute(values, axis, [(i, i ^ step) for i in range(size)])]
    unnamed x66 -> x59, local copies, waits for them, and re-layouts: 1.66 us -> 3.89 us
  transfers between devices with their start and end apart: 33 -> 26, of which waited for: 14 -> 8; matrix products, arithmetic and copies ran while one was open for 1% -> 2% of each run, Pallas kernels for 17% -> 17%
where the time goes in v4:
time: 117 us; the launch traced here: 116 us
  starting transfers between devices  55.8 us (48%)
  waiting for transfers between devices  29.8 us (25%)
  Pallas kernels  25.2 us (22%)
  local copies, waits for them, and re-layouts  4.63 us (4%)
    ppermute x24, starting transfers between devices, exchange(): return lax.ppermute(values, axis, [(i, i ^ step) for i in range(size)])  45.3 us
    ppermute x24, waiting for transfers between devices, exchange(): return lax.ppermute(values, axis, [(i, i ^ step) for i in range(size)])  29 us
    all_to_all x2, starting transfers between devices, spread(): lax.all_to_all(values, 'seq', split_axis=0, concat_axis=0, tiled=True)  10.5 us
    pallas_call x1, Pallas kernels, convolve_apart(): pl.pallas_call(functools.partial(conv_apart_kernel, first, pairs), grid=(...  7.17 us
    pallas_call x1, Pallas kernels, convolve(): pl.pallas_call(functools.partial(conv_kernel, first), grid=(groups // PAI...  6.93 us
    unnamed x59, local copies, waits for them, and re-layouts  3.89 us
    pallas_call x1, Pallas kernels, home_apart(): pl.pallas_call(home_apart_kernel, grid=(1,), in_specs=[pl.BlockSpec(memor...  3.06 us
    pallas_call x1, Pallas kernels, home(): pl.pallas_call(home_kernel, grid=(cols // step,), in_specs=in_specs, out_...  2.85 us
  transfers between devices with their start and end apart: 26, of which 8 were waited for; matrix products, arithmetic and copies ran while one was open for 2% of the time, Pallas kernels for 17%

profile of v4, /device:TPU:9, one launch (start us, length us, event | category | flops | bytes accessed | tf_op | source)
XLA Modules:
  0.0 116.3 jit_solution(86519182359408364)
XLA Ops:
  0.0 2.6 %turn_taps.1 = f32[16,72,256]{2,1,0:T(8,128)} custom-call(f32[256,2048]{1,0:T(8,128)} %rest_16_.1, f32[128,256]{1,0:T(8,128)} %taps_ref.1), custom_call_target="tpu_custom_call" | custom-call | bytes 2097152 | tf_op jit(solution)/shard_map/turn_taps/pallas_call | solution.py:53
  2.6 6.6 %all-to-all-start = ((f32[16,72,256]{2,1,0:T(8,128)}), f32[16,72,256]{2,1,0:T(8,128)S(1)}, u32[]{:S(2)}, u32[]{:S(2)}) async-start(f32[16,72,256]{2,1,0:T(8,128)} %turn_taps.1), calls=%async_computation | async-start | bytes 2359296 | tf_op jit(solution)/shard_map/all_to_all | solution.py:306
  9.8 2.6 %turn_apart.1 = (f32[2,64,256]{2,1,0:T(8,128)}, f32[2,64,256]{2,1,0:T(8,128)}, f32[2,64,256]{2,1,0:T(8,128)}, f32[2,64,256]{2,1,0:T(8,128)}, f32[2,64,256]{2,1,0...) custom-call(s32[2]{0:T(128)} %pad_add_fusion.place_ref, f32[256,2048]{1,0:T(8,128)} %rest_16_.1), custom_call_target="tpu_custom_call" | custom-call | bytes 2097152 | tf_op jit(solution)/shard_map/turn_apart/pallas_call | solution.py:81
  12.4 1.2 %collective-permute-start = (f32[2,64,256]{2,1,0:T(8,128)}, f32[2,64,256]{2,1,0:T(8,128)S(1)}, u32[]{:S(2)}, u32[]{:S(2)}) collective-permute-start(f32[2,64,256]{2,1,0:T(8,128)} %get-tuple-element.33), channel_id=1, source_target_pairs={{0,4},{2,6},{4,0},{6,2},{8,12},{10,14},{12,8},{14,10},{16,20},{18,... | collective-permute-start | bytes 393224 | tf_op jit(solution)/shard_map/ppermute | solution.py:302
  13.8 1.2 %collective-permute-start.2 = (f32[2,64,256]{2,1,0:T(8,128)}, f32[2,64,256]{2,1,0:T(8,128)S(1)}, u32[]{:S(2)}, u32[]{:S(2)}) collective-permute-start(f32[2,64,256]{2,1,0:T(8,128)} %get-tuple-element.35), channel_id=1, source_target_pairs={{0,12},{2,14},{4,8},{6,10},{8,4},{10,6},{12,0},{14,2},{16,28},{18,... | collective-permute-start | bytes 393224 | tf_op jit(solution)/shard_map/ppermute | solution.py:302
  15.0 2.1 %collective-permute-start.4 = (f32[2,64,256]{2,1,0:T(8,128)}, f32[2,64,256]{2,1,0:T(8,128)S(1)}, u32[]{:S(2)}, u32[]{:S(2)}) collective-permute-start(f32[2,64,256]{2,1,0:T(8,128)} %get-tuple-element.38), channel_id=1, source_target_pairs={{0,16},{2,18},{4,20},{6,22},{8,24},{10,26},{12,28},{14,30},{16,0},... | collective-permute-start | bytes 393224 | tf_op jit(solution)/shard_map/ppermute | solution.py:302
  17.1 1.2 %collective-permute-start.5 = (f32[2,64,256]{2,1,0:T(8,128)}, f32[2,64,256]{2,1,0:T(8,128)S(1)}, u32[]{:S(2)}, u32[]{:S(2)}) collective-permute-start(f32[2,64,256]{2,1,0:T(8,128)} %get-tuple-element.39), channel_id=1, source_target_pairs={{0,20},{2,22},{4,16},{6,18},{8,28},{10,30},{12,24},{14,26},{16,4},... | collective-permute-start | bytes 393224 | tf_op jit(solution)/shard_map/ppermute | solution.py:302
  19.2 13.4 %collective-permute-done.1.rest_2_ = f32[2,64,256]{2,1,0:T(8,128)S(1)} collective-permute-done((f32[2,64,256]{2,1,0:T(8,128)}, f32[2,64,256]{2,1,0:T(8,128)S(1)}, u32[]{:S(2)}, u32[]{:S(2)}) %collective-permute-start.1) | collective-permute-done | bytes 131104 | tf_op jit(solution)/shard_map/ppermute | solution.py:302
  32.6 4.4 %collective-permute-done.2.rest_3_ = f32[2,64,256]{2,1,0:T(8,128)S(1)} collective-permute-done((f32[2,64,256]{2,1,0:T(8,128)}, f32[2,64,256]{2,1,0:T(8,128)S(1)}, u32[]{:S(2)}, u32[]{:S(2)}) %collective-permute-start.2) | collective-permute-done | bytes 131104 | tf_op jit(solution)/shard_map/ppermute | solution.py:302
  38.5 1.2 %collective-permute-start.3 = (f32[16,8,128]{2,1,0:T(8,128)S(1)}, f32[16,8,128]{2,1,0:T(8,128)S(1)}, u32[]{:S(2)}, u32[]{:S(2)}) collective-permute-start(f32[16,8,128]{2,1,0:T(8,128)S(1)} %get-tuple-element.61), channel_id=1, source_target_pairs={{0,1},{1,0},{2,3},{3,2},{4,5},{5,4},{6,7},{7,6},{8,9},{9,8},{10,11... | collective-permute-start | bytes 196616 | tf_op jit(solution)/shard_map/ppermute | solution.py:302
  39.8 1.3 %collective-permute-start.6 = (f32[2,64,256]{2,1,0:T(8,128)}, f32[2,64,256]{2,1,0:T(8,128)S(1)}, u32[]{:S(2)}, u32[]{:S(2)}) collective-permute-start(f32[2,64,256]{2,1,0:T(8,128)} %get-tuple-element.41), channel_id=1, source_target_pairs={{0,24},{2,26},{4,28},{6,30},{8,16},{10,18},{12,20},{14,22},{16,8},... | collective-permute-start | bytes 393224 | tf_op jit(solution)/shard_map/ppermute | solution.py:302
  41.1 9.1 %collective-permute-start.7 = (f32[2,64,256]{2,1,0:T(8,128)}, f32[2,64,256]{2,1,0:T(8,128)S(1)}, u32[]{:S(2)}, u32[]{:S(2)}) collective-permute-start(f32[2,64,256]{2,1,0:T(8,128)} %get-tuple-element.43), channel_id=1, source_target_pairs={{0,28},{2,30},{4,24},{6,26},{8,20},{10,22},{12,16},{14,18},{16,12}... | collective-permute-start | bytes 393224 | tf_op jit(solution)/shard_map/ppermute | solution.py:302
  50.8 6.9 %convolve.1 = f32[16,64,256]{2,1,0:T(8,128)} custom-call(s32[2]{0:T(128)} %pad_add_fusion.place_ref, f32[16,8,128]{2,1,0:T(8,128)} %get-tuple-element.62.own_ref, f32[16,8,128]{2,1,0:T(8,128)} %copy-done.25, f32[16,72,256]{2,1,0:T(8,128)} %copy-done.1), custom_call_target="tpu_custom_call" | custom-call | flops 3422552064 | bytes 2097152 | tf_op jit(solution)/shard_map/convolve/pallas_call | solution.py:231
  57.8 2.6 %collective-permute-done.7.rest_7_ = f32[2,64,256]{2,1,0:T(8,128)S(1)} collective-permute-done((f32[2,64,256]{2,1,0:T(8,128)}, f32[2,64,256]{2,1,0:T(8,128)S(1)}, u32[]{:S(2)}, u32[]{:S(2)}) %collective-permute-start.7) | collective-permute-done | bytes 131104 | tf_op jit(solution)/shard_map/ppermute | solution.py:302
  60.5 3.9 %all-to-all-start.1 = ((f32[16,64,256]{2,1,0:T(8,128)}), f32[16,64,256]{2,1,0:T(8,128)S(1)}, u32[]{:S(2)}, u32[]{:S(2)}) async-start(f32[16,64,256]{2,1,0:T(8,128)} %convolve.1), calls=%async_computation.1 | async-start | bytes 2097152 | tf_op jit(solution)/shard_map/all_to_all | solution.py:306
  64.9 1.5 %collective-permute-done.8.passed_ref = f32[8,64,256]{2,1,0:T(8,128)S(1)} collective-permute-done((f32[8,64,256]{2,1,0:T(8,128)S(1)}, f32[8,64,256]{2,1,0:T(8,128)S(1)}, u32[]{:S(2)}, u32[]{:S(2)}) %collective-permute-start.8) | collective-permute-done | bytes 524320 | tf_op jit(solution)/shard_map/ppermute | solution.py:302
  67.2 7.2 %convolve_apart.1 = (f32[64,256]{1,0:T(8,128)}, f32[64,256]{1,0:T(8,128)}, f32[64,256]{1,0:T(8,128)}, f32[64,256]{1,0:T(8,128)}, f32[64,256]{1,0:T(8,128)}, /*in...) custom-call(s32[2]{0:T(128)} %pad_add_fusion.place_ref, ...), custom_call_target="tpu_custom_call" | custom-call | flops 3422552064 | bytes 2097152 | tf_op jit(solution)/shard_map/convolve_apart/pallas_call | solution.py:249
  74.8 1.2 %collective-permute-start.10 = (f32[64,256]{1,0:T(8,128)}, f32[64,256]{1,0:T(8,128)S(1)}, u32[]{:S(2)}, u32[]{:S(2)}) collective-permute-start(f32[64,256]{1,0:T(8,128)} %get-tuple-element.46), channel_id=1, source_target_pairs={{0,4},{2,6},{4,0},{6,2},{8,12},{10,14},{12,8},{14,10},{16,20},{18,... | collective-permute-start | bytes 196616 | tf_op jit(solution)/shard_map/ppermute | solution.py:302
  76.7 1.6 %collective-permute-start.13 = (f32[64,256]{1,0:T(8,128)}, f32[64,256]{1,0:T(8,128)S(1)}, u32[]{:S(2)}, u32[]{:S(2)}) collective-permute-start(f32[64,256]{1,0:T(8,128)} %get-tuple-element.49), channel_id=1, source_target_pairs={{0,10},{2,8},{4,14},{6,12},{8,2},{10,0},{12,6},{14,4},{16,26},{18,... | collective-permute-start | bytes 196616 | tf_op jit(solution)/shard_map/ppermute | solution.py:302
  78.3 1.2 %collective-permute-start.14 = (f32[64,256]{1,0:T(8,128)}, f32[64,256]{1,0:T(8,128)S(1)}, u32[]{:S(2)}, u32[]{:S(2)}) collective-permute-start(f32[64,256]{1,0:T(8,128)} %get-tuple-element.50), channel_id=1, source_target_pairs={{0,12},{2,14},{4,8},{6,10},{8,4},{10,6},{12,0},{14,2},{16,28},{18,... | collective-permute-start | bytes 196616 | tf_op jit(solution)/shard_map/ppermute | solution.py:302
  79.5 3.9 %collective-permute-start.15 = (f32[64,256]{1,0:T(8,128)}, f32[64,256]{1,0:T(8,128)S(1)}, u32[]{:S(2)}, u32[]{:S(2)}) collective-permute-start(f32[64,256]{1,0:T(8,128)} %get-tuple-element.51), channel_id=1, source_target_pairs={{0,14},{2,12},{4,10},{6,8},{8,6},{10,4},{12,2},{14,0},{16,30},{18,... | collective-permute-start | bytes 196616 | tf_op jit(solution)/shard_map/ppermute | solution.py:302
  83.4 1.3 %collective-permute-start.16 = (f32[64,256]{1,0:T(8,128)}, f32[64,256]{1,0:T(8,128)S(1)}, u32[]{:S(2)}, u32[]{:S(2)}) collective-permute-start(f32[64,256]{1,0:T(8,128)} %get-tuple-element.52), channel_id=1, source_target_pairs={{0,16},{2,18},{4,20},{6,22},{8,24},{10,26},{12,28},{14,30},{16,0},... | collective-permute-start | bytes 196616 | tf_op jit(solution)/shard_map/ppermute | solution.py:302
  84.7 2.1 %collective-permute-start.17 = (f32[64,256]{1,0:T(8,128)}, f32[64,256]{1,0:T(8,128)S(1)}, u32[]{:S(2)}, u32[]{:S(2)}) collective-permute-start(f32[64,256]{1,0:T(8,128)} %get-tuple-element.53), channel_id=1, source_target_pairs={{0,18},{2,16},{4,22},{6,20},{8,26},{10,24},{12,30},{14,28},{16,2},... | collective-permute-start | bytes 196616 | tf_op jit(solution)/shard_map/ppermute | solution.py:302
  86.8 3.5 %collective-permute-start.18 = (f32[64,256]{1,0:T(8,128)}, f32[64,256]{1,0:T(8,128)S(1)}, u32[]{:S(2)}, u32[]{:S(2)}) collective-permute-start(f32[64,256]{1,0:T(8,128)} %get-tuple-element.54), channel_id=1, source_target_pairs={{0,20},{2,22},{4,16},{6,18},{8,28},{10,30},{12,24},{14,26},{16,4},... | collective-permute-start | bytes 196616 | tf_op jit(solution)/shard_map/ppermute | solution.py:302
  90.3 3.0 %collective-permute-start.19 = (f32[64,256]{1,0:T(8,128)}, f32[64,256]{1,0:T(8,128)S(1)}, u32[]{:S(2)}, u32[]{:S(2)}) collective-permute-start(f32[64,256]{1,0:T(8,128)} %get-tuple-element.55), channel_id=1, source_target_pairs={{0,22},{2,20},{4,18},{6,16},{8,30},{10,28},{12,26},{14,24},{16,6},... | collective-permute-start | bytes 196616 | tf_op jit(solution)/shard_map/ppermute | solution.py:302
  93.4 4.7 %collective-permute-start.21 = (f32[64,256]{1,0:T(8,128)}, f32[64,256]{1,0:T(8,128)S(1)}, u32[]{:S(2)}, u32[]{:S(2)}) collective-permute-start(f32[64,256]{1,0:T(8,128)} %get-tuple-element.57), channel_id=1, source_target_pairs={{0,26},{2,24},{4,30},{6,28},{8,18},{10,16},{12,22},{14,20},{16,10}... | collective-permute-start | bytes 196616 | tf_op jit(solution)/shard_map/ppermute | solution.py:302
  99.2 2.7 %collective-permute-start.23 = (f32[64,256]{1,0:T(8,128)}, f32[64,256]{1,0:T(8,128)S(1)}, u32[]{:S(2)}, u32[]{:S(2)}) collective-permute-start(f32[64,256]{1,0:T(8,128)} %get-tuple-element.59), channel_id=1, source_target_pairs={{0,30},{2,28},{4,26},{6,24},{8,22},{10,20},{12,18},{14,16},{16,14}... | collective-permute-start | bytes 196616 | tf_op jit(solution)/shard_map/ppermute | solution.py:302
  102.8 2.9 %home.1.rest_18_ = f32[256,2048]{1,0:T(8,128)} custom-call(f32[1024,256]{1,0:T(8,128)} %bitcast.4, f32[256,2048]{1,0:T(8,128)} %rest_16_.1, f32[1,2048]{1,0:T(1,128)} %bitcast.5), custom_call_target="tpu_custom_call" | custom-call | bytes 3145728 | tf_op jit(solution)/shard_map/home/pallas_call | solution.py:117
  105.7 3.7 %collective-permute-done.21.rest_13_ = f32[64,256]{1,0:T(8,128)S(1)} collective-permute-done((f32[64,256]{1,0:T(8,128)}, f32[64,256]{1,0:T(8,128)S(1)}, u32[]{:S(2)}, u32[]{:S(2)}) %collective-permute-start.21) | collective-permute-done | bytes 65568 | tf_op jit(solution)/shard_map/ppermute | solution.py:302
  109.4 1.7 %collective-permute-done.22.rest_14_ = f32[64,256]{1,0:T(8,128)S(1)} collective-permute-done((f32[64,256]{1,0:T(8,128)}, f32[64,256]{1,0:T(8,128)S(1)}, u32[]{:S(2)}, u32[]{:S(2)}) %collective-permute-start.22) | collective-permute-done | bytes 65568 | tf_op jit(solution)/shard_map/ppermute | solution.py:302
  111.1 1.6 %collective-permute-done.23.rest_15_ = f32[64,256]{1,0:T(8,128)S(1)} collective-permute-done((f32[64,256]{1,0:T(8,128)}, f32[64,256]{1,0:T(8,128)S(1)}, u32[]{:S(2)}, u32[]{:S(2)}) %collective-permute-start.23) | collective-permute-done | bytes 65568 | tf_op jit(solution)/shard_map/ppermute | solution.py:302
  113.3 3.1 %home_apart.1 = f32[256,2048]{1,0:T(8,128)} custom-call(s32[2]{0:T(128)} %pad_add_fusion.place_ref, f32[64,256]{1,0:T(8,128)} %get-tuple-element.44.rest_0_, f32[64,256]{1,0:T(8,128)} %copy-done.2, f32[64,256]{1,0:T(8,128)} %copy-done.3, f32[64,256]{1,0:T(8,128)} %copy-done.4, f32[64,256]{1,0:T(8,128)} %copy-done.5, ...), custom_call_target="tpu_custom_call", output_to_operand_aliasing={{}: (19, {})} | custom-call | bytes 3145728 | tf_op jit(solution)/shard_map/home_apart/pallas_call | solution.py:283
  (89 shorter events, 8.9 us)
Async XLA Ops:
  2.6 35.2 %all-to-all-start = ((f32[16,72,256]{2,1,0:T(8,128)}), f32[16,72,256]{2,1,0:T(8,128)S(1)}, u32[]{:S(2)}, u32[]{:S(2)}) async-start(f32[16,72,256]{2,1,0:T(8,128)} %turn_taps.1), calls=%async_computation | async-start | bytes 2359296 | tf_op jit(solution)/shard_map/all_to_all | solution.py:306
  12.4 6.8 %collective-permute-start = (f32[2,64,256]{2,1,0:T(8,128)}, f32[2,64,256]{2,1,0:T(8,128)S(1)}, u32[]{:S(2)}, u32[]{:S(2)}) collective-permute-start(f32[2,64,256]{2,1,0:T(8,128)} %get-tuple-element.33), channel_id=1, source_target_pairs={{0,4},{2,6},{4,0},{6,2},{8,12},{10,14},{12,8},{14,10},{16,20},{18,... | collective-permute-start | bytes 393224 | tf_op jit(solution)/shard_map/ppermute | solution.py:302
  13.6 19.0 %collective-permute-start.1 = (f32[2,64,256]{2,1,0:T(8,128)}, f32[2,64,256]{2,1,0:T(8,128)S(1)}, u32[]{:S(2)}, u32[]{:S(2)}) collective-permute-start(f32[2,64,256]{2,1,0:T(8,128)} %get-tuple-element.34), channel_id=1, source_target_pairs={{0,8},{2,10},{4,12},{6,14},{8,0},{10,2},{12,4},{14,6},{16,24},{18,... | collective-permute-start | bytes 393224 | tf_op jit(solution)/shard_map/ppermute | solution.py:302
  13.8 23.2 %collective-permute-start.2 = (f32[2,64,256]{2,1,0:T(8,128)}, f32[2,64,256]{2,1,0:T(8,128)S(1)}, u32[]{:S(2)}, u32[]{:S(2)}) collective-permute-start(f32[2,64,256]{2,1,0:T(8,128)} %get-tuple-element.35), channel_id=1, source_target_pairs={{0,12},{2,14},{4,8},{6,10},{8,4},{10,6},{12,0},{14,2},{16,28},{18,... | collective-permute-start | bytes 393224 | tf_op jit(solution)/shard_map/ppermute | solution.py:302
  15.0 42.7 %collective-permute-start.4 = (f32[2,64,256]{2,1,0:T(8,128)}, f32[2,64,256]{2,1,0:T(8,128)S(1)}, u32[]{:S(2)}, u32[]{:S(2)}) collective-permute-start(f32[2,64,256]{2,1,0:T(8,128)} %get-tuple-element.38), channel_id=1, source_target_pairs={{0,16},{2,18},{4,20},{6,22},{8,24},{10,26},{12,28},{14,30},{16,0},... | collective-permute-start | bytes 393224 | tf_op jit(solution)/shard_map/ppermute | solution.py:302
  17.1 40.7 %collective-permute-start.5 = (f32[2,64,256]{2,1,0:T(8,128)}, f32[2,64,256]{2,1,0:T(8,128)S(1)}, u32[]{:S(2)}, u32[]{:S(2)}) collective-permute-start(f32[2,64,256]{2,1,0:T(8,128)} %get-tuple-element.39), channel_id=1, source_target_pairs={{0,20},{2,22},{4,16},{6,18},{8,28},{10,30},{12,24},{14,26},{16,4},... | collective-permute-start | bytes 393224 | tf_op jit(solution)/shard_map/ppermute | solution.py:302
  19.1 38.6 %copy-start.17 = (f32[2,64,256]{2,1,0:T(8,128)}, f32[2,64,256]{2,1,0:T(8,128)S(1)}, u32[]{:S(2)}) copy-start(f32[2,64,256]{2,1,0:T(8,128)S(1)} %collective-permute-done.rest_1_) | copy-start | bytes 393220
  37.0 27.4 %copy-start.19 = (f32[2,64,256]{2,1,0:T(8,128)}, f32[2,64,256]{2,1,0:T(8,128)S(1)}, u32[]{:S(2)}) copy-start(f32[2,64,256]{2,1,0:T(8,128)S(1)} %collective-permute-done.2.rest_3_) | copy-start | bytes 393220
  38.5 11.7 %collective-permute-start.3 = (f32[16,8,128]{2,1,0:T(8,128)S(1)}, f32[16,8,128]{2,1,0:T(8,128)S(1)}, u32[]{:S(2)}, u32[]{:S(2)}) collective-permute-start(f32[16,8,128]{2,1,0:T(8,128)S(1)} %get-tuple-element.61), channel_id=1, source_target_pairs={{0,1},{1,0},{2,3},{3,2},{4,5},{5,4},{6,7},{7,6},{8,9},{9,8},{10,11... | collective-permute-start | bytes 196616 | tf_op jit(solution)/shard_map/ppermute | solution.py:302
  39.8 18.0 %collective-permute-start.6 = (f32[2,64,256]{2,1,0:T(8,128)}, f32[2,64,256]{2,1,0:T(8,128)S(1)}, u32[]{:S(2)}, u32[]{:S(2)}) collective-permute-start(f32[2,64,256]{2,1,0:T(8,128)} %get-tuple-element.41), channel_id=1, source_target_pairs={{0,24},{2,26},{4,28},{6,30},{8,16},{10,18},{12,20},{14,22},{16,8},... | collective-permute-start | bytes 393224 | tf_op jit(solution)/shard_map/ppermute | solution.py:302
  41.1 19.4 %collective-permute-start.7 = (f32[2,64,256]{2,1,0:T(8,128)}, f32[2,64,256]{2,1,0:T(8,128)S(1)}, u32[]{:S(2)}, u32[]{:S(2)}) collective-permute-start(f32[2,64,256]{2,1,0:T(8,128)} %get-tuple-element.43), channel_id=1, source_target_pairs={{0,28},{2,30},{4,24},{6,26},{8,20},{10,22},{12,16},{14,18},{16,12}... | collective-permute-start | bytes 393224 | tf_op jit(solution)/shard_map/ppermute | solution.py:302
  60.5 41.4 %all-to-all-start.1 = ((f32[16,64,256]{2,1,0:T(8,128)}), f32[16,64,256]{2,1,0:T(8,128)S(1)}, u32[]{:S(2)}, u32[]{:S(2)}) async-start(f32[16,64,256]{2,1,0:T(8,128)} %convolve.1), calls=%async_computation.1 | async-start | bytes 2097152 | tf_op jit(solution)/shard_map/all_to_all | solution.py:306
  64.4 2.0 %collective-permute-start.8 = (f32[8,64,256]{2,1,0:T(8,128)S(1)}, f32[8,64,256]{2,1,0:T(8,128)S(1)}, u32[]{:S(2)}, u32[]{:S(2)}) collective-permute-start(f32[8,64,256]{2,1,0:T(8,128)S(1)} %slice_dynamic-update-slice_fusion), channel_id=1, source_target_pairs={{0,2},{2,0},{4,6},{6,4},{8,10},{10,8},{12,14},{14,12},{16,18},{18,... | collective-permute-start | bytes 1572872 | tf_op jit(solution)/shard_map/ppermute | solution.py:302
  74.4 3.9 %collective-permute-start.9 = (f32[64,256]{1,0:T(8,128)}, f32[64,256]{1,0:T(8,128)S(1)}, u32[]{:S(2)}, u32[]{:S(2)}) collective-permute-start(f32[64,256]{1,0:T(8,128)} %get-tuple-element.45), channel_id=1, source_target_pairs={{0,2},{2,0},{4,6},{6,4},{8,10},{10,8},{12,14},{14,12},{16,18},{18,... | collective-permute-start | bytes 196616 | tf_op jit(solution)/shard_map/ppermute | solution.py:302
  74.8 4.7 %collective-permute-start.10 = (f32[64,256]{1,0:T(8,128)}, f32[64,256]{1,0:T(8,128)S(1)}, u32[]{:S(2)}, u32[]{:S(2)}) collective-permute-start(f32[64,256]{1,0:T(8,128)} %get-tuple-element.46), channel_id=1, source_target_pairs={{0,4},{2,6},{4,0},{6,2},{8,12},{10,14},{12,8},{14,10},{16,20},{18,... | collective-permute-start | bytes 196616 | tf_op jit(solution)/shard_map/ppermute | solution.py:302
  76.0 7.4 %collective-permute-start.11 = (f32[64,256]{1,0:T(8,128)}, f32[64,256]{1,0:T(8,128)S(1)}, u32[]{:S(2)}, u32[]{:S(2)}) collective-permute-start(f32[64,256]{1,0:T(8,128)} %get-tuple-element.47), channel_id=1, source_target_pairs={{0,6},{2,4},{4,2},{6,0},{8,14},{10,12},{12,10},{14,8},{16,22},{18,... | collective-permute-start | bytes 196616 | tf_op jit(solution)/shard_map/ppermute | solution.py:302
  76.6 8.1 %collective-permute-start.12 = (f32[64,256]{1,0:T(8,128)}, f32[64,256]{1,0:T(8,128)S(1)}, u32[]{:S(2)}, u32[]{:S(2)}) collective-permute-start(f32[64,256]{1,0:T(8,128)} %get-tuple-element.48), channel_id=1, source_target_pairs={{0,8},{2,10},{4,12},{6,14},{8,0},{10,2},{12,4},{14,6},{16,24},{18,... | collective-permute-start | bytes 196616 | tf_op jit(solution)/shard_map/ppermute | solution.py:302
  76.7 10.1 %collective-permute-start.13 = (f32[64,256]{1,0:T(8,128)}, f32[64,256]{1,0:T(8,128)S(1)}, u32[]{:S(2)}, u32[]{:S(2)}) collective-permute-start(f32[64,256]{1,0:T(8,128)} %get-tuple-element.49), channel_id=1, source_target_pairs={{0,10},{2,8},{4,14},{6,12},{8,2},{10,0},{12,6},{14,4},{16,26},{18,... | collective-permute-start | bytes 196616 | tf_op jit(solution)/shard_map/ppermute | solution.py:302
  78.3 34.3 %copy-start.2 = (f32[64,256]{1,0:T(8,128)}, f32[64,256]{1,0:T(8,128)S(1)}, u32[]{:S(2)}) copy-start(f32[64,256]{1,0:T(8,128)S(1)} %collective-permute-done.9.rest_1_) | copy-start | bytes 196612
  78.3 12.0 %collective-permute-start.14 = (f32[64,256]{1,0:T(8,128)}, f32[64,256]{1,0:T(8,128)S(1)}, u32[]{:S(2)}, u32[]{:S(2)}) collective-permute-start(f32[64,256]{1,0:T(8,128)} %get-tuple-element.50), channel_id=1, source_target_pairs={{0,12},{2,14},{4,8},{6,10},{8,4},{10,6},{12,0},{14,2},{16,28},{18,... | collective-permute-start | bytes 196616 | tf_op jit(solution)/shard_map/ppermute | solution.py:302
  79.5 33.1 %copy-start.3 = (f32[64,256]{1,0:T(8,128)}, f32[64,256]{1,0:T(8,128)S(1)}, u32[]{:S(2)}) copy-start(f32[64,256]{1,0:T(8,128)S(1)} %collective-permute-done.10.rest_2_) | copy-start | bytes 196612
  79.5 13.8 %collective-permute-start.15 = (f32[64,256]{1,0:T(8,128)}, f32[64,256]{1,0:T(8,128)S(1)}, u32[]{:S(2)}, u32[]{:S(2)}) collective-permute-start(f32[64,256]{1,0:T(8,128)} %get-tuple-element.51), channel_id=1, source_target_pairs={{0,14},{2,12},{4,10},{6,8},{8,6},{10,4},{12,2},{14,0},{16,30},{18,... | collective-permute-start | bytes 196616 | tf_op jit(solution)/shard_map/ppermute | solution.py:302
  83.4 29.3 %copy-start.4 = (f32[64,256]{1,0:T(8,128)}, f32[64,256]{1,0:T(8,128)S(1)}, u32[]{:S(2)}) copy-start(f32[64,256]{1,0:T(8,128)S(1)} %collective-permute-done.11.rest_3_) | copy-start | bytes 196612
  83.4 10.0 %collective-permute-start.16 = (f32[64,256]{1,0:T(8,128)}, f32[64,256]{1,0:T(8,128)S(1)}, u32[]{:S(2)}, u32[]{:S(2)}) collective-permute-start(f32[64,256]{1,0:T(8,128)} %get-tuple-element.52), channel_id=1, source_target_pairs={{0,16},{2,18},{4,20},{6,22},{8,24},{10,26},{12,28},{14,30},{16,0},... | collective-permute-start | bytes 196616 | tf_op jit(solution)/shard_map/ppermute | solution.py:302
  84.7 28.0 %copy-start.5 = (f32[64,256]{1,0:T(8,128)}, f32[64,256]{1,0:T(8,128)S(1)}, u32[]{:S(2)}) copy-start(f32[64,256]{1,0:T(8,128)S(1)} %collective-permute-done.12.rest_4_) | copy-start | bytes 196612
  84.7 13.4 %collective-permute-start.17 = (f32[64,256]{1,0:T(8,128)}, f32[64,256]{1,0:T(8,128)S(1)}, u32[]{:S(2)}, u32[]{:S(2)}) collective-permute-start(f32[64,256]{1,0:T(8,128)} %get-tuple-element.53), channel_id=1, source_target_pairs={{0,18},{2,16},{4,22},{6,20},{8,26},{10,24},{12,30},{14,28},{16,2},... | collective-permute-start | bytes 196616 | tf_op jit(solution)/shard_map/ppermute | solution.py:302
  86.8 12.4 %collective-permute-start.18 = (f32[64,256]{1,0:T(8,128)}, f32[64,256]{1,0:T(8,128)S(1)}, u32[]{:S(2)}, u32[]{:S(2)}) collective-permute-start(f32[64,256]{1,0:T(8,128)} %get-tuple-element.54), channel_id=1, source_target_pairs={{0,20},{2,22},{4,16},{6,18},{8,28},{10,30},{12,24},{14,26},{16,4},... | collective-permute-start | bytes 196616 | tf_op jit(solution)/shard_map/ppermute | solution.py:302
  90.3 15.4 %collective-permute-start.19 = (f32[64,256]{1,0:T(8,128)}, f32[64,256]{1,0:T(8,128)S(1)}, u32[]{:S(2)}, u32[]{:S(2)}) collective-permute-start(f32[64,256]{1,0:T(8,128)} %get-tuple-element.55), channel_id=1, source_target_pairs={{0,22},{2,20},{4,18},{6,16},{8,30},{10,28},{12,26},{14,24},{16,6},... | collective-permute-start | bytes 196616 | tf_op jit(solution)/shard_map/ppermute | solution.py:302
  93.3 12.4 %collective-permute-start.20 = (f32[64,256]{1,0:T(8,128)}, f32[64,256]{1,0:T(8,128)S(1)}, u32[]{:S(2)}, u32[]{:S(2)}) collective-permute-start(f32[64,256]{1,0:T(8,128)} %get-tuple-element.56), channel_id=1, source_target_pairs={{0,24},{2,26},{4,28},{6,30},{8,16},{10,18},{12,20},{14,22},{16,8},... | collective-permute-start | bytes 196616 | tf_op jit(solution)/shard_map/ppermute | solution.py:302
  93.4 16.0 %collective-permute-start.21 = (f32[64,256]{1,0:T(8,128)}, f32[64,256]{1,0:T(8,128)S(1)}, u32[]{:S(2)}, u32[]{:S(2)}) collective-permute-start(f32[64,256]{1,0:T(8,128)} %get-tuple-element.57), channel_id=1, source_target_pairs={{0,26},{2,24},{4,30},{6,28},{8,18},{10,16},{12,22},{14,20},{16,10}... | collective-permute-start | bytes 196616 | tf_op jit(solution)/shard_map/ppermute | solution.py:302
  98.1 13.0 %collective-permute-start.22 = (f32[64,256]{1,0:T(8,128)}, f32[64,256]{1,0:T(8,128)S(1)}, u32[]{:S(2)}, u32[]{:S(2)}) collective-permute-start(f32[64,256]{1,0:T(8,128)} %get-tuple-element.58), channel_id=1, source_target_pairs={{0,28},{2,30},{4,24},{6,26},{8,20},{10,22},{12,16},{14,18},{16,12}... | collective-permute-start | bytes 196616 | tf_op jit(solution)/shard_map/ppermute | solution.py:302
  99.2 13.5 %collective-permute-start.23 = (f32[64,256]{1,0:T(8,128)}, f32[64,256]{1,0:T(8,128)S(1)}, u32[]{:S(2)}, u32[]{:S(2)}) collective-permute-start(f32[64,256]{1,0:T(8,128)} %get-tuple-element.59), channel_id=1, source_target_pairs={{0,30},{2,28},{4,26},{6,24},{8,22},{10,20},{12,18},{14,16},{16,14}... | collective-permute-start | bytes 196616 | tf_op jit(solution)/shard_map/ppermute | solution.py:302
  (20 other events, 206.8 us)

commit v5 on v4

--- a/solution.py
+++ b/solution.py
@@ -323,14 +323,14 @@
     gain = skip_gain.reshape(1, width)
     first = spread(turn_taps(signal, filters, blocks, (count, count)))
     raw = turn_apart(place, signal, blocks)
-    parts = scatter(raw[:6], CORES)
+    parts = scatter(raw[:5], CORES)
     first = after(first, *parts[1:4])
-    parts += [exchange(after(part, first), "seq", CORES * (6 + j)) for j, part in enumerate(raw[6:])]
+    parts += [exchange(after(part, parts[3]), "seq", CORES * (5 + j)) for j, part in enumerate(raw[5:])]
     taps = first[:, count * GROUP :, :]
     own = lax.dynamic_slice_in_dim(taps, side * HALF, HALF, axis=2)
     other = exchange(lax.dynamic_slice_in_dim(taps, (1 - side) * HALF, HALF, axis=2), "ch", 1)
     values = convolve(place, own, other, first, 0, count)
-    values = after(values, *parts[4:8])
+    values = after(values, *parts[1:5])
     back = spread(values).reshape(-1, rows)
     passed = exchange(jnp.stack([part[1] for part in parts]), "seq", 1)
     parts = scatter(convolve_apart(place, own, other, passed, parts, count), 1)

time: 117 us -> 115 us (0.983)
  starting transfers between devices: 55.8 us -> 54 us
    ppermute x24, starting transfers between devices: 45.3 us -> 36.9 us  [exchange(): return lax.ppermute(values, axis, [(i, i ^ step) for i in range(size)])]
    all_to_all x2, starting transfers between devices: 10.5 us -> 17.1 us  [spread(): lax.all_to_all(values, 'seq', split_axis=0, concat_axis=0, tiled=True)]
  transfers between devices with their start and end apart: 26 -> 26, of which waited for: 8 -> 6; matrix products, arithmetic and copies ran while one was open for 2% -> 2% of each run, Pallas kernels for 17% -> 17%
where the time goes in v5:
time: 115 us
  starting transfers between devices  54 us (47%)
  waiting for transfers between devices  29.7 us (26%)
  Pallas kernels  25.2 us (22%)
  local copies, waits for them, and re-layouts  4.69 us (4%)
    ppermute x24, starting transfers between devices, exchange(): return lax.ppermute(values, axis, [(i, i ^ step) for i in range(size)])  36.9 us
    ppermute x24, waiting for transfers between devices, exchange(): return lax.ppermute(values, axis, [(i, i ^ step) for i in range(size)])  29.7 us
    all_to_all x2, starting transfers between devices, spread(): lax.all_to_all(values, 'seq', split_axis=0, concat_axis=0, tiled=True)  17.1 us
    pallas_call x1, Pallas kernels, convolve_apart(): pl.pallas_call(functools.partial(conv_apart_kernel, first, pairs), grid=(...  7.17 us
    pallas_call x1, Pallas kernels, convolve(): pl.pallas_call(functools.partial(conv_kernel, first), grid=(groups // PAI...  6.93 us
    unnamed x59, local copies, waits for them, and re-layouts  3.89 us
    pallas_call x1, Pallas kernels, home_apart(): pl.pallas_call(home_apart_kernel, grid=(1,), in_specs=[pl.BlockSpec(memor...  3.06 us
    pallas_call x1, Pallas kernels, home(): pl.pallas_call(home_kernel, grid=(cols // step,), in_specs=in_specs, out_...  2.85 us
  transfers between devices with their start and end apart: 26, of which 6 were waited for; matrix products, arithmetic and copies ran while one was open for 2% of the time, Pallas kernels for 17%

profile of v5, /device:TPU:9, one launch (start us, length us, event | category | flops | bytes accessed | tf_op | source)
XLA Modules:
  0.0 114.5 jit_solution(8984453634488296452)
XLA Ops:
  0.0 2.6 %turn_taps.1 = f32[16,72,256]{2,1,0:T(8,128)} custom-call(f32[256,2048]{1,0:T(8,128)} %rest_16_.1, f32[128,256]{1,0:T(8,128)} %taps_ref.1), custom_call_target="tpu_custom_call" | custom-call | bytes 2097152 | tf_op jit(solution)/shard_map/turn_taps/pallas_call | solution.py:53
  2.6 6.6 %all-to-all-start = ((f32[16,72,256]{2,1,0:T(8,128)}), f32[16,72,256]{2,1,0:T(8,128)S(1)}, u32[]{:S(2)}, u32[]{:S(2)}) async-start(f32[16,72,256]{2,1,0:T(8,128)} %turn_taps.1), calls=%async_computation | async-start | bytes 2359296 | tf_op jit(solution)/shard_map/all_to_all | solution.py:306
  9.8 2.6 %turn_apart.1 = (f32[2,64,256]{2,1,0:T(8,128)}, f32[2,64,256]{2,1,0:T(8,128)}, f32[2,64,256]{2,1,0:T(8,128)}, f32[2,64,256]{2,1,0:T(8,128)}, f32[2,64,256]{2,1,0...) custom-call(s32[2]{0:T(128)} %pad_add_fusion.place_ref, f32[256,2048]{1,0:T(8,128)} %rest_16_.1), custom_call_target="tpu_custom_call" | custom-call | bytes 2097152 | tf_op jit(solution)/shard_map/turn_apart/pallas_call | solution.py:81
  12.4 1.2 %collective-permute-start = (f32[2,64,256]{2,1,0:T(8,128)}, f32[2,64,256]{2,1,0:T(8,128)S(1)}, u32[]{:S(2)}, u32[]{:S(2)}) collective-permute-start(f32[2,64,256]{2,1,0:T(8,128)} %get-tuple-element.34), channel_id=1, source_target_pairs={{0,4},{2,6},{4,0},{6,2},{8,12},{10,14},{12,8},{14,10},{16,20},{18,... | collective-permute-start | bytes 393224 | tf_op jit(solution)/shard_map/ppermute | solution.py:302
  13.8 1.2 %collective-permute-start.2 = (f32[2,64,256]{2,1,0:T(8,128)}, f32[2,64,256]{2,1,0:T(8,128)S(1)}, u32[]{:S(2)}, u32[]{:S(2)}) collective-permute-start(f32[2,64,256]{2,1,0:T(8,128)} %get-tuple-element.36), channel_id=1, source_target_pairs={{0,12},{2,14},{4,8},{6,10},{8,4},{10,6},{12,0},{14,2},{16,28},{18,... | collective-permute-start | bytes 393224 | tf_op jit(solution)/shard_map/ppermute | solution.py:302
  15.0 2.1 %collective-permute-start.4 = (f32[2,64,256]{2,1,0:T(8,128)}, f32[2,64,256]{2,1,0:T(8,128)S(1)}, u32[]{:S(2)}, u32[]{:S(2)}) collective-permute-start(f32[2,64,256]{2,1,0:T(8,128)} %get-tuple-element.39), channel_id=1, source_target_pairs={{0,16},{2,18},{4,20},{6,22},{8,24},{10,26},{12,28},{14,30},{16,0},... | collective-permute-start | bytes 393224 | tf_op jit(solution)/shard_map/ppermute | solution.py:302
  18.0 19.0 %collective-permute-done.2.rest_3_ = f32[2,64,256]{2,1,0:T(8,128)S(1)} collective-permute-done((f32[2,64,256]{2,1,0:T(8,128)}, f32[2,64,256]{2,1,0:T(8,128)S(1)}, u32[]{:S(2)}, u32[]{:S(2)}) %collective-permute-start.2) | collective-permute-done | bytes 131104 | tf_op jit(solution)/shard_map/ppermute | solution.py:302
  37.7 1.4 %collective-permute-start.6 = (f32[2,64,256]{2,1,0:T(8,128)}, f32[2,64,256]{2,1,0:T(8,128)S(1)}, u32[]{:S(2)}, u32[]{:S(2)}) collective-permute-start(f32[2,64,256]{2,1,0:T(8,128)} %get-tuple-element.43), channel_id=1, source_target_pairs={{0,24},{2,26},{4,28},{6,30},{8,16},{10,18},{12,20},{14,22},{16,8},... | collective-permute-start | bytes 393224 | tf_op jit(solution)/shard_map/ppermute | solution.py:302
  39.1 1.1 collective-permute-start.7
  41.0 1.2 %collective-permute-start.3 = (f32[16,8,128]{2,1,0:T(8,128)S(1)}, f32[16,8,128]{2,1,0:T(8,128)S(1)}, u32[]{:S(2)}, u32[]{:S(2)}) collective-permute-start(f32[16,8,128]{2,1,0:T(8,128)S(1)} %get-tuple-element.63), channel_id=1, source_target_pairs={{0,1},{1,0},{2,3},{3,2},{4,5},{5,4},{6,7},{7,6},{8,9},{9,8},{10,11... | collective-permute-start | bytes 196616 | tf_op jit(solution)/shard_map/ppermute | solution.py:302
  42.3 2.2 %collective-permute-done.3.other_ref = f32[16,8,128]{2,1,0:T(8,128)S(1)} collective-permute-done((f32[16,8,128]{2,1,0:T(8,128)S(1)}, f32[16,8,128]{2,1,0:T(8,128)S(1)}, u32[]{:S(2)}, u32[]{:S(2)}) %collective-permute-start.3) | collective-permute-done | bytes 65568 | tf_op jit(solution)/shard_map/ppermute | solution.py:302
  45.1 6.9 %convolve.1 = f32[16,64,256]{2,1,0:T(8,128)} custom-call(s32[2]{0:T(128)} %pad_add_fusion.place_ref, f32[16,8,128]{2,1,0:T(8,128)} %get-tuple-element.64.own_ref, f32[16,8,128]{2,1,0:T(8,128)} %copy-done.25, f32[16,72,256]{2,1,0:T(8,128)} %copy-done.1), custom_call_target="tpu_custom_call" | custom-call | flops 3422552064 | bytes 2097152 | tf_op jit(solution)/shard_map/convolve/pallas_call | solution.py:231
  52.0 10.5 %all-to-all-start.1 = ((f32[16,64,256]{2,1,0:T(8,128)}), f32[16,64,256]{2,1,0:T(8,128)S(1)}, u32[]{:S(2)}, u32[]{:S(2)}) async-start(f32[16,64,256]{2,1,0:T(8,128)} %convolve.1), calls=%async_computation.1 | async-start | bytes 2097152 | tf_op jit(solution)/shard_map/all_to_all | solution.py:306
  63.1 1.5 %collective-permute-done.8.passed_ref = f32[8,64,256]{2,1,0:T(8,128)S(1)} collective-permute-done((f32[8,64,256]{2,1,0:T(8,128)S(1)}, f32[8,64,256]{2,1,0:T(8,128)S(1)}, u32[]{:S(2)}, u32[]{:S(2)}) %collective-permute-start.8) | collective-permute-done | bytes 524320 | tf_op jit(solution)/shard_map/ppermute | solution.py:302
  65.5 7.2 %convolve_apart.1 = (f32[64,256]{1,0:T(8,128)}, f32[64,256]{1,0:T(8,128)}, f32[64,256]{1,0:T(8,128)}, f32[64,256]{1,0:T(8,128)}, f32[64,256]{1,0:T(8,128)}, /*in...) custom-call(s32[2]{0:T(128)} %pad_add_fusion.place_ref, ...), custom_call_target="tpu_custom_call" | custom-call | flops 3422552064 | bytes 2097152 | tf_op jit(solution)/shard_map/convolve_apart/pallas_call | solution.py:249
  73.1 1.2 %collective-permute-start.10 = (f32[64,256]{1,0:T(8,128)}, f32[64,256]{1,0:T(8,128)S(1)}, u32[]{:S(2)}, u32[]{:S(2)}) collective-permute-start(f32[64,256]{1,0:T(8,128)} %get-tuple-element.48), channel_id=1, source_target_pairs={{0,4},{2,6},{4,0},{6,2},{8,12},{10,14},{12,8},{14,10},{16,20},{18,... | collective-permute-start | bytes 196616 | tf_op jit(solution)/shard_map/ppermute | solution.py:302
  74.9 1.7 %collective-permute-start.13 = (f32[64,256]{1,0:T(8,128)}, f32[64,256]{1,0:T(8,128)S(1)}, u32[]{:S(2)}, u32[]{:S(2)}) collective-permute-start(f32[64,256]{1,0:T(8,128)} %get-tuple-element.51), channel_id=1, source_target_pairs={{0,10},{2,8},{4,14},{6,12},{8,2},{10,0},{12,6},{14,4},{16,26},{18,... | collective-permute-start | bytes 196616 | tf_op jit(solution)/shard_map/ppermute | solution.py:302
  76.6 1.2 %collective-permute-start.14 = (f32[64,256]{1,0:T(8,128)}, f32[64,256]{1,0:T(8,128)S(1)}, u32[]{:S(2)}, u32[]{:S(2)}) collective-permute-start(f32[64,256]{1,0:T(8,128)} %get-tuple-element.52), channel_id=1, source_target_pairs={{0,12},{2,14},{4,8},{6,10},{8,4},{10,6},{12,0},{14,2},{16,28},{18,... | collective-permute-start | bytes 196616 | tf_op jit(solution)/shard_map/ppermute | solution.py:302
  77.7 3.8 %collective-permute-start.15 = (f32[64,256]{1,0:T(8,128)}, f32[64,256]{1,0:T(8,128)S(1)}, u32[]{:S(2)}, u32[]{:S(2)}) collective-permute-start(f32[64,256]{1,0:T(8,128)} %get-tuple-element.53), channel_id=1, source_target_pairs={{0,14},{2,12},{4,10},{6,8},{8,6},{10,4},{12,2},{14,0},{16,30},{18,... | collective-permute-start | bytes 196616 | tf_op jit(solution)/shard_map/ppermute | solution.py:302
  81.6 1.4 %collective-permute-start.16 = (f32[64,256]{1,0:T(8,128)}, f32[64,256]{1,0:T(8,128)S(1)}, u32[]{:S(2)}, u32[]{:S(2)}) collective-permute-start(f32[64,256]{1,0:T(8,128)} %get-tuple-element.54), channel_id=1, source_target_pairs={{0,16},{2,18},{4,20},{6,22},{8,24},{10,26},{12,28},{14,30},{16,0},... | collective-permute-start | bytes 196616 | tf_op jit(solution)/shard_map/ppermute | solution.py:302
  82.9 2.1 %collective-permute-start.17 = (f32[64,256]{1,0:T(8,128)}, f32[64,256]{1,0:T(8,128)S(1)}, u32[]{:S(2)}, u32[]{:S(2)}) collective-permute-start(f32[64,256]{1,0:T(8,128)} %get-tuple-element.55), channel_id=1, source_target_pairs={{0,18},{2,16},{4,22},{6,20},{8,26},{10,24},{12,30},{14,28},{16,2},... | collective-permute-start | bytes 196616 | tf_op jit(solution)/shard_map/ppermute | solution.py:302
  85.0 3.5 %collective-permute-start.18 = (f32[64,256]{1,0:T(8,128)}, f32[64,256]{1,0:T(8,128)S(1)}, u32[]{:S(2)}, u32[]{:S(2)}) collective-permute-start(f32[64,256]{1,0:T(8,128)} %get-tuple-element.56), channel_id=1, source_target_pairs={{0,20},{2,22},{4,16},{6,18},{8,28},{10,30},{12,24},{14,26},{16,4},... | collective-permute-start | bytes 196616 | tf_op jit(solution)/shard_map/ppermute | solution.py:302
  88.5 3.0 %collective-permute-start.19 = (f32[64,256]{1,0:T(8,128)}, f32[64,256]{1,0:T(8,128)S(1)}, u32[]{:S(2)}, u32[]{:S(2)}) collective-permute-start(f32[64,256]{1,0:T(8,128)} %get-tuple-element.57), channel_id=1, source_target_pairs={{0,22},{2,20},{4,18},{6,16},{8,30},{10,28},{12,26},{14,24},{16,6},... | collective-permute-start | bytes 196616 | tf_op jit(solution)/shard_map/ppermute | solution.py:302
  91.5 4.8 %collective-permute-start.21 = (f32[64,256]{1,0:T(8,128)}, f32[64,256]{1,0:T(8,128)S(1)}, u32[]{:S(2)}, u32[]{:S(2)}) collective-permute-start(f32[64,256]{1,0:T(8,128)} %get-tuple-element.59), channel_id=1, source_target_pairs={{0,26},{2,24},{4,30},{6,28},{8,18},{10,16},{12,22},{14,20},{16,10}... | collective-permute-start | bytes 196616 | tf_op jit(solution)/shard_map/ppermute | solution.py:302
  96.3 1.0 collective-permute-start.22
  97.3 2.8 %collective-permute-start.23 = (f32[64,256]{1,0:T(8,128)}, f32[64,256]{1,0:T(8,128)S(1)}, u32[]{:S(2)}, u32[]{:S(2)}) collective-permute-start(f32[64,256]{1,0:T(8,128)} %get-tuple-element.61), channel_id=1, source_target_pairs={{0,30},{2,28},{4,26},{6,24},{8,22},{10,20},{12,18},{14,16},{16,14}... | collective-permute-start | bytes 196616 | tf_op jit(solution)/shard_map/ppermute | solution.py:302
  100.0 1.0 copy-done
  101.0 2.9 %home.1.rest_18_ = f32[256,2048]{1,0:T(8,128)} custom-call(f32[1024,256]{1,0:T(8,128)} %bitcast.4, f32[256,2048]{1,0:T(8,128)} %rest_16_.1, f32[1,2048]{1,0:T(1,128)} %bitcast.5), custom_call_target="tpu_custom_call" | custom-call | bytes 3145728 | tf_op jit(solution)/shard_map/home/pallas_call | solution.py:117
  103.9 3.7 %collective-permute-done.21.rest_13_ = f32[64,256]{1,0:T(8,128)S(1)} collective-permute-done((f32[64,256]{1,0:T(8,128)}, f32[64,256]{1,0:T(8,128)S(1)}, u32[]{:S(2)}, u32[]{:S(2)}) %collective-permute-start.21) | collective-permute-done | bytes 65568 | tf_op jit(solution)/shard_map/ppermute | solution.py:302
  107.6 1.7 %collective-permute-done.22.rest_14_ = f32[64,256]{1,0:T(8,128)S(1)} collective-permute-done((f32[64,256]{1,0:T(8,128)}, f32[64,256]{1,0:T(8,128)S(1)}, u32[]{:S(2)}, u32[]{:S(2)}) %collective-permute-start.22) | collective-permute-done | bytes 65568 | tf_op jit(solution)/shard_map/ppermute | solution.py:302
  109.3 1.6 %collective-permute-done.23.rest_15_ = f32[64,256]{1,0:T(8,128)S(1)} collective-permute-done((f32[64,256]{1,0:T(8,128)}, f32[64,256]{1,0:T(8,128)S(1)}, u32[]{:S(2)}, u32[]{:S(2)}) %collective-permute-start.23) | collective-permute-done | bytes 65568 | tf_op jit(solution)/shard_map/ppermute | solution.py:302
  111.5 3.1 %home_apart.1 = f32[256,2048]{1,0:T(8,128)} custom-call(s32[2]{0:T(128)} %pad_add_fusion.place_ref, f32[64,256]{1,0:T(8,128)} %get-tuple-element.46.rest_0_, f32[64,256]{1,0:T(8,128)} %copy-done.2, f32[64,256]{1,0:T(8,128)} %copy-done.3, f32[64,256]{1,0:T(8,128)} %copy-done.4, f32[64,256]{1,0:T(8,128)} %copy-done.5, ...), custom_call_target="tpu_custom_call", output_to_operand_aliasing={{}: (19, {})} | custom-call | bytes 3145728 | tf_op jit(solution)/shard_map/home_apart/pallas_call | solution.py:283
  (89 shorter events, 6.8 us)
Async XLA Ops:
  2.6 37.6 %all-to-all-start = ((f32[16,72,256]{2,1,0:T(8,128)}), f32[16,72,256]{2,1,0:T(8,128)S(1)}, u32[]{:S(2)}, u32[]{:S(2)}) async-start(f32[16,72,256]{2,1,0:T(8,128)} %turn_taps.1), calls=%async_computation | async-start | bytes 2359296 | tf_op jit(solution)/shard_map/all_to_all | solution.py:306
  12.4 26.7 %collective-permute-start = (f32[2,64,256]{2,1,0:T(8,128)}, f32[2,64,256]{2,1,0:T(8,128)S(1)}, u32[]{:S(2)}, u32[]{:S(2)}) collective-permute-start(f32[2,64,256]{2,1,0:T(8,128)} %get-tuple-element.34), channel_id=1, source_target_pairs={{0,4},{2,6},{4,0},{6,2},{8,12},{10,14},{12,8},{14,10},{16,20},{18,... | collective-permute-start | bytes 393224 | tf_op jit(solution)/shard_map/ppermute | solution.py:302
  13.6 26.6 %collective-permute-start.1 = (f32[2,64,256]{2,1,0:T(8,128)}, f32[2,64,256]{2,1,0:T(8,128)S(1)}, u32[]{:S(2)}, u32[]{:S(2)}) collective-permute-start(f32[2,64,256]{2,1,0:T(8,128)} %get-tuple-element.35), channel_id=1, source_target_pairs={{0,8},{2,10},{4,12},{6,14},{8,0},{10,2},{12,4},{14,6},{16,24},{18,... | collective-permute-start | bytes 393224 | tf_op jit(solution)/shard_map/ppermute | solution.py:302
  13.8 23.2 %collective-permute-start.2 = (f32[2,64,256]{2,1,0:T(8,128)}, f32[2,64,256]{2,1,0:T(8,128)S(1)}, u32[]{:S(2)}, u32[]{:S(2)}) collective-permute-start(f32[2,64,256]{2,1,0:T(8,128)} %get-tuple-element.36), channel_id=1, source_target_pairs={{0,12},{2,14},{4,8},{6,10},{8,4},{10,6},{12,0},{14,2},{16,28},{18,... | collective-permute-start | bytes 393224 | tf_op jit(solution)/shard_map/ppermute | solution.py:302
  15.0 37.0 %collective-permute-start.4 = (f32[2,64,256]{2,1,0:T(8,128)}, f32[2,64,256]{2,1,0:T(8,128)S(1)}, u32[]{:S(2)}, u32[]{:S(2)}) collective-permute-start(f32[2,64,256]{2,1,0:T(8,128)} %get-tuple-element.39), channel_id=1, source_target_pairs={{0,16},{2,18},{4,20},{6,22},{8,24},{10,26},{12,28},{14,30},{16,0},... | collective-permute-start | bytes 393224 | tf_op jit(solution)/shard_map/ppermute | solution.py:302
  37.0 25.5 %copy-start.19 = (f32[2,64,256]{2,1,0:T(8,128)}, f32[2,64,256]{2,1,0:T(8,128)S(1)}, u32[]{:S(2)}) copy-start(f32[2,64,256]{2,1,0:T(8,128)S(1)} %collective-permute-done.2.rest_3_) | copy-start | bytes 393220
  37.0 25.6 %collective-permute-start.5 = (f32[2,64,256]{2,1,0:T(8,128)}, f32[2,64,256]{2,1,0:T(8,128)S(1)}, u32[]{:S(2)}, u32[]{:S(2)}) collective-permute-start(f32[2,64,256]{2,1,0:T(8,128)} %get-tuple-element.41), channel_id=1, source_target_pairs={{0,20},{2,22},{4,16},{6,18},{8,28},{10,30},{12,24},{14,26},{16,4},... | collective-permute-start | bytes 393224 | tf_op jit(solution)/shard_map/ppermute | solution.py:302
  37.7 24.9 %collective-permute-start.6 = (f32[2,64,256]{2,1,0:T(8,128)}, f32[2,64,256]{2,1,0:T(8,128)S(1)}, u32[]{:S(2)}, u32[]{:S(2)}) collective-permute-start(f32[2,64,256]{2,1,0:T(8,128)} %get-tuple-element.43), channel_id=1, source_target_pairs={{0,24},{2,26},{4,28},{6,30},{8,16},{10,18},{12,20},{14,22},{16,8},... | collective-permute-start | bytes 393224 | tf_op jit(solution)/shard_map/ppermute | solution.py:302
  39.1 23.5 %collective-permute-start.7 = (f32[2,64,256]{2,1,0:T(8,128)}, f32[2,64,256]{2,1,0:T(8,128)S(1)}, u32[]{:S(2)}, u32[]{:S(2)}) collective-permute-start(f32[2,64,256]{2,1,0:T(8,128)} %get-tuple-element.45), channel_id=1, source_target_pairs={{0,28},{2,30},{4,24},{6,26},{8,20},{10,22},{12,16},{14,18},{16,12}... | collective-permute-start | bytes 393224 | tf_op jit(solution)/shard_map/ppermute | solution.py:302
  41.0 3.4 %collective-permute-start.3 = (f32[16,8,128]{2,1,0:T(8,128)S(1)}, f32[16,8,128]{2,1,0:T(8,128)S(1)}, u32[]{:S(2)}, u32[]{:S(2)}) collective-permute-start(f32[16,8,128]{2,1,0:T(8,128)S(1)} %get-tuple-element.63), channel_id=1, source_target_pairs={{0,1},{1,0},{2,3},{3,2},{4,5},{5,4},{6,7},{7,6},{8,9},{9,8},{10,11... | collective-permute-start | bytes 196616 | tf_op jit(solution)/shard_map/ppermute | solution.py:302
  52.0 48.0 %all-to-all-start.1 = ((f32[16,64,256]{2,1,0:T(8,128)}), f32[16,64,256]{2,1,0:T(8,128)S(1)}, u32[]{:S(2)}, u32[]{:S(2)}) async-start(f32[16,64,256]{2,1,0:T(8,128)} %convolve.1), calls=%async_computation.1 | async-start | bytes 2097152 | tf_op jit(solution)/shard_map/all_to_all | solution.py:306
  62.7 2.0 %collective-permute-start.8 = (f32[8,64,256]{2,1,0:T(8,128)S(1)}, f32[8,64,256]{2,1,0:T(8,128)S(1)}, u32[]{:S(2)}, u32[]{:S(2)}) collective-permute-start(f32[8,64,256]{2,1,0:T(8,128)S(1)} %slice_dynamic-update-slice_fusion), channel_id=1, source_target_pairs={{0,2},{2,0},{4,6},{6,4},{8,10},{10,8},{12,14},{14,12},{16,18},{18,... | collective-permute-start | bytes 1572872 | tf_op jit(solution)/shard_map/ppermute | solution.py:302
  72.6 3.9 %collective-permute-start.9 = (f32[64,256]{1,0:T(8,128)}, f32[64,256]{1,0:T(8,128)S(1)}, u32[]{:S(2)}, u32[]{:S(2)}) collective-permute-start(f32[64,256]{1,0:T(8,128)} %get-tuple-element.47), channel_id=1, source_target_pairs={{0,2},{2,0},{4,6},{6,4},{8,10},{10,8},{12,14},{14,12},{16,18},{18,... | collective-permute-start | bytes 196616 | tf_op jit(solution)/shard_map/ppermute | solution.py:302
  73.1 4.7 %collective-permute-start.10 = (f32[64,256]{1,0:T(8,128)}, f32[64,256]{1,0:T(8,128)S(1)}, u32[]{:S(2)}, u32[]{:S(2)}) collective-permute-start(f32[64,256]{1,0:T(8,128)} %get-tuple-element.48), channel_id=1, source_target_pairs={{0,4},{2,6},{4,0},{6,2},{8,12},{10,14},{12,8},{14,10},{16,20},{18,... | collective-permute-start | bytes 196616 | tf_op jit(solution)/shard_map/ppermute | solution.py:302
  74.3 7.3 %collective-permute-start.11 = (f32[64,256]{1,0:T(8,128)}, f32[64,256]{1,0:T(8,128)S(1)}, u32[]{:S(2)}, u32[]{:S(2)}) collective-permute-start(f32[64,256]{1,0:T(8,128)} %get-tuple-element.49), channel_id=1, source_target_pairs={{0,6},{2,4},{4,2},{6,0},{8,14},{10,12},{12,10},{14,8},{16,22},{18,... | collective-permute-start | bytes 196616 | tf_op jit(solution)/shard_map/ppermute | solution.py:302
  74.9 8.1 %collective-permute-start.12 = (f32[64,256]{1,0:T(8,128)}, f32[64,256]{1,0:T(8,128)S(1)}, u32[]{:S(2)}, u32[]{:S(2)}) collective-permute-start(f32[64,256]{1,0:T(8,128)} %get-tuple-element.50), channel_id=1, source_target_pairs={{0,8},{2,10},{4,12},{6,14},{8,0},{10,2},{12,4},{14,6},{16,24},{18,... | collective-permute-start | bytes 196616 | tf_op jit(solution)/shard_map/ppermute | solution.py:302
  74.9 10.1 %collective-permute-start.13 = (f32[64,256]{1,0:T(8,128)}, f32[64,256]{1,0:T(8,128)S(1)}, u32[]{:S(2)}, u32[]{:S(2)}) collective-permute-start(f32[64,256]{1,0:T(8,128)} %get-tuple-element.51), channel_id=1, source_target_pairs={{0,10},{2,8},{4,14},{6,12},{8,2},{10,0},{12,6},{14,4},{16,26},{18,... | collective-permute-start | bytes 196616 | tf_op jit(solution)/shard_map/ppermute | solution.py:302
  76.6 34.3 %copy-start.2 = (f32[64,256]{1,0:T(8,128)}, f32[64,256]{1,0:T(8,128)S(1)}, u32[]{:S(2)}) copy-start(f32[64,256]{1,0:T(8,128)S(1)} %collective-permute-done.9.rest_1_) | copy-start | bytes 196612
  76.6 11.9 %collective-permute-start.14 = (f32[64,256]{1,0:T(8,128)}, f32[64,256]{1,0:T(8,128)S(1)}, u32[]{:S(2)}, u32[]{:S(2)}) collective-permute-start(f32[64,256]{1,0:T(8,128)} %get-tuple-element.52), channel_id=1, source_target_pairs={{0,12},{2,14},{4,8},{6,10},{8,4},{10,6},{12,0},{14,2},{16,28},{18,... | collective-permute-start | bytes 196616 | tf_op jit(solution)/shard_map/ppermute | solution.py:302
  77.7 33.1 %copy-start.3 = (f32[64,256]{1,0:T(8,128)}, f32[64,256]{1,0:T(8,128)S(1)}, u32[]{:S(2)}) copy-start(f32[64,256]{1,0:T(8,128)S(1)} %collective-permute-done.10.rest_2_) | copy-start | bytes 196612
  77.7 13.7 %collective-permute-start.15 = (f32[64,256]{1,0:T(8,128)}, f32[64,256]{1,0:T(8,128)S(1)}, u32[]{:S(2)}, u32[]{:S(2)}) collective-permute-start(f32[64,256]{1,0:T(8,128)} %get-tuple-element.53), channel_id=1, source_target_pairs={{0,14},{2,12},{4,10},{6,8},{8,6},{10,4},{12,2},{14,0},{16,30},{18,... | collective-permute-start | bytes 196616 | tf_op jit(solution)/shard_map/ppermute | solution.py:302
  81.6 29.3 %copy-start.4 = (f32[64,256]{1,0:T(8,128)}, f32[64,256]{1,0:T(8,128)S(1)}, u32[]{:S(2)}) copy-start(f32[64,256]{1,0:T(8,128)S(1)} %collective-permute-done.11.rest_3_) | copy-start | bytes 196612
  81.6 9.9 %collective-permute-start.16 = (f32[64,256]{1,0:T(8,128)}, f32[64,256]{1,0:T(8,128)S(1)}, u32[]{:S(2)}, u32[]{:S(2)}) collective-permute-start(f32[64,256]{1,0:T(8,128)} %get-tuple-element.54), channel_id=1, source_target_pairs={{0,16},{2,18},{4,20},{6,22},{8,24},{10,26},{12,28},{14,30},{16,0},... | collective-permute-start | bytes 196616 | tf_op jit(solution)/shard_map/ppermute | solution.py:302
  82.9 27.9 %copy-start.5 = (f32[64,256]{1,0:T(8,128)}, f32[64,256]{1,0:T(8,128)S(1)}, u32[]{:S(2)}) copy-start(f32[64,256]{1,0:T(8,128)S(1)} %collective-permute-done.12.rest_4_) | copy-start | bytes 196612
  82.9 13.4 %collective-permute-start.17 = (f32[64,256]{1,0:T(8,128)}, f32[64,256]{1,0:T(8,128)S(1)}, u32[]{:S(2)}, u32[]{:S(2)}) collective-permute-start(f32[64,256]{1,0:T(8,128)} %get-tuple-element.55), channel_id=1, source_target_pairs={{0,18},{2,16},{4,22},{6,20},{8,26},{10,24},{12,30},{14,28},{16,2},... | collective-permute-start | bytes 196616 | tf_op jit(solution)/shard_map/ppermute | solution.py:302
  85.0 25.9 %copy-start.6 = (f32[64,256]{1,0:T(8,128)}, f32[64,256]{1,0:T(8,128)S(1)}, u32[]{:S(2)}) copy-start(f32[64,256]{1,0:T(8,128)S(1)} %collective-permute-done.13.rest_5_) | copy-start | bytes 196612
  85.0 12.2 %collective-permute-start.18 = (f32[64,256]{1,0:T(8,128)}, f32[64,256]{1,0:T(8,128)S(1)}, u32[]{:S(2)}, u32[]{:S(2)}) collective-permute-start(f32[64,256]{1,0:T(8,128)} %get-tuple-element.56), channel_id=1, source_target_pairs={{0,20},{2,22},{4,16},{6,18},{8,28},{10,30},{12,24},{14,26},{16,4},... | collective-permute-start | bytes 196616 | tf_op jit(solution)/shard_map/ppermute | solution.py:302
  88.5 15.4 %collective-permute-start.19 = (f32[64,256]{1,0:T(8,128)}, f32[64,256]{1,0:T(8,128)S(1)}, u32[]{:S(2)}, u32[]{:S(2)}) collective-permute-start(f32[64,256]{1,0:T(8,128)} %get-tuple-element.57), channel_id=1, source_target_pairs={{0,22},{2,20},{4,18},{6,16},{8,30},{10,28},{12,26},{14,24},{16,6},... | collective-permute-start | bytes 196616 | tf_op jit(solution)/shard_map/ppermute | solution.py:302
  91.5 12.4 %collective-permute-start.20 = (f32[64,256]{1,0:T(8,128)}, f32[64,256]{1,0:T(8,128)S(1)}, u32[]{:S(2)}, u32[]{:S(2)}) collective-permute-start(f32[64,256]{1,0:T(8,128)} %get-tuple-element.58), channel_id=1, source_target_pairs={{0,24},{2,26},{4,28},{6,30},{8,16},{10,18},{12,20},{14,22},{16,8},... | collective-permute-start | bytes 196616 | tf_op jit(solution)/shard_map/ppermute | solution.py:302
  91.5 16.1 %collective-permute-start.21 = (f32[64,256]{1,0:T(8,128)}, f32[64,256]{1,0:T(8,128)S(1)}, u32[]{:S(2)}, u32[]{:S(2)}) collective-permute-start(f32[64,256]{1,0:T(8,128)} %get-tuple-element.59), channel_id=1, source_target_pairs={{0,26},{2,24},{4,30},{6,28},{8,18},{10,16},{12,22},{14,20},{16,10}... | collective-permute-start | bytes 196616 | tf_op jit(solution)/shard_map/ppermute | solution.py:302
  96.3 13.0 %collective-permute-start.22 = (f32[64,256]{1,0:T(8,128)}, f32[64,256]{1,0:T(8,128)S(1)}, u32[]{:S(2)}, u32[]{:S(2)}) collective-permute-start(f32[64,256]{1,0:T(8,128)} %get-tuple-element.60), channel_id=1, source_target_pairs={{0,28},{2,30},{4,24},{6,26},{8,20},{10,22},{12,16},{14,18},{16,12}... | collective-permute-start | bytes 196616 | tf_op jit(solution)/shard_map/ppermute | solution.py:302
  97.3 13.6 %collective-permute-start.23 = (f32[64,256]{1,0:T(8,128)}, f32[64,256]{1,0:T(8,128)S(1)}, u32[]{:S(2)}, u32[]{:S(2)}) collective-permute-start(f32[64,256]{1,0:T(8,128)} %get-tuple-element.61), channel_id=1, source_target_pairs={{0,30},{2,28},{4,26},{6,24},{8,22},{10,20},{12,18},{14,16},{16,14}... | collective-permute-start | bytes 196616 | tf_op jit(solution)/shard_map/ppermute | solution.py:302
  (20 other events, 159.4 us)

commit v6 on v5

--- a/solution.py
+++ b/solution.py
@@ -12,6 +12,7 @@
 HALF = 128
 PAIR = 2
 CORES = 2
+STEPS = 2
 VMEM_BYTES = 60 * 1024 * 1024
 
 HIGHEST_PRECISION = lax.Precision.HIGHEST
@@ -27,38 +28,40 @@
     return in_ref[...].T
 
 
-def turn_taps_kernel(counts, sig_ref, taps_ref, out_ref):
-    blocks, _, rows = out_ref.shape
-    per_chunk = sig_ref.shape[1] // blocks
+def turn_taps_kernel(counts, sig_ref, taps_ref, out_ref, lines_ref):
+    homes, _, rows = out_ref.shape
+    per_chunk = sig_ref.shape[1] // homes
     lag_rows, groups = taps_ref.shape
-    out_ref[:, :per_chunk, :] = turned(sig_ref).reshape(blocks, per_chunk, rows)
-    lines = turned(taps_ref)
+    out_ref[:, :per_chunk, :] = turned(sig_ref).reshape(homes, per_chunk, rows)
+    lines_ref[...] = turned(taps_ref)
     sides = rows // lag_rows
     for side in range(sides):
         row = per_chunk
         start = side * (groups // sides)
         for count in counts:
-            for q in range(blocks):
-                here = start + q * count
-                at = slice(side * lag_rows, (side + 1) * lag_rows)
-                out_ref[q, row : row + count, at] = lines[here : here + count]
+            here = start + pl.program_id(0) * (homes * count)
+            lines = lines_ref[pl.ds(pl.multiple_of(here, 8), homes * count), :]
+            at = slice(side * lag_rows, (side + 1) * lag_rows)
+            for q in range(homes):
+                out_ref[q, row : row + count, at] = lines[q * count : (q + 1) * count]
             row += count
-            start += blocks * count
+            start += homes * pl.num_programs(0) * count
 
 
 def turn_taps(signal, filters, blocks, counts):
     rows, width = signal.shape
     cols = blocks * counts[0] * GROUP
-    shape = (blocks, counts[0] * GROUP + sum(counts), rows)
+    deep = counts[0] * GROUP + sum(counts)
     return pl.pallas_call(
         functools.partial(turn_taps_kernel, counts),
-        grid=(1,),
+        grid=(STEPS,),
         in_specs=[
-            pl.BlockSpec((rows, cols), lambda i: (0, 0)),
+            pl.BlockSpec((rows, cols // STEPS), lambda i: (0, i)),
             pl.BlockSpec(filters.shape, lambda i: (0, 0)),
         ],
-        out_specs=pl.BlockSpec(shape, lambda i: (0, 0, 0)),
-        out_shape=jax.ShapeDtypeStruct(shape, jnp.float32),
+        out_specs=pl.BlockSpec((blocks // STEPS, deep, rows), lambda i: (i, 0, 0)),
+        out_shape=jax.ShapeDtypeStruct((blocks, deep, rows), jnp.float32),
+        scratch_shapes=[pltpu.VMEM(filters.shape[::-1], jnp.float32)],
         compiler_params=pltpu.CompilerParams(vmem_limit_bytes=VMEM_BYTES),
         cost_estimate=pl.CostEstimate(flops=0, bytes_accessed=8 * rows * cols, transcendentals=0),
         name="turn_taps",
@@ -269,9 +272,15 @@
 def home_apart_kernel(place_ref, *rest):
     back_refs, (sig_ref, gain_ref, _, out_ref, hold_ref) = rest[:-5], rest[-5:]
     me = place_ref[0]
-    for j, back_ref in enumerate(back_refs):
-        hold_ref[me ^ j] = back_ref[...]
-    values = hold_ref[...].reshape(sig_ref.shape[1], sig_ref.shape[0])
+    step = pl.program_id(0)
+
+    @pl.when(step == 0)
+    def _():
+        for j, back_ref in enumerate(back_refs):
+            hold_ref[me ^ j] = back_ref[...]
+
+    homes = hold_ref.shape[0] // STEPS
+    values = hold_ref[pl.ds(step * homes, homes)].reshape(sig_ref.shape[1], sig_ref.shape[0])
     out_ref[...] = values.T + gain_ref[...] * sig_ref[...]
 
 
@@ -279,15 +288,15 @@
     rows, width = signal.shape
     blocks, per_chunk = len(backs), backs[0].shape[0]
     cols = blocks * per_chunk
-    here = lambda i: (0, 1)
+    here = lambda i: (0, STEPS + i)
     return pl.pallas_call(
         home_apart_kernel,
-        grid=(1,),
+        grid=(STEPS,),
         in_specs=[pl.BlockSpec(memory_space=pltpu.SMEM)]
         + [pl.BlockSpec((per_chunk, rows), lambda i: (0, 0))] * blocks
-        + [pl.BlockSpec((rows, cols), here), pl.BlockSpec((1, cols), here)]
+        + [pl.BlockSpec((rows, cols // STEPS), here), pl.BlockSpec((1, cols // STEPS), here)]
         + [pl.BlockSpec(memory_space=pl.ANY)],
-        out_specs=pl.BlockSpec((rows, cols), here),
+        out_specs=pl.BlockSpec((rows, cols // STEPS), here),
         out_shape=jax.ShapeDtypeStruct((rows, width), jnp.float32),
         input_output_aliases={blocks + 3: 0},
         scratch_shapes=[pltpu.VMEM((blocks, per_chunk, rows), jnp.float32)],
@@ -424,6 +433,8 @@
         and width % (blocks * 2 * PAIR * GROUP) == 0
         and rows == 2 * HALF
         and lag_rows == HALF
+        and width % (2 * STEPS * HALF) == 0
+        and blocks % STEPS == 0
     )
     if fits:
         return fast_body(signal, filters, skip_gain)

time: 115 us -> 114 us (level)
  no operation moved by 1% of the time
where the time goes in v6:
time: 114 us
  starting transfers between devices  54 us (47%)
  waiting for transfers between devices  29.7 us (26%)
  Pallas kernels  24.6 us (22%)
  local copies, waits for them, and re-layouts  4.69 us (4%)
    ppermute x24, starting transfers between devices, exchange(): return lax.ppermute(values, axis, [(i, i ^ step) for i in range(size)])  36.9 us
    ppermute x24, waiting for transfers between devices, exchange(): return lax.ppermute(values, axis, [(i, i ^ step) for i in range(size)])  29.7 us
    all_to_all x2, starting transfers between devices, spread(): lax.all_to_all(values, 'seq', split_axis=0, concat_axis=0, tiled=True)  17.1 us
    pallas_call x1, Pallas kernels, convolve_apart(): pl.pallas_call(functools.partial(conv_apart_kernel, first, pairs), grid=(...  7.17 us
    pallas_call x1, Pallas kernels, convolve(): pl.pallas_call(functools.partial(conv_kernel, first), grid=(groups // PAI...  6.94 us
    unnamed x59, local copies, waits for them, and re-layouts  3.89 us
    pallas_call x1, Pallas kernels, home(): pl.pallas_call(home_kernel, grid=(cols // step,), in_specs=in_specs, out_...  2.85 us
    pallas_call x1, Pallas kernels, home_apart(): pl.pallas_call(home_apart_kernel, grid=(STEPS,), in_specs=[pl.BlockSpec(m...  2.71 us
  transfers between devices with their start and end apart: 26, of which 6 were waited for; matrix products, arithmetic and copies ran while one was open for 2% of the time, Pallas kernels for 17%

profile of v6, /device:TPU:9, one launch (start us, length us, event | category | flops | bytes accessed | tf_op | source)
XLA Modules:
  0.0 114.0 jit_solution(10712632728302177493)
XLA Ops:
  0.0 2.4 %turn_taps.1 = f32[16,72,256]{2,1,0:T(8,128)} custom-call(f32[256,2048]{1,0:T(8,128)} %rest_16_.1, f32[128,256]{1,0:T(8,128)} %taps_ref.1), custom_call_target="tpu_custom_call" | custom-call | bytes 2097152 | tf_op jit(solution)/shard_map/turn_taps/pallas_call | solution.py:55
  2.4 6.6 %all-to-all-start = ((f32[16,72,256]{2,1,0:T(8,128)}), f32[16,72,256]{2,1,0:T(8,128)S(1)}, u32[]{:S(2)}, u32[]{:S(2)}) async-start(f32[16,72,256]{2,1,0:T(8,128)} %turn_taps.1), calls=%async_computation | async-start | bytes 2359296 | tf_op jit(solution)/shard_map/all_to_all | solution.py:315
  9.6 2.6 %turn_apart.1 = (f32[2,64,256]{2,1,0:T(8,128)}, f32[2,64,256]{2,1,0:T(8,128)}, f32[2,64,256]{2,1,0:T(8,128)}, f32[2,64,256]{2,1,0:T(8,128)}, f32[2,64,256]{2,1,0...) custom-call(s32[2]{0:T(128)} %pad_add_fusion.place_ref, f32[256,2048]{1,0:T(8,128)} %rest_16_.1), custom_call_target="tpu_custom_call" | custom-call | bytes 2097152 | tf_op jit(solution)/shard_map/turn_apart/pallas_call | solution.py:84
  12.2 1.2 %collective-permute-start = (f32[2,64,256]{2,1,0:T(8,128)}, f32[2,64,256]{2,1,0:T(8,128)S(1)}, u32[]{:S(2)}, u32[]{:S(2)}) collective-permute-start(f32[2,64,256]{2,1,0:T(8,128)} %get-tuple-element.34), channel_id=1, source_target_pairs={{0,4},{2,6},{4,0},{6,2},{8,12},{10,14},{12,8},{14,10},{16,20},{18,... | collective-permute-start | bytes 393224 | tf_op jit(solution)/shard_map/ppermute | solution.py:311
  13.6 1.2 %collective-permute-start.2 = (f32[2,64,256]{2,1,0:T(8,128)}, f32[2,64,256]{2,1,0:T(8,128)S(1)}, u32[]{:S(2)}, u32[]{:S(2)}) collective-permute-start(f32[2,64,256]{2,1,0:T(8,128)} %get-tuple-element.36), channel_id=1, source_target_pairs={{0,12},{2,14},{4,8},{6,10},{8,4},{10,6},{12,0},{14,2},{16,28},{18,... | collective-permute-start | bytes 393224 | tf_op jit(solution)/shard_map/ppermute | solution.py:311
  14.8 2.1 %collective-permute-start.4 = (f32[2,64,256]{2,1,0:T(8,128)}, f32[2,64,256]{2,1,0:T(8,128)S(1)}, u32[]{:S(2)}, u32[]{:S(2)}) collective-permute-start(f32[2,64,256]{2,1,0:T(8,128)} %get-tuple-element.39), channel_id=1, source_target_pairs={{0,16},{2,18},{4,20},{6,22},{8,24},{10,26},{12,28},{14,30},{16,0},... | collective-permute-start | bytes 393224 | tf_op jit(solution)/shard_map/ppermute | solution.py:311
  17.7 19.0 %collective-permute-done.2.rest_3_ = f32[2,64,256]{2,1,0:T(8,128)S(1)} collective-permute-done((f32[2,64,256]{2,1,0:T(8,128)}, f32[2,64,256]{2,1,0:T(8,128)S(1)}, u32[]{:S(2)}, u32[]{:S(2)}) %collective-permute-start.2) | collective-permute-done | bytes 131104 | tf_op jit(solution)/shard_map/ppermute | solution.py:311
  37.5 1.4 %collective-permute-start.6 = (f32[2,64,256]{2,1,0:T(8,128)}, f32[2,64,256]{2,1,0:T(8,128)S(1)}, u32[]{:S(2)}, u32[]{:S(2)}) collective-permute-start(f32[2,64,256]{2,1,0:T(8,128)} %get-tuple-element.43), channel_id=1, source_target_pairs={{0,24},{2,26},{4,28},{6,30},{8,16},{10,18},{12,20},{14,22},{16,8},... | collective-permute-start | bytes 393224 | tf_op jit(solution)/shard_map/ppermute | solution.py:311
  38.9 1.1 collective-permute-start.7
  40.8 1.2 %collective-permute-start.3 = (f32[16,8,128]{2,1,0:T(8,128)S(1)}, f32[16,8,128]{2,1,0:T(8,128)S(1)}, u32[]{:S(2)}, u32[]{:S(2)}) collective-permute-start(f32[16,8,128]{2,1,0:T(8,128)S(1)} %get-tuple-element.63), channel_id=1, source_target_pairs={{0,1},{1,0},{2,3},{3,2},{4,5},{5,4},{6,7},{7,6},{8,9},{9,8},{10,11... | collective-permute-start | bytes 196616 | tf_op jit(solution)/shard_map/ppermute | solution.py:311
  42.0 2.2 %collective-permute-done.3.other_ref = f32[16,8,128]{2,1,0:T(8,128)S(1)} collective-permute-done((f32[16,8,128]{2,1,0:T(8,128)S(1)}, f32[16,8,128]{2,1,0:T(8,128)S(1)}, u32[]{:S(2)}, u32[]{:S(2)}) %collective-permute-start.3) | collective-permute-done | bytes 65568 | tf_op jit(solution)/shard_map/ppermute | solution.py:311
  44.8 6.9 %convolve.1 = f32[16,64,256]{2,1,0:T(8,128)} custom-call(s32[2]{0:T(128)} %pad_add_fusion.place_ref, f32[16,8,128]{2,1,0:T(8,128)} %get-tuple-element.64.own_ref, f32[16,8,128]{2,1,0:T(8,128)} %copy-done.25, f32[16,72,256]{2,1,0:T(8,128)} %copy-done.1), custom_call_target="tpu_custom_call" | custom-call | flops 3422552064 | bytes 2097152 | tf_op jit(solution)/shard_map/convolve/pallas_call | solution.py:234
  51.8 10.5 %all-to-all-start.1 = ((f32[16,64,256]{2,1,0:T(8,128)}), f32[16,64,256]{2,1,0:T(8,128)S(1)}, u32[]{:S(2)}, u32[]{:S(2)}) async-start(f32[16,64,256]{2,1,0:T(8,128)} %convolve.1), calls=%async_computation.1 | async-start | bytes 2097152 | tf_op jit(solution)/shard_map/all_to_all | solution.py:315
  62.9 1.5 %collective-permute-done.8.passed_ref = f32[8,64,256]{2,1,0:T(8,128)S(1)} collective-permute-done((f32[8,64,256]{2,1,0:T(8,128)S(1)}, f32[8,64,256]{2,1,0:T(8,128)S(1)}, u32[]{:S(2)}, u32[]{:S(2)}) %collective-permute-start.8) | collective-permute-done | bytes 524320 | tf_op jit(solution)/shard_map/ppermute | solution.py:311
  65.2 7.2 %convolve_apart.1 = (f32[64,256]{1,0:T(8,128)}, f32[64,256]{1,0:T(8,128)}, f32[64,256]{1,0:T(8,128)}, f32[64,256]{1,0:T(8,128)}, f32[64,256]{1,0:T(8,128)}, /*in...) custom-call(s32[2]{0:T(128)} %pad_add_fusion.place_ref, ...), custom_call_target="tpu_custom_call" | custom-call | flops 3422552064 | bytes 2097152 | tf_op jit(solution)/shard_map/convolve_apart/pallas_call | solution.py:252
  72.8 1.2 %collective-permute-start.10 = (f32[64,256]{1,0:T(8,128)}, f32[64,256]{1,0:T(8,128)S(1)}, u32[]{:S(2)}, u32[]{:S(2)}) collective-permute-start(f32[64,256]{1,0:T(8,128)} %get-tuple-element.48), channel_id=1, source_target_pairs={{0,4},{2,6},{4,0},{6,2},{8,12},{10,14},{12,8},{14,10},{16,20},{18,... | collective-permute-start | bytes 196616 | tf_op jit(solution)/shard_map/ppermute | solution.py:311
  74.7 1.7 %collective-permute-start.13 = (f32[64,256]{1,0:T(8,128)}, f32[64,256]{1,0:T(8,128)S(1)}, u32[]{:S(2)}, u32[]{:S(2)}) collective-permute-start(f32[64,256]{1,0:T(8,128)} %get-tuple-element.51), channel_id=1, source_target_pairs={{0,10},{2,8},{4,14},{6,12},{8,2},{10,0},{12,6},{14,4},{16,26},{18,... | collective-permute-start | bytes 196616 | tf_op jit(solution)/shard_map/ppermute | solution.py:311
  76.3 1.2 %collective-permute-start.14 = (f32[64,256]{1,0:T(8,128)}, f32[64,256]{1,0:T(8,128)S(1)}, u32[]{:S(2)}, u32[]{:S(2)}) collective-permute-start(f32[64,256]{1,0:T(8,128)} %get-tuple-element.52), channel_id=1, source_target_pairs={{0,12},{2,14},{4,8},{6,10},{8,4},{10,6},{12,0},{14,2},{16,28},{18,... | collective-permute-start | bytes 196616 | tf_op jit(solution)/shard_map/ppermute | solution.py:311
  77.5 3.8 %collective-permute-start.15 = (f32[64,256]{1,0:T(8,128)}, f32[64,256]{1,0:T(8,128)S(1)}, u32[]{:S(2)}, u32[]{:S(2)}) collective-permute-start(f32[64,256]{1,0:T(8,128)} %get-tuple-element.53), channel_id=1, source_target_pairs={{0,14},{2,12},{4,10},{6,8},{8,6},{10,4},{12,2},{14,0},{16,30},{18,... | collective-permute-start | bytes 196616 | tf_op jit(solution)/shard_map/ppermute | solution.py:311
  81.3 1.4 %collective-permute-start.16 = (f32[64,256]{1,0:T(8,128)}, f32[64,256]{1,0:T(8,128)S(1)}, u32[]{:S(2)}, u32[]{:S(2)}) collective-permute-start(f32[64,256]{1,0:T(8,128)} %get-tuple-element.54), channel_id=1, source_target_pairs={{0,16},{2,18},{4,20},{6,22},{8,24},{10,26},{12,28},{14,30},{16,0},... | collective-permute-start | bytes 196616 | tf_op jit(solution)/shard_map/ppermute | solution.py:311
  82.7 2.1 %collective-permute-start.17 = (f32[64,256]{1,0:T(8,128)}, f32[64,256]{1,0:T(8,128)S(1)}, u32[]{:S(2)}, u32[]{:S(2)}) collective-permute-start(f32[64,256]{1,0:T(8,128)} %get-tuple-element.55), channel_id=1, source_target_pairs={{0,18},{2,16},{4,22},{6,20},{8,26},{10,24},{12,30},{14,28},{16,2},... | collective-permute-start | bytes 196616 | tf_op jit(solution)/shard_map/ppermute | solution.py:311
  84.8 3.5 %collective-permute-start.18 = (f32[64,256]{1,0:T(8,128)}, f32[64,256]{1,0:T(8,128)S(1)}, u32[]{:S(2)}, u32[]{:S(2)}) collective-permute-start(f32[64,256]{1,0:T(8,128)} %get-tuple-element.56), channel_id=1, source_target_pairs={{0,20},{2,22},{4,16},{6,18},{8,28},{10,30},{12,24},{14,26},{16,4},... | collective-permute-start | bytes 196616 | tf_op jit(solution)/shard_map/ppermute | solution.py:311
  88.3 3.0 %collective-permute-start.19 = (f32[64,256]{1,0:T(8,128)}, f32[64,256]{1,0:T(8,128)S(1)}, u32[]{:S(2)}, u32[]{:S(2)}) collective-permute-start(f32[64,256]{1,0:T(8,128)} %get-tuple-element.57), channel_id=1, source_target_pairs={{0,22},{2,20},{4,18},{6,16},{8,30},{10,28},{12,26},{14,24},{16,6},... | collective-permute-start | bytes 196616 | tf_op jit(solution)/shard_map/ppermute | solution.py:311
  91.3 4.8 %collective-permute-start.21 = (f32[64,256]{1,0:T(8,128)}, f32[64,256]{1,0:T(8,128)S(1)}, u32[]{:S(2)}, u32[]{:S(2)}) collective-permute-start(f32[64,256]{1,0:T(8,128)} %get-tuple-element.59), channel_id=1, source_target_pairs={{0,26},{2,24},{4,30},{6,28},{8,18},{10,16},{12,22},{14,20},{16,10}... | collective-permute-start | bytes 196616 | tf_op jit(solution)/shard_map/ppermute | solution.py:311
  96.1 1.0 collective-permute-start.22
  97.1 2.8 %collective-permute-start.23 = (f32[64,256]{1,0:T(8,128)}, f32[64,256]{1,0:T(8,128)S(1)}, u32[]{:S(2)}, u32[]{:S(2)}) collective-permute-start(f32[64,256]{1,0:T(8,128)} %get-tuple-element.61), channel_id=1, source_target_pairs={{0,30},{2,28},{4,26},{6,24},{8,22},{10,20},{12,18},{14,16},{16,14}... | collective-permute-start | bytes 196616 | tf_op jit(solution)/shard_map/ppermute | solution.py:311
  99.8 1.0 copy-done
  100.8 2.9 %home.1.rest_18_ = f32[256,2048]{1,0:T(8,128)} custom-call(f32[1024,256]{1,0:T(8,128)} %bitcast.4, f32[256,2048]{1,0:T(8,128)} %rest_16_.1, f32[1,2048]{1,0:T(1,128)} %bitcast.5), custom_call_target="tpu_custom_call" | custom-call | bytes 3145728 | tf_op jit(solution)/shard_map/home/pallas_call | solution.py:120
  103.7 3.7 %collective-permute-done.21.rest_13_ = f32[64,256]{1,0:T(8,128)S(1)} collective-permute-done((f32[64,256]{1,0:T(8,128)}, f32[64,256]{1,0:T(8,128)S(1)}, u32[]{:S(2)}, u32[]{:S(2)}) %collective-permute-start.21) | collective-permute-done | bytes 65568 | tf_op jit(solution)/shard_map/ppermute | solution.py:311
  107.4 1.7 %collective-permute-done.22.rest_14_ = f32[64,256]{1,0:T(8,128)S(1)} collective-permute-done((f32[64,256]{1,0:T(8,128)}, f32[64,256]{1,0:T(8,128)S(1)}, u32[]{:S(2)}, u32[]{:S(2)}) %collective-permute-start.22) | collective-permute-done | bytes 65568 | tf_op jit(solution)/shard_map/ppermute | solution.py:311
  109.1 1.6 %collective-permute-done.23.rest_15_ = f32[64,256]{1,0:T(8,128)S(1)} collective-permute-done((f32[64,256]{1,0:T(8,128)}, f32[64,256]{1,0:T(8,128)S(1)}, u32[]{:S(2)}, u32[]{:S(2)}) %collective-permute-start.23) | collective-permute-done | bytes 65568 | tf_op jit(solution)/shard_map/ppermute | solution.py:311
  111.3 2.7 %home_apart.1 = f32[256,2048]{1,0:T(8,128)} custom-call(s32[2]{0:T(128)} %pad_add_fusion.place_ref, f32[64,256]{1,0:T(8,128)} %get-tuple-element.46.rest_0_, f32[64,256]{1,0:T(8,128)} %copy-done.2, f32[64,256]{1,0:T(8,128)} %copy-done.3, f32[64,256]{1,0:T(8,128)} %copy-done.4, f32[64,256]{1,0:T(8,128)} %copy-done.5, ...), custom_call_target="tpu_custom_call", output_to_operand_aliasing={{}: (19, {})} | custom-call | bytes 3145728 | tf_op jit(solution)/shard_map/home_apart/pallas_call | solution.py:292
  (89 shorter events, 6.8 us)
Async XLA Ops:
  2.4 37.6 %all-to-all-start = ((f32[16,72,256]{2,1,0:T(8,128)}), f32[16,72,256]{2,1,0:T(8,128)S(1)}, u32[]{:S(2)}, u32[]{:S(2)}) async-start(f32[16,72,256]{2,1,0:T(8,128)} %turn_taps.1), calls=%async_computation | async-start | bytes 2359296 | tf_op jit(solution)/shard_map/all_to_all | solution.py:315
  12.2 26.7 %collective-permute-start = (f32[2,64,256]{2,1,0:T(8,128)}, f32[2,64,256]{2,1,0:T(8,128)S(1)}, u32[]{:S(2)}, u32[]{:S(2)}) collective-permute-start(f32[2,64,256]{2,1,0:T(8,128)} %get-tuple-element.34), channel_id=1, source_target_pairs={{0,4},{2,6},{4,0},{6,2},{8,12},{10,14},{12,8},{14,10},{16,20},{18,... | collective-permute-start | bytes 393224 | tf_op jit(solution)/shard_map/ppermute | solution.py:311
  13.3 26.6 %collective-permute-start.1 = (f32[2,64,256]{2,1,0:T(8,128)}, f32[2,64,256]{2,1,0:T(8,128)S(1)}, u32[]{:S(2)}, u32[]{:S(2)}) collective-permute-start(f32[2,64,256]{2,1,0:T(8,128)} %get-tuple-element.35), channel_id=1, source_target_pairs={{0,8},{2,10},{4,12},{6,14},{8,0},{10,2},{12,4},{14,6},{16,24},{18,... | collective-permute-start | bytes 393224 | tf_op jit(solution)/shard_map/ppermute | solution.py:311
  13.6 23.2 %collective-permute-start.2 = (f32[2,64,256]{2,1,0:T(8,128)}, f32[2,64,256]{2,1,0:T(8,128)S(1)}, u32[]{:S(2)}, u32[]{:S(2)}) collective-permute-start(f32[2,64,256]{2,1,0:T(8,128)} %get-tuple-element.36), channel_id=1, source_target_pairs={{0,12},{2,14},{4,8},{6,10},{8,4},{10,6},{12,0},{14,2},{16,28},{18,... | collective-permute-start | bytes 393224 | tf_op jit(solution)/shard_map/ppermute | solution.py:311
  14.8 37.0 %collective-permute-start.4 = (f32[2,64,256]{2,1,0:T(8,128)}, f32[2,64,256]{2,1,0:T(8,128)S(1)}, u32[]{:S(2)}, u32[]{:S(2)}) collective-permute-start(f32[2,64,256]{2,1,0:T(8,128)} %get-tuple-element.39), channel_id=1, source_target_pairs={{0,16},{2,18},{4,20},{6,22},{8,24},{10,26},{12,28},{14,30},{16,0},... | collective-permute-start | bytes 393224 | tf_op jit(solution)/shard_map/ppermute | solution.py:311
  36.8 25.5 %copy-start.19 = (f32[2,64,256]{2,1,0:T(8,128)}, f32[2,64,256]{2,1,0:T(8,128)S(1)}, u32[]{:S(2)}) copy-start(f32[2,64,256]{2,1,0:T(8,128)S(1)} %collective-permute-done.2.rest_3_) | copy-start | bytes 393220
  36.8 25.6 %collective-permute-start.5 = (f32[2,64,256]{2,1,0:T(8,128)}, f32[2,64,256]{2,1,0:T(8,128)S(1)}, u32[]{:S(2)}, u32[]{:S(2)}) collective-permute-start(f32[2,64,256]{2,1,0:T(8,128)} %get-tuple-element.41), channel_id=1, source_target_pairs={{0,20},{2,22},{4,16},{6,18},{8,28},{10,30},{12,24},{14,26},{16,4},... | collective-permute-start | bytes 393224 | tf_op jit(solution)/shard_map/ppermute | solution.py:311
  37.5 24.9 %collective-permute-start.6 = (f32[2,64,256]{2,1,0:T(8,128)}, f32[2,64,256]{2,1,0:T(8,128)S(1)}, u32[]{:S(2)}, u32[]{:S(2)}) collective-permute-start(f32[2,64,256]{2,1,0:T(8,128)} %get-tuple-element.43), channel_id=1, source_target_pairs={{0,24},{2,26},{4,28},{6,30},{8,16},{10,18},{12,20},{14,22},{16,8},... | collective-permute-start | bytes 393224 | tf_op jit(solution)/shard_map/ppermute | solution.py:311
  38.9 23.5 %collective-permute-start.7 = (f32[2,64,256]{2,1,0:T(8,128)}, f32[2,64,256]{2,1,0:T(8,128)S(1)}, u32[]{:S(2)}, u32[]{:S(2)}) collective-permute-start(f32[2,64,256]{2,1,0:T(8,128)} %get-tuple-element.45), channel_id=1, source_target_pairs={{0,28},{2,30},{4,24},{6,26},{8,20},{10,22},{12,16},{14,18},{16,12}... | collective-permute-start | bytes 393224 | tf_op jit(solution)/shard_map/ppermute | solution.py:311
  40.8 3.4 %collective-permute-start.3 = (f32[16,8,128]{2,1,0:T(8,128)S(1)}, f32[16,8,128]{2,1,0:T(8,128)S(1)}, u32[]{:S(2)}, u32[]{:S(2)}) collective-permute-start(f32[16,8,128]{2,1,0:T(8,128)S(1)} %get-tuple-element.63), channel_id=1, source_target_pairs={{0,1},{1,0},{2,3},{3,2},{4,5},{5,4},{6,7},{7,6},{8,9},{9,8},{10,11... | collective-permute-start | bytes 196616 | tf_op jit(solution)/shard_map/ppermute | solution.py:311
  51.8 48.0 %all-to-all-start.1 = ((f32[16,64,256]{2,1,0:T(8,128)}), f32[16,64,256]{2,1,0:T(8,128)S(1)}, u32[]{:S(2)}, u32[]{:S(2)}) async-start(f32[16,64,256]{2,1,0:T(8,128)} %convolve.1), calls=%async_computation.1 | async-start | bytes 2097152 | tf_op jit(solution)/shard_map/all_to_all | solution.py:315
  62.5 2.0 %collective-permute-start.8 = (f32[8,64,256]{2,1,0:T(8,128)S(1)}, f32[8,64,256]{2,1,0:T(8,128)S(1)}, u32[]{:S(2)}, u32[]{:S(2)}) collective-permute-start(f32[8,64,256]{2,1,0:T(8,128)S(1)} %slice_dynamic-update-slice_fusion), channel_id=1, source_target_pairs={{0,2},{2,0},{4,6},{6,4},{8,10},{10,8},{12,14},{14,12},{16,18},{18,... | collective-permute-start | bytes 1572872 | tf_op jit(solution)/shard_map/ppermute | solution.py:311
  72.4 3.9 %collective-permute-start.9 = (f32[64,256]{1,0:T(8,128)}, f32[64,256]{1,0:T(8,128)S(1)}, u32[]{:S(2)}, u32[]{:S(2)}) collective-permute-start(f32[64,256]{1,0:T(8,128)} %get-tuple-element.47), channel_id=1, source_target_pairs={{0,2},{2,0},{4,6},{6,4},{8,10},{10,8},{12,14},{14,12},{16,18},{18,... | collective-permute-start | bytes 196616 | tf_op jit(solution)/shard_map/ppermute | solution.py:311
  72.8 4.7 %collective-permute-start.10 = (f32[64,256]{1,0:T(8,128)}, f32[64,256]{1,0:T(8,128)S(1)}, u32[]{:S(2)}, u32[]{:S(2)}) collective-permute-start(f32[64,256]{1,0:T(8,128)} %get-tuple-element.48), channel_id=1, source_target_pairs={{0,4},{2,6},{4,0},{6,2},{8,12},{10,14},{12,8},{14,10},{16,20},{18,... | collective-permute-start | bytes 196616 | tf_op jit(solution)/shard_map/ppermute | solution.py:311
  74.0 7.3 %collective-permute-start.11 = (f32[64,256]{1,0:T(8,128)}, f32[64,256]{1,0:T(8,128)S(1)}, u32[]{:S(2)}, u32[]{:S(2)}) collective-permute-start(f32[64,256]{1,0:T(8,128)} %get-tuple-element.49), channel_id=1, source_target_pairs={{0,6},{2,4},{4,2},{6,0},{8,14},{10,12},{12,10},{14,8},{16,22},{18,... | collective-permute-start | bytes 196616 | tf_op jit(solution)/shard_map/ppermute | solution.py:311
  74.6 8.1 %collective-permute-start.12 = (f32[64,256]{1,0:T(8,128)}, f32[64,256]{1,0:T(8,128)S(1)}, u32[]{:S(2)}, u32[]{:S(2)}) collective-permute-start(f32[64,256]{1,0:T(8,128)} %get-tuple-element.50), channel_id=1, source_target_pairs={{0,8},{2,10},{4,12},{6,14},{8,0},{10,2},{12,4},{14,6},{16,24},{18,... | collective-permute-start | bytes 196616 | tf_op jit(solution)/shard_map/ppermute | solution.py:311
  74.7 10.1 %collective-permute-start.13 = (f32[64,256]{1,0:T(8,128)}, f32[64,256]{1,0:T(8,128)S(1)}, u32[]{:S(2)}, u32[]{:S(2)}) collective-permute-start(f32[64,256]{1,0:T(8,128)} %get-tuple-element.51), channel_id=1, source_target_pairs={{0,10},{2,8},{4,14},{6,12},{8,2},{10,0},{12,6},{14,4},{16,26},{18,... | collective-permute-start | bytes 196616 | tf_op jit(solution)/shard_map/ppermute | solution.py:311
  76.3 34.3 %copy-start.2 = (f32[64,256]{1,0:T(8,128)}, f32[64,256]{1,0:T(8,128)S(1)}, u32[]{:S(2)}) copy-start(f32[64,256]{1,0:T(8,128)S(1)} %collective-permute-done.9.rest_1_) | copy-start | bytes 196612
  76.3 11.9 %collective-permute-start.14 = (f32[64,256]{1,0:T(8,128)}, f32[64,256]{1,0:T(8,128)S(1)}, u32[]{:S(2)}, u32[]{:S(2)}) collective-permute-start(f32[64,256]{1,0:T(8,128)} %get-tuple-element.52), channel_id=1, source_target_pairs={{0,12},{2,14},{4,8},{6,10},{8,4},{10,6},{12,0},{14,2},{16,28},{18,... | collective-permute-start | bytes 196616 | tf_op jit(solution)/shard_map/ppermute | solution.py:311
  77.5 33.1 %copy-start.3 = (f32[64,256]{1,0:T(8,128)}, f32[64,256]{1,0:T(8,128)S(1)}, u32[]{:S(2)}) copy-start(f32[64,256]{1,0:T(8,128)S(1)} %collective-permute-done.10.rest_2_) | copy-start | bytes 196612
  77.5 13.7 %collective-permute-start.15 = (f32[64,256]{1,0:T(8,128)}, f32[64,256]{1,0:T(8,128)S(1)}, u32[]{:S(2)}, u32[]{:S(2)}) collective-permute-start(f32[64,256]{1,0:T(8,128)} %get-tuple-element.53), channel_id=1, source_target_pairs={{0,14},{2,12},{4,10},{6,8},{8,6},{10,4},{12,2},{14,0},{16,30},{18,... | collective-permute-start | bytes 196616 | tf_op jit(solution)/shard_map/ppermute | solution.py:311
  81.3 29.3 %copy-start.4 = (f32[64,256]{1,0:T(8,128)}, f32[64,256]{1,0:T(8,128)S(1)}, u32[]{:S(2)}) copy-start(f32[64,256]{1,0:T(8,128)S(1)} %collective-permute-done.11.rest_3_) | copy-start | bytes 196612
  81.3 9.9 %collective-permute-start.16 = (f32[64,256]{1,0:T(8,128)}, f32[64,256]{1,0:T(8,128)S(1)}, u32[]{:S(2)}, u32[]{:S(2)}) collective-permute-start(f32[64,256]{1,0:T(8,128)} %get-tuple-element.54), channel_id=1, source_target_pairs={{0,16},{2,18},{4,20},{6,22},{8,24},{10,26},{12,28},{14,30},{16,0},... | collective-permute-start | bytes 196616 | tf_op jit(solution)/shard_map/ppermute | solution.py:311
  82.7 27.9 %copy-start.5 = (f32[64,256]{1,0:T(8,128)}, f32[64,256]{1,0:T(8,128)S(1)}, u32[]{:S(2)}) copy-start(f32[64,256]{1,0:T(8,128)S(1)} %collective-permute-done.12.rest_4_) | copy-start | bytes 196612
  82.7 13.4 %collective-permute-start.17 = (f32[64,256]{1,0:T(8,128)}, f32[64,256]{1,0:T(8,128)S(1)}, u32[]{:S(2)}, u32[]{:S(2)}) collective-permute-start(f32[64,256]{1,0:T(8,128)} %get-tuple-element.55), channel_id=1, source_target_pairs={{0,18},{2,16},{4,22},{6,20},{8,26},{10,24},{12,30},{14,28},{16,2},... | collective-permute-start | bytes 196616 | tf_op jit(solution)/shard_map/ppermute | solution.py:311
  84.8 25.9 %copy-start.6 = (f32[64,256]{1,0:T(8,128)}, f32[64,256]{1,0:T(8,128)S(1)}, u32[]{:S(2)}) copy-start(f32[64,256]{1,0:T(8,128)S(1)} %collective-permute-done.13.rest_5_) | copy-start | bytes 196612
  84.8 12.2 %collective-permute-start.18 = (f32[64,256]{1,0:T(8,128)}, f32[64,256]{1,0:T(8,128)S(1)}, u32[]{:S(2)}, u32[]{:S(2)}) collective-permute-start(f32[64,256]{1,0:T(8,128)} %get-tuple-element.56), channel_id=1, source_target_pairs={{0,20},{2,22},{4,16},{6,18},{8,28},{10,30},{12,24},{14,26},{16,4},... | collective-permute-start | bytes 196616 | tf_op jit(solution)/shard_map/ppermute | solution.py:311
  88.3 15.4 %collective-permute-start.19 = (f32[64,256]{1,0:T(8,128)}, f32[64,256]{1,0:T(8,128)S(1)}, u32[]{:S(2)}, u32[]{:S(2)}) collective-permute-start(f32[64,256]{1,0:T(8,128)} %get-tuple-element.57), channel_id=1, source_target_pairs={{0,22},{2,20},{4,18},{6,16},{8,30},{10,28},{12,26},{14,24},{16,6},... | collective-permute-start | bytes 196616 | tf_op jit(solution)/shard_map/ppermute | solution.py:311
  91.3 12.4 %collective-permute-start.20 = (f32[64,256]{1,0:T(8,128)}, f32[64,256]{1,0:T(8,128)S(1)}, u32[]{:S(2)}, u32[]{:S(2)}) collective-permute-start(f32[64,256]{1,0:T(8,128)} %get-tuple-element.58), channel_id=1, source_target_pairs={{0,24},{2,26},{4,28},{6,30},{8,16},{10,18},{12,20},{14,22},{16,8},... | collective-permute-start | bytes 196616 | tf_op jit(solution)/shard_map/ppermute | solution.py:311
  91.3 16.1 %collective-permute-start.21 = (f32[64,256]{1,0:T(8,128)}, f32[64,256]{1,0:T(8,128)S(1)}, u32[]{:S(2)}, u32[]{:S(2)}) collective-permute-start(f32[64,256]{1,0:T(8,128)} %get-tuple-element.59), channel_id=1, source_target_pairs={{0,26},{2,24},{4,30},{6,28},{8,18},{10,16},{12,22},{14,20},{16,10}... | collective-permute-start | bytes 196616 | tf_op jit(solution)/shard_map/ppermute | solution.py:311
  96.1 13.0 %collective-permute-start.22 = (f32[64,256]{1,0:T(8,128)}, f32[64,256]{1,0:T(8,128)S(1)}, u32[]{:S(2)}, u32[]{:S(2)}) collective-permute-start(f32[64,256]{1,0:T(8,128)} %get-tuple-element.60), channel_id=1, source_target_pairs={{0,28},{2,30},{4,24},{6,26},{8,20},{10,22},{12,16},{14,18},{16,12}... | collective-permute-start | bytes 196616 | tf_op jit(solution)/shard_map/ppermute | solution.py:311
  97.1 13.6 %collective-permute-start.23 = (f32[64,256]{1,0:T(8,128)}, f32[64,256]{1,0:T(8,128)S(1)}, u32[]{:S(2)}, u32[]{:S(2)}) collective-permute-start(f32[64,256]{1,0:T(8,128)} %get-tuple-element.61), channel_id=1, source_target_pairs={{0,30},{2,28},{4,26},{6,24},{8,22},{10,20},{12,18},{14,16},{16,14}... | collective-permute-start | bytes 196616 | tf_op jit(solution)/shard_map/ppermute | solution.py:311
  (20 other events, 159.4 us)
